TPU v7x, 512 devices: a whole 4x4x16 slice. The times are simulated.
512 devices in a mesh: ctx: 32 (over x, y, core), head: 16 (over z).
Axes of the slice: x: 4, y: 4, z: 16, core: 2. Of those that a mesh axis runs over, the one named last changes fastest.
Arguments:
- queries: float32 [2048, 128, 576], P('ctx', 'head'), may hold values from -1 to 14
- latent: float32 [16384, 576], P('ctx'), may hold values from -12 to 12
- selected: int32 [32, 32], replicated, may hold values from 0 to 255, as said below
- value_proj: bfloat16 [128, 512, 128], P('head'), may hold values from -2 to 2
- out_proj: bfloat16 [16384, 7168], P('head', 'ctx'), may hold values from -0.046875 to 0.046875
Outputs:
- attn_out: bfloat16 [2048, 7168], P('head', 'ctx')
Inputs may be any that keep to these rules, and one draw needn't show every extreme that they name: `selected`: row j lists 32 distinct key-block ids, each at most 224 + j, including that block itself; at most 2 ids of a row lie in one aligned run of 8 blocks (one device's share of the context), and the last row reaches 2.
All inputs are finite; a program needn't handle non-finite values.
Results may differ from a plain program's by a relative error of at most 0.0049.
Values may be sent and summed in bfloat16 or wider, within the bound.
No kernel may reach another device: no remote copies, remote signals or barrier semaphores. Data moves between devices by JAX's collectives and lax.ppermute only.
A program may use at most 128 MiB of HBM per device.

v0:
```python
import jax
import jax.numpy as jnp
from jax import lax
from jax.sharding import PartitionSpec as P

neg_large = -1e30
score_scale = 1.0 / 192.0**0.5


def slot_table(chosen, owner_index, per_owner, capacity):
    on_owner = chosen // per_owner == owner_index
    counted = jnp.cumsum(on_owner.astype(jnp.int32), axis=-1) - 1
    slot_ids = jnp.arange(capacity, dtype=jnp.int32)
    matched = on_owner[..., None] & (counted[..., None] == slot_ids)
    block_numbers = jnp.sum(jnp.where(matched, chosen[..., None], 0), axis=-2)
    filled = jnp.any(matched, axis=-2)
    return (block_numbers, filled)


def on_device(queries, latent, selected, value_proj, out_proj):
    ctx_count = lax.axis_size("ctx")
    ctx_index = lax.axis_index("ctx")
    block_rows = queries.shape[0]
    heads_here = queries.shape[1]
    row_width = latent.shape[1]
    lat_width = value_proj.shape[1]
    per_owner = latent.shape[0] // block_rows
    top_blocks = selected.shape[1]
    capacity = max(2, per_owner // 4, 2 * top_blocks // ctx_count)
    key_blocks = per_owner * ctx_count
    cache_blocks = latent.reshape(per_owner, block_rows, row_width)
    wanted, present = slot_table(selected, ctx_index, per_owner, capacity)
    local_ids = jnp.where(present, wanted - ctx_index * per_owner, 0)
    parcel = jnp.take(cache_blocks, local_ids, axis=0)
    arrived = lax.all_to_all(parcel, "ctx", split_axis=0, concat_axis=0, tiled=True)
    own_list = lax.dynamic_slice_in_dim(selected, ctx_index, 1, 0)[0]
    owner_of = own_list // per_owner
    order_ids = jnp.arange(top_blocks, dtype=jnp.int32)
    earlier = (owner_of[None, :] == owner_of[:, None]) & (order_ids[None, :] < order_ids[:, None])
    slot_of = jnp.sum(earlier.astype(jnp.int32), axis=1)
    source_index = owner_of * capacity + slot_of
    slot_blocks = arrived.reshape(ctx_count * capacity, block_rows, row_width)
    key_count = top_blocks * block_rows
    key_rows = jnp.take(slot_blocks, source_index, axis=0).reshape(key_count, row_width)
    offsets = jnp.arange(block_rows, dtype=jnp.int32)
    key_pos = (own_list[:, None] * block_rows + offsets[None, :]).reshape(key_count)
    query_pos = (key_blocks - ctx_count + ctx_index) * block_rows + offsets
    visible = key_pos[None, :] <= query_pos[:, None]
    flat_queries = queries.reshape(block_rows * heads_here, row_width)
    scores = (
        lax.dot_general(
            flat_queries,
            key_rows,
            (((1,), (1,)), ((), ())),
            precision=lax.Precision.HIGHEST,
            preferred_element_type=jnp.float32,
        )
        * score_scale
    )
    scores = scores.reshape(block_rows, heads_here, key_count)
    masked = jnp.where(visible[:, None, :], scores, neg_large)
    row_peak = jnp.max(masked, axis=-1, keepdims=True)
    exponent = jnp.where(visible[:, None, :], jnp.exp(masked - row_peak), 0.0)
    weights = exponent / jnp.sum(exponent, axis=-1, keepdims=True)
    mixture = jnp.dot(
        weights.reshape(block_rows * heads_here, key_count),
        key_rows[:, :lat_width],
        precision=lax.Precision.HIGHEST,
        preferred_element_type=jnp.float32,
    )
    attended = mixture.reshape(block_rows, heads_here, lat_width)
    head_out = jnp.einsum(
        "bhl,hlv->bhv", attended, value_proj.astype(jnp.float32), precision=lax.Precision.HIGHEST
    ).astype(jnp.bfloat16)
    head_flat = head_out.reshape(block_rows, heads_here * value_proj.shape[2])
    gathered = lax.all_gather(head_flat, "ctx", axis=0, tiled=True)
    summed = lax.psum_scatter(
        jnp.dot(gathered, out_proj, preferred_element_type=jnp.float32),
        "head",
        scatter_dimension=0,
        tiled=True,
    )
    return summed.astype(jnp.bfloat16)


def solution(mesh):
    in_specs = (
        P("ctx", "head", None),
        P("ctx", None),
        P(),
        P("head", None, None),
        P("head", "ctx"),
    )
    out_specs = P("head", "ctx")
    return jax.shard_map(
        on_device, mesh=mesh, in_specs=in_specs, out_specs=out_specs, check_vma=False
    )
```

profile of v0, /device:TPU:8, one launch (start us, length us, event | category | flops | bytes accessed | tf_op | source)
XLA Modules:
  0.0 380.6 jit_solution(1959558491291851732)
XLA Ops:
  6.5 0.8 fusion.31
  7.4 0.2 reduce_window_sum.11
  7.6 0.8 select_reduce_fusion
  8.4 0.1 fusion.20
  8.8 1.7 copy.13
  10.5 5.2 %gather_fusion = f32[64,64,576]{2,1,0:T(8,128)} fusion(f32[8,64,576]{2,1,0:T(8,128)S(1)} %bitcast.82, s32[1024]{0:T(1024)S(1)} %pad_clamp_fusion.1), kind=kCustom, calls=%fused_computation | custom fusion | bytes 18874624 | tf_op jit(solution)/shard_map/jit(_take)/gather | solution.py:34
  15.8 9.9 %broadcast_select_fusion = f32[32,2,64,576]{3,2,1,0:T(8,128)} fusion(f32[32,2,64,576]{3,2,1,0:T(8,128)} %bitcast.84, pred[32,2]{1,0:T(8,128)(4,1)S(1)} %copy.12), kind=kLoop, calls=%fused_computation.4 | loop fusion | flops 2359296 | bytes 18874432 | tf_op jit(solution)/shard_map/jit(_take)/select_n | solution.py:34
  25.7 10.4 %all-to-all-start = ((f32[32,2,64,576]{3,2,1,0:T(8,128)}), f32[32,2,64,576]{3,2,1,0:T(8,128)}, u32[]{:S(2)}, u32[]{:S(2)}) async-start(f32[32,2,64,576]{3,2,1,0:T(8,128)} %broadcast_select_fusion), calls=%async_computation | async-start | bytes 20971520 | tf_op jit(solution)/shard_map/all_to_all | solution.py:35
  36.1 0.2 all-gather.2.cloned.1.call-start
  36.3 0.7 bitcast_multiply_fusion
  37.2 0.2 convert_reduce_fusion
  37.6 0.1 broadcast_compare_fusion
  37.8 162.6 %all-to-all-done = f32[32,2,64,576]{3,2,1,0:T(8,128)} async-done(((f32[32,2,64,576]{3,2,1,0:T(8,128)}), f32[32,2,64,576]{3,2,1,0:T(8,128)}, u32[]{:S(2)}, u32[]{:S(2)}) %all-to-all-start) | async-done | bytes 9437216 | tf_op jit(solution)/shard_map/all_to_all | solution.py:35
  200.4 7.2 %gather_fusion.1 = f32[32,64,576]{2,1,0:T(8,128)} fusion(f32[64,64,576]{2,1,0:T(8,128)} %bitcast.6, s32[1024]{0:T(1024)S(1)} %pad_clamp_fusion), kind=kCustom, calls=%fused_computation.1 | custom fusion | bytes 9437312 | tf_op jit(solution)/shard_map/jit(_take)/gather | solution.py:44
  207.6 3.0 broadcast_select_fusion.1
  210.7 10.7 %fusion.5 = (f32[512]{0:T(512)S(1)}, f32[2048,512]{0,1:T(8,128)S(1)}) fusion(pred[64,2048]{1,0:T(8,128)(4,1)S(1)} %broadcast_compare_fusion, f32[2048,576]{1,0:T(8,128)S(1)} %bitcast.83, f32[64,8,576]{2,1,0:T(8,128)S(1)} %copy-done), kind=kOutput, calls=%fused_computation.10 | convolution fusion | flops 7250902528 | bytes 10225664 | tf_op jit(solution)/shard_map/dot_general | solution.py:51
  221.4 1.7 fusion.6
  223.1 8.4 %fusion.1 = f32[64,8,512]{2,1,0:T(8,128)S(1)} fusion(f32[2048,576]{1,0:T(8,128)S(1)} %bitcast.87, f32[2048,512]{0,1:T(8,128)S(1)} %get-tuple-element.10, f32[512]{0:T(512)S(1)} %fusion.6, f32[512]{0:T(512)S(1)} %get-tuple-element.9, pred[2048]{0:T(1024)(128)(4,1)S(1)} %broadcast_in_dim.93, pred[64,2048]{1,0:T(8,128)(4,1)S(1)} %broadcast_compare_fusion), kind=kOutput, calls=%fused_computation.7 | convolution fusion | flops 6448742400 | bytes 9574400 | tf_op jit(solution)/shard_map/dot_general | solution.py:65
  231.6 1.2 fusion.17
  232.8 0.7 copy.21
  233.5 61.3 %all-gather.2.cloned.1.call-done = bf16[2048,1024]{1,0:T(8,128)(2,1)} async-done(((bf16[64,1024]{1,0:T(8,128)(2,1)}), bf16[2048,1024]{1,0:T(8,128)(2,1)}) %all-gather.2.cloned.1.call-update) | async-done | bytes 4194320 | tf_op jit(solution)/shard_map/all_gather | solution.py:76
  294.8 4.9 %fusion.33 = f32[2048,224]{0,1:T(8,128)} fusion(bf16[2048,1024]{1,0:T(8,128)(2,1)} %all-gather.2.cloned.1.call-done, bf16[1024,224]{0,1:T(8,128)(2,1)S(1)} %copy-done.2), kind=kOutput, calls=%fused_computation.79 | convolution fusion | flops 939524096 | bytes 6488064 | tf_op jit(solution)/shard_map/dot_general | solution.py:78
  299.7 72.6 %reduce-scatter.2.cloned.1.call-done = f32[128,224]{0,1:T(8,128)} async-done(((f32[2048,224]{0,1:T(8,128)}), f32[128,224]{0,1:T(8,128)}) %reduce-scatter.2.cloned.1.call-update) | async-done | bytes 114704 | tf_op jit(solution)/shard_map/reduce_scatter | solution.py:77
  372.3 1.5 convert_element_type.20
  (31 shorter events, 0.8 us)
Async XLA Ops:
  6.5 204.2 %copy-start = (f32[64,8,576]{2,1,0:T(8,128)S(1)}, f32[64,8,576]{2,1,0:T(8,128)}, u32[]{:S(2)}) copy-start(f32[64,8,576]{2,1,0:T(8,128)} %param.5) | copy-start | bytes 3538948
  25.7 174.7 %all-to-all-start = ((f32[32,2,64,576]{3,2,1,0:T(8,128)}), f32[32,2,64,576]{3,2,1,0:T(8,128)}, u32[]{:S(2)}, u32[]{:S(2)}) async-start(f32[32,2,64,576]{3,2,1,0:T(8,128)} %broadcast_select_fusion), calls=%async_computation | async-start | bytes 20971520 | tf_op jit(solution)/shard_map/all_to_all | solution.py:35
  36.1 258.7 %all-gather.2.cloned.1.call-start = ((), (), s32[]{:S(2)}) async-start(), calls=%async_computation.2 | async-start | bytes 4325376 | tf_op jit(solution)/shard_map/all_gather | solution.py:76
  210.7 12.4 %slice-start = ((s8[5242880]{0:T(1024)(128)(4,1)}), s8[4194304]{0:T(1024)(128)(4,1)S(1)}, s32[]{:S(2)}) async-start(s8[5242880]{0:T(1024)(128)(4,1)} %bitcast.85), calls=%async_computation.4 | async-start | bytes 8388608
  210.7 12.4 %slice-start.1 = ((s8[5242880]{0:T(1024)(128)(4,1)}), s8[1048576]{0:T(1024)(128)(4,1)S(1)}, s32[]{:S(2)}) async-start(s8[5242880]{0:T(1024)(128)(4,1)} %bitcast.85), calls=%async_computation.5 | async-start | bytes 2097152
  223.1 8.5 %copy-start.1 = (bf16[8,512,128]{2,1,0:T(8,128)(2,1)S(1)}, bf16[8,512,128]{2,1,0:T(8,128)(2,1)}, u32[]{:S(2)}) copy-start(bf16[8,512,128]{2,1,0:T(8,128)(2,1)} %param.8) | copy-start | bytes 3145732
  223.1 71.7 %copy-start.2 = (bf16[1024,224]{0,1:T(8,128)(2,1)S(1)}, bf16[1024,224]{0,1:T(8,128)(2,1)}, u32[]{:S(2)}) copy-start(bf16[1024,224]{0,1:T(8,128)(2,1)} %param.9) | copy-start | bytes 1376260
  233.5 138.8 %reduce-scatter.2.cloned.1.call-start = ((), (), s32[]{:S(2)}) async-start(), calls=%async_computation.3 | async-start | bytes 1949696 | tf_op jit(solution)/shard_map/reduce_scatter | solution.py:77
Sparse Core Ops, SparseCore 0:
  233.6 61.1 all-gather.1
  299.8 72.4 reduce-scatter.1
where the time goes:
time: 381 us
  waiting for transfers between devices  297 us (78%)
  matrix products  25.2 us (7%)
  other arithmetic  19.3 us (5%)
  local copies, waits for them, and re-layouts  15.3 us (4%)
  between operations  13.6 us (4%)
  starting transfers between devices  10.7 us (3%)
    all_to_all x1, waiting for transfers between devices, on_device(): lax.all_to_all(parcel, 'ctx', split_axis=0, concat_axis=0, tiled=True)  163 us
    reduce_scatter x1, waiting for transfers between devices, on_device(): lax.psum_scatter(jnp.dot(gathered, out_proj, preferred_element_type=jnp.f...  72.6 us
    all_gather x1, waiting for transfers between devices, on_device(): gathered = lax.all_gather(head_flat, 'ctx', axis=0, tiled=True)  61.3 us
    dot_general x1, matrix products, on_device(): lax.dot_general(flat_queries, key_rows, (((1,), (1,)), ((), ())), precisi...  10.7 us
    all_to_all x1, starting transfers between devices, on_device(): lax.all_to_all(parcel, 'ctx', split_axis=0, concat_axis=0, tiled=True)  10.4 us
    select_n x2, other arithmetic, on_device(): parcel = jnp.take(cache_blocks, local_ids, axis=0)  9.94 us
    dot_general x1, matrix products, on_device(): jnp.dot(weights.reshape(block_rows * heads_here, key_count), key_rows[:,...  8.43 us
  transfers between devices with their start and end apart: 3, of which 3 were waited for; matrix products, arithmetic and copies ran while one was open for 0% of the time, Pallas kernels for 0%

commit v1 on v0

v1 whole, which is shorter than its diff:
```python
import functools

import jax
import jax.numpy as jnp
from jax import lax
from jax.experimental import pallas as pl
from jax.experimental.pallas import tpu as pltpu
from jax.sharding import Mesh
from jax.sharding import PartitionSpec as P

NEG = -1e30
SCALE = 1.0 / 192.0**0.5
F32, BF16, S16 = jnp.float32, jnp.bfloat16, jnp.int16
LANES = 128
ZL = 4
LIMIT = 48 * 1024 * 1024


def row_code(peak):
    return jnp.ceil(jnp.log2(jnp.maximum(peak, 1e-30)) * 256.0)


def to_int(x, code):
    y = jnp.round(x * (jnp.exp2(code * (-1.0 / 256.0)) * 32767.0))
    return jnp.clip(y, -32767.0, 32767.0)


def scale_of(code):
    return jnp.exp2(code * (1.0 / 256.0)) * (1.0 / 32767.0)


def as_s16(x):
    return x.astype(jnp.int32).astype(S16)


def as_f32(x):
    return x.astype(jnp.int32).astype(F32)


def lane_ids(shape):
    return lax.broadcasted_iota(jnp.int32, shape, len(shape) - 1)


def dot_nt(a, b):
    return lax.dot_general(a, b, (((1,), (1,)), ((), ())), preferred_element_type=F32)


def dot_nn(a, b):
    return jnp.dot(a, b, preferred_element_type=F32)


def halves(x):
    high = x.astype(BF16)
    return high, (x - high.astype(F32)).astype(BF16)


def parcel_kernel(ids, latent, out, wide, coded, sems):
    blocks, rows, width = latent.shape
    padded = wide.shape[-1]
    for b in range(blocks):
        x = latent[b]
        wide[:, :width] = x
        code = row_code(jnp.max(jnp.abs(x), axis=-1, keepdims=True))
        lanes = lane_ids((rows, padded))
        full = jnp.where(lanes < width, to_int(wide[...], code), code)
        coded[b] = as_s16(full)
    receivers = out.shape[0]
    copies = []
    for d in range(receivers):
        for s in range(2):
            copy = pltpu.make_async_copy(coded.at[ids[d, s]], out.at[d, s], sems.at[2 * d + s])
            copy.start()
            copies.append(copy)
    for copy in copies:
        copy.wait()


def make_parcels(ids, latent, receivers, padded):
    blocks, rows, width = latent.shape
    return pl.pallas_call(
        parcel_kernel,
        out_shape=jax.ShapeDtypeStruct((receivers, 2, rows, padded), S16),
        in_specs=[pl.BlockSpec(memory_space=pltpu.SMEM), pl.BlockSpec(memory_space=pltpu.VMEM)],
        out_specs=pl.BlockSpec(memory_space=pl.ANY),
        scratch_shapes=[
            pltpu.VMEM((rows, padded), F32),
            pltpu.VMEM((blocks, rows, padded), S16),
            pltpu.SemaphoreType.DMA((2 * receivers,)),
        ],
        compiler_params=pltpu.CompilerParams(vmem_limit_bytes=LIMIT),
        cost_estimate=pl.CostEstimate(flops=10**7, bytes_accessed=7 * 10**6, transcendentals=0),
        name="parcels",
    )(ids, latent)


def attend_kernel(places, block_ids, own, q, arrived, value_proj, out, slots, kh_s, kl_s, s_s, sems):
    count = places.shape[0]
    rows, padded = slots.shape[1:]
    heads, lat, vdim = value_proj.shape
    copies = []
    for i in range(count):
        copy = pltpu.make_async_copy(arrived.at[places[i]], slots.at[i], sems.at[i])
        copy.start()
        copies.append(copy)
    width = 576
    lanes = lane_ids((heads * rows, padded))
    qh, ql = halves(jnp.where(lanes < width, q[...], 0.0))
    step = 4
    keys = step * rows
    total = heads * rows
    lane = lane_ids((total, keys))
    row = lax.broadcasted_iota(jnp.int32, (total, keys), 0)
    ahead = lane % rows - row % rows
    which = lane_ids((1, keys)) // rows
    peak = jnp.full((total, 1), NEG, F32)
    for c in range(count // step):
        for i in range(c * step, (c + 1) * step):
            copies[i].wait()
        raw = slots[c * step : (c + 1) * step].reshape(keys, padded)
        wide = as_f32(raw)
        factor = scale_of(wide[:, padded - LANES :])[:, LANES - 1 :]
        kh, kl = halves(wide * factor)
        span = pl.ds(c * keys, keys)
        kh_s[span, :] = kh
        kl_s[span, :] = kl
        s = dot_nt(qh, kh) + dot_nt(ql, kh) + dot_nt(qh, kl)
        room = jnp.zeros((1, keys), jnp.int32)
        for i in range(step):
            room = jnp.where(which == i, (own[0] - block_ids[c * step + i]) * rows, room)
        s = jnp.where(ahead <= room, s, NEG)
        s_s[:, span] = s
        peak = jnp.maximum(peak, jnp.max(s, axis=-1, keepdims=True))
    acc = jnp.zeros((total, lat), F32)
    norm = jnp.zeros((total, 1), F32)
    for c in range(count // step):
        span = pl.ds(c * keys, keys)
        p = jnp.exp((s_s[:, span] - peak) * SCALE)
        norm = norm + jnp.sum(p, axis=-1, keepdims=True)
        ph, plo = halves(p)
        vh = kh_s[span, :lat]
        acc = acc + dot_nn(ph, vh) + dot_nn(plo, vh) + dot_nn(ph, kl_s[span, :lat])
    ah, al = halves(acc / norm)
    pieces = []
    for h in range(heads):
        part = slice(h * rows, (h + 1) * rows)
        pieces.append(dot_nn(ah[part], value_proj[h]) + dot_nn(al[part], value_proj[h]))
    head_out = jnp.concatenate(pieces, axis=-1).astype(BF16).astype(F32)
    code = row_code(jnp.max(jnp.abs(head_out), axis=-1, keepdims=True))
    out[:, : heads * vdim] = as_s16(to_int(head_out, code))
    out[:, heads * vdim :] = as_s16(jnp.broadcast_to(code, (rows, LANES)))


def attend(places, block_ids, own, q, arrived, value_proj):
    count = places.shape[0]
    _, rows, padded = arrived.shape
    heads, lat, vdim = value_proj.shape
    smem = pl.BlockSpec(memory_space=pltpu.SMEM)
    vmem = pl.BlockSpec(memory_space=pltpu.VMEM)
    return pl.pallas_call(
        attend_kernel,
        out_shape=jax.ShapeDtypeStruct((rows, heads * vdim + LANES), S16),
        in_specs=[smem, smem, smem, vmem, pl.BlockSpec(memory_space=pl.ANY), vmem],
        out_specs=vmem,
        scratch_shapes=[
            pltpu.VMEM((count, rows, padded), S16),
            pltpu.VMEM((count * rows, padded), BF16),
            pltpu.VMEM((count * rows, padded), BF16),
            pltpu.VMEM((heads * rows, count * rows), F32),
            pltpu.SemaphoreType.DMA((count,)),
        ],
        compiler_params=pltpu.CompilerParams(vmem_limit_bytes=LIMIT),
        cost_estimate=pl.CostEstimate(flops=7 * 10**9, bytes_accessed=8 * 10**6, transcendentals=10**6),
        name="attend",
    )(places, block_ids, own, q, arrived, value_proj)


def project_kernel(rows_in, weights, out, wide):
    chips, groups, rows, padded = rows_in.shape
    inner = padded - LANES
    cores, _, _, columns = weights.shape
    sums = [None] * cores
    for g in range(groups):
        factor = scale_of(as_f32(rows_in[:, g, :, inner:]).reshape(chips * rows, LANES))[:, :1]
        a = as_f32(rows_in[:, g, :, :inner]).reshape(chips * rows, inner)
        a = (a * factor).astype(BF16)
        for k in range(cores):
            term = dot_nn(a, weights[k, g])
            sums[k] = term if g == 0 else sums[k] + term
    for k in range(cores):
        code = row_code(jnp.max(jnp.abs(sums[k]), axis=-1, keepdims=True))
        wide[:, :columns] = sums[k]
        lanes = lane_ids(wide.shape)
        full = jnp.where(lanes < columns, to_int(wide[...], code), code)
        out[k] = as_s16(full).reshape(out.shape[1:])


def project(rows_in, weights):
    chips, groups, rows, padded = rows_in.shape
    cores, _, inner, columns = weights.shape
    vmem = pl.BlockSpec(memory_space=pltpu.VMEM)
    return pl.pallas_call(
        project_kernel,
        out_shape=jax.ShapeDtypeStruct((cores, chips, rows, 2 * LANES), S16),
        in_specs=[vmem, vmem],
        out_specs=vmem,
        scratch_shapes=[pltpu.VMEM((chips * rows, 2 * LANES), F32)],
        compiler_params=pltpu.CompilerParams(vmem_limit_bytes=LIMIT),
        cost_estimate=pl.CostEstimate(flops=10**9, bytes_accessed=7 * 10**6, transcendentals=0),
        name="project",
    )(rows_in, weights)


def add_kernel(parts, out):
    cores, outer, groups, rows, _ = parts.shape
    columns = out.shape[-1]
    for k in range(cores):
        for g in range(groups):
            total = None
            for z in range(outer):
                x = as_f32(parts[k, z, g])
                x = x * scale_of(x[:, LANES:])[:, LANES - 1 :]
                total = x if z == 0 else total + x
            at = (k * groups + g) * rows
            out[at : at + rows, :] = total[:, :columns].astype(BF16)


def add_parts(parts, columns):
    cores, _, groups, rows, _ = parts.shape
    vmem = pl.BlockSpec(memory_space=pltpu.VMEM)
    return pl.pallas_call(
        add_kernel,
        out_shape=jax.ShapeDtypeStruct((cores * groups * rows, columns), BF16),
        in_specs=[vmem],
        out_specs=vmem,
        name="add_parts",
    )(parts)


def on_device(queries, latent, selected, value_proj, out_proj):
    plane = ("x", "y", "core")
    ctx_count = lax.axis_size(plane)
    ctx_index = lax.axis_index(plane)
    block_rows, heads, width = queries.shape
    per_owner = latent.shape[0] // block_rows
    key_blocks = per_owner * ctx_count
    padded = -(-width // LANES) * LANES
    columns = out_proj.shape[1]

    weights = lax.all_gather(out_proj, ("core", "zl"), axis=0, tiled=False)
    weights = weights.reshape(2, ZL, *out_proj.shape)

    offset = selected - ctx_index * per_owner
    mine = (offset >= 0) & (offset < per_owner)
    first = jnp.min(jnp.where(mine, offset, per_owner - 1), axis=1)
    last = jnp.max(jnp.where(mine, offset, 0), axis=1)
    ids = jnp.stack([first, last], axis=1)
    parcels = make_parcels(ids, latent.reshape(per_owner, block_rows, width), ctx_count, padded)
    arrived = lax.all_to_all(parcels, plane, split_axis=0, concat_axis=0, tiled=True)

    own_list = lax.dynamic_slice_in_dim(selected, ctx_index, 1, 0)[0]
    owner = own_list // per_owner
    second = jnp.any((owner[None, :] == owner[:, None]) & (own_list[None, :] < own_list[:, None]), axis=1)
    places = owner * 2 + second.astype(jnp.int32)
    own = (key_blocks - ctx_count + ctx_index)[None].astype(jnp.int32)

    q = jnp.transpose(queries, (1, 0, 2)).reshape(heads * block_rows, width)
    q = jnp.pad(q, ((0, 0), (0, padded - width)))
    head_out = attend(
        places, own_list, own, q, arrived.reshape(2 * ctx_count, block_rows, padded), value_proj
    )

    rows = block_rows // ZL
    traded = lax.all_to_all(
        head_out.reshape(ZL, rows, head_out.shape[1]), "zl", split_axis=0, concat_axis=0, tiled=True
    )
    gathered = lax.all_gather(traded, ("x", "y"), axis=0, tiled=False)
    partial = project(gathered, weights)
    sent = lax.all_to_all(
        partial.reshape(-1, rows, 2 * LANES), ("core", "zh", "zl"), split_axis=0, concat_axis=0, tiled=True
    )
    return add_parts(sent.reshape(2, -1, ZL, rows, 2 * LANES), columns)


def solution(mesh):
    shape = (4, 4, 2, mesh.shape["head"] // ZL, ZL)
    fine = Mesh(mesh.devices.reshape(shape), ("x", "y", "core", "zh", "zl"))
    ctx, head = ("x", "y", "core"), ("zh", "zl")
    in_specs = (
        P(ctx, head, None),
        P(ctx, None),
        P(),
        P(head, None, None),
        P(head, ctx),
    )
    return jax.shard_map(on_device, mesh=fine, in_specs=in_specs, out_specs=P(head, ctx), check_vma=False)
```

time: 381 us -> 205 us (0.54)
  the two profiles are of different devices: /device:TPU:8 before, /device:TPU:1 now
where the time goes in v1:
time: 205 us
  blocking collectives  76.5 us (37%)
  waiting for transfers between devices  60.3 us (29%)
  Pallas kernels  28.1 us (14%)
  between operations  13.5 us (7%)
  local copies, waits for them, and re-layouts  12.3 us (6%)
  starting transfers between devices  11.5 us (6%)
  other arithmetic  2.44 us (1%)
    all_to_all x1, waiting for transfers between devices, on_device(): lax.all_to_all(parcels, plane, split_axis=0, concat_axis=0, tiled=True)  59.6 us
    all_to_all x1, blocking collectives, on_device(): lax.all_to_all(partial.reshape(-1, rows, 2 * LANES), ('core', 'zh', 'zl')...  40.3 us
    all_gather x1, blocking collectives, on_device(): gathered = lax.all_gather(traded, ('x', 'y'), axis=0, tiled=False)  24.4 us
    pallas_call x1, Pallas kernels, attend(): pl.pallas_call(attend_kernel, out_shape=jax.ShapeDtypeStruct((rows, heads...  18.6 us
    all_to_all x1, blocking collectives, on_device(): lax.all_to_all(head_out.reshape(ZL, rows, head_out.shape[1]), 'zl', split...  11.8 us
    all_to_all x1, starting transfers between devices, on_device(): lax.all_to_all(parcels, plane, split_axis=0, concat_axis=0, tiled=True)  11.5 us
    all_gather x1, local copies, waits for them, and re-layouts, on_device(): weights = lax.all_gather(out_proj, ('core', 'zl'), axis=0, tiled=False)  6.25 us
  transfers between devices with their start and end apart: 2, of which 1 were waited for; matrix products, arithmetic and copies ran while one was open for 2% of the time, Pallas kernels for 9%

profile of v1, /device:TPU:1, one launch (start us, length us, event | category | flops | bytes accessed | tf_op | source)
XLA Modules:
  0.0 204.6 jit_solution(5110751675145386906)
XLA Ops:
  6.5 0.8 select_reduce_fusion.1
  7.4 0.1 copy.19.ids
  7.5 1.7 copy.18
  9.2 4.1 %parcels.1 = s16[32,2,64,640]{3,2,1,0:T(8,128)(2,1)} custom-call(s32[32,2]{1,0:T(8,128)S(1)} %copy.19.ids, f32[8,64,576]{2,1,0:T(8,128)S(1)} %bitcast.18), custom_call_target="tpu_custom_call" | custom-call | flops 10000000 | bytes 7000000 | tf_op jit(solution)/shard_map/parcels/pallas_call | solution.py:80
  13.2 0.0 copy-start.1
  13.2 11.5 %all-to-all-start = ((s16[32,2,64,640]{3,2,1,0:T(8,128)(2,1)}), s16[32,2,64,640]{3,2,1,0:T(8,128)(2,1)}, u32[]{:S(2)}, u32[]{:S(2)}) async-start(s16[32,2,64,640]{3,2,1,0:T(8,128)(2,1)} %parcels.1), calls=%async_computation | async-start | bytes 10485760 | tf_op jit(solution)/shard_map/all_to_all | solution.py:258
  24.7 0.0 all-gather.5.cloned.1.call-start
  24.8 0.7 all-gather.5.cloned.1.call-update
  25.5 0.0 copy-start
  25.5 1.3 copy.17
  26.8 1.4 pad.4.q
  28.2 0.7 fusion
  28.9 0.7 and_select_fusion.1
  29.6 0.2 and_reduce_fusion
  29.8 59.6 %all-to-all-done = s16[32,2,64,640]{3,2,1,0:T(8,128)(2,1)} async-done(((s16[32,2,64,640]{3,2,1,0:T(8,128)(2,1)}), s16[32,2,64,640]{3,2,1,0:T(8,128)(2,1)}, u32[]{:S(2)}, u32[]{:S(2)}) %all-to-all-start) | async-done | bytes 5242912 | tf_op jit(solution)/shard_map/all_to_all | solution.py:258
  89.4 18.6 %attend.1 = s16[64,1152]{1,0:T(8,128)(2,1)S(1)} custom-call(s32[32]{0:T(128)S(1)} %convert_add_fusion.places, s32[32]{0:T(128)S(1)} %get-tuple-element.8.block_ids, s32[1]{0:T(128)} %bitcast.2.own, f32[512,640]{1,0:T(8,128)S(1)} %pad.4.q, s16[64,64,640]{2,1,0:T(8,128)(2,1)} %bitcast.8.arrived, bf16[8,512,128]{2,1,0:T(8,128)(2,1)S(1)} %copy-done), custom_call_target="tpu_custom_call" | custom-call | flops 7000000000 | bytes 8000000 | tf_op jit(solution)/shard_map/attend/pallas_call | solution.py:159
  108.0 11.8 %all_to_all.15 = s16[4,16,1152]{2,1,0:T(8,128)(2,1)S(1)} all-to-all(s16[4,16,1152]{2,1,0:T(8,128)(2,1)S(1)} %bitcast.20), channel_id=1, replica_groups=mesh['x'=4,'y'=4,'core'=2,'zh'=4,'zl'=4] {'zl'}, dimensions={0} | all-to-all | bytes 294912 | tf_op jit(solution)/shard_map/all_to_all | solution.py:273
  119.8 24.4 %all-gather.6 = s16[64,16,1152]{2,1,0:T(8,128)(2,1)S(1)} all-gather(s16[4,16,1152]{2,1,0:T(8,128)(2,1)S(1)} %all_to_all.15), channel_id=2, replica_groups=mesh['x'=4,'y'=4,'core'=2,'zh'=4,'zl'=4] {'x','y'}, dimensions={0}, use_global_device_ids=true | all-gather | bytes 2506752 | tf_op jit(solution)/shard_map/all_gather | solution.py:276
  144.2 0.0 all-gather.5.cloned.1.call-done
  144.2 6.2 %copy.20 = bf16[8192,224]{1,0:T(8,128)(2,1)} copy(bf16[8192,224]{0,1:T(8,128)(2,1)} %all-gather.5.cloned.1.call-done) | data formatting | bytes 7340032 | tf_op jit(solution)/shard_map/all_gather | solution.py:249
  150.5 3.7 %project.1 = s16[2,16,16,256]{3,2,1,0:T(8,128)(2,1)S(1)} custom-call(s16[16,4,16,1152]{3,2,1,0:T(8,128)(2,1)S(1)} %bitcast.17, bf16[2,4,1024,224]{3,2,1,0:T(8,128)(2,1)} %bitcast.21), custom_call_target="tpu_custom_call" | custom-call | flops 1000000000 | bytes 7000000 | tf_op jit(solution)/shard_map/project/pallas_call | solution.py:201
  154.2 40.3 %all_to_all.16 = s16[32,16,256]{2,1,0:T(8,128)(2,1)} all-to-all(s16[32,16,256]{2,1,0:T(8,128)(2,1)S(1)} %bitcast.19), channel_id=1, replica_groups=mesh['x'=4,'y'=4,'core'=2,'zh'=4,'zl'=4] {'core','zh','zl'}, dimensions={0} | all-to-all | bytes 524288 | tf_op jit(solution)/shard_map/all_to_all | solution.py:278
  194.5 1.7 add_parts.1
  196.2 1.6 copy.21
  (4 shorter events, 0.0 us)
Async XLA Ops:
  13.2 12.2 %copy-start.1 = (f32[64,8,576]{2,1,0:T(8,128)S(1)}, f32[64,8,576]{2,1,0:T(8,128)}, u32[]{:S(2)}) copy-start(f32[64,8,576]{2,1,0:T(8,128)} %param.5) | copy-start | bytes 3538948
  13.2 76.2 %all-to-all-start = ((s16[32,2,64,640]{3,2,1,0:T(8,128)(2,1)}), s16[32,2,64,640]{3,2,1,0:T(8,128)(2,1)}, u32[]{:S(2)}, u32[]{:S(2)}) async-start(s16[32,2,64,640]{3,2,1,0:T(8,128)(2,1)} %parcels.1), calls=%async_computation | async-start | bytes 10485760 | tf_op jit(solution)/shard_map/all_to_all | solution.py:258
  24.7 119.5 %all-gather.5.cloned.1.call-start = ((), (), s32[]{:S(2)}) async-start(), calls=%async_computation.3 | async-start | bytes 4128768 | tf_op jit(solution)/shard_map/all_gather | solution.py:249
  25.5 63.9 %copy-start = (bf16[8,512,128]{2,1,0:T(8,128)(2,1)S(1)}, bf16[8,512,128]{2,1,0:T(8,128)(2,1)}, u32[]{:S(2)}) copy-start(bf16[8,512,128]{2,1,0:T(8,128)(2,1)} %value_proj.1) | copy-start | bytes 3145732
Sparse Core Ops, SparseCore 0:
  27.7 91.4 all-gather.4

commit v2 on v1

v2 whole, which is shorter than its diff:
```python
import functools
import math

import jax
import jax.numpy as jnp
from jax import lax
from jax.experimental import pallas as pl
from jax.experimental.pallas import tpu as pltpu
from jax.sharding import Mesh
from jax.sharding import PartitionSpec as P

NEG = -1e30
SCALE = 1.0 / 192.0**0.5
LOG2E = math.log2(math.e)
F32, BF16, S16 = jnp.float32, jnp.bfloat16, jnp.int16
LANES = 128
PAIR = 2
LIMIT = 48 * 1024 * 1024
WHOLE = 60 * 1024 * 1024
SMEM = pl.BlockSpec(memory_space=pltpu.SMEM)
VMEM = pl.BlockSpec(memory_space=pltpu.VMEM)
ANY = pl.BlockSpec(memory_space=pl.ANY)
HBM = pl.BlockSpec(memory_space=pltpu.HBM)
PARAMS = pltpu.CompilerParams(vmem_limit_bytes=LIMIT)


def row_code(peak):
    return jnp.ceil(jnp.log2(jnp.maximum(peak, 1e-30)) * 256.0)


def to_int(x, code):
    y = jnp.round(x * (jnp.exp2(code * (-1.0 / 256.0)) * 32767.0))
    return jnp.clip(y, -32767.0, 32767.0)


def scale_of(code):
    return jnp.exp2(code * (1.0 / 256.0)) * (1.0 / 32767.0)


def as_s16(x):
    return x.astype(jnp.int32).astype(S16)


def as_f32(x):
    return x.astype(jnp.int32).astype(F32)


def row_peak(x):
    return jnp.max(jnp.abs(x), axis=-1, keepdims=True)


def lane_ids(shape):
    return lax.broadcasted_iota(jnp.int32, shape, len(shape) - 1)


def dot_nt(a, b):
    return lax.dot_general(a, b, (((1,), (1,)), ((), ())), preferred_element_type=F32)


def dot_nn(a, b):
    return jnp.dot(a, b, preferred_element_type=F32)


def halves(x):
    high = x.astype(BF16)
    return high, (x - high.astype(F32)).astype(BF16)


def cost(flops, nbytes, exps=0):
    return pl.CostEstimate(flops=flops, bytes_accessed=nbytes, transcendentals=exps)


def parcel_kernel(where, selected, latent_t, out, lists, stage, wide, coded, ids_v, ids, in_sems, id_sems, sems):
    width, total = latent_t.shape
    blocks, part, padded = coded.shape
    block = total // blocks
    groups = total // LANES
    fetch = pltpu.make_async_copy(selected, lists, id_sems.at[0])
    fetch.start()
    loads = []
    for n in range(groups):
        columns = pl.ds(n * LANES, LANES)
        load = pltpu.make_async_copy(latent_t.at[:, columns], stage.at[:, columns], in_sems.at[n])
        load.start()
        loads.append(load)
    fetch.wait()
    offset = lists[...] - where[0]
    mine = (offset >= 0) & (offset < blocks)
    first = jnp.min(jnp.where(mine, offset, blocks - 1), axis=1, keepdims=True)
    last = jnp.max(jnp.where(mine, offset, 0), axis=1, keepdims=True)
    ids_v[...] = jnp.where(lane_ids(ids_v.shape) == 0, first, last)
    move = pltpu.make_async_copy(ids_v, ids, id_sems.at[1])
    move.start()
    lanes = lane_ids((part, padded))
    for n in range(groups):
        loads[n].wait()
        wide[:, :width] = stage[:, n * LANES : (n + 1) * LANES].T
        for m in range(LANES // block):
            at = pl.multiple_of(m * block + where[1], part)
            x = jnp.where(lanes < width, wide[pl.ds(at, part), :], 0.0)
            code = row_code(row_peak(x))
            full = jnp.where(lanes < width, to_int(x, code), code)
            coded[n * (LANES // block) + m] = as_s16(full)
    move.wait()
    copies = []
    for d in range(out.shape[0]):
        for s in range(2):
            copy = pltpu.make_async_copy(coded.at[ids[d, s]], out.at[d, s], sems.at[2 * d + s])
            copy.start()
            copies.append(copy)
    for copy in copies:
        copy.wait()


def make_parcels(where, selected, latent_t, blocks, part, padded):
    receivers = selected.shape[0]
    width, total = latent_t.shape
    return pl.pallas_call(
        parcel_kernel,
        out_shape=jax.ShapeDtypeStruct((receivers, 2, part, padded), S16),
        in_specs=[SMEM, HBM, HBM],
        out_specs=HBM,
        scratch_shapes=[
            pltpu.VMEM(selected.shape, jnp.int32),
            pltpu.VMEM((width, total), F32),
            pltpu.VMEM((LANES, padded), F32),
            pltpu.VMEM((blocks, part, padded), S16),
            pltpu.VMEM((receivers, LANES), jnp.int32),
            pltpu.SMEM((receivers, LANES), jnp.int32),
            pltpu.SemaphoreType.DMA((total // LANES,)),
            pltpu.SemaphoreType.DMA((2,)),
            pltpu.SemaphoreType.DMA((2 * receivers,)),
        ],
        compiler_params=pltpu.CompilerParams(vmem_limit_bytes=WHOLE),
        cost_estimate=cost(10**7, 4 * 10**6),
        name="parcels",
    )(where, selected, latent_t)


def pack_kernel(q, out, wide):
    width = q.shape[-1]
    wide[:, :width] = q[...]
    lanes = lane_ids(wide.shape)
    x = jnp.where(lanes < width, wide[...], 0.0)
    code = row_code(row_peak(x))
    out[...] = as_s16(jnp.where(lanes < width, to_int(x, code), code))


def pack_queries(q, padded):
    rows = q.shape[0]
    return pl.pallas_call(
        pack_kernel,
        out_shape=jax.ShapeDtypeStruct((rows, padded), S16),
        in_specs=[VMEM],
        out_specs=VMEM,
        scratch_shapes=[pltpu.VMEM((rows, padded), F32)],
        compiler_params=PARAMS,
        cost_estimate=cost(10**7, 2 * 10**6),
        name="pack_queries",
    )(q)


def split_kernel(core, own, other, out):
    rows, padded = own.shape
    lat = padded - LANES
    half = rows // 2
    rope = lane_ids((half, LANES)) < LANES // 2
    orders = ((own, 0), (own, half), (other, core[0] * half), (other, (1 - core[0]) * half))
    for n, (q, at) in enumerate(orders):
        span = slice(n * half, (n + 1) * half)
        wide = as_f32(q[pl.ds(at if n < 2 else pl.multiple_of(at, half), half), :])
        wide = wide * (scale_of(wide[:, lat:])[:, LANES - 1 :] * (SCALE * LOG2E))
        high, low = halves(wide[:, :lat])
        out[span, :lat] = high
        out[span, lat : 2 * lat] = low
        tail = jnp.where(rope, wide[:, lat:], 0.0)
        high, low = halves(tail)
        both = high.astype(F32) + pltpu.roll(low.astype(F32), LANES // 2, 1)
        out[span, 2 * lat : 2 * lat + LANES] = both.astype(BF16)
        out[span, 2 * lat + LANES :] = high


def split_queries(core, own, other):
    rows, padded = own.shape
    return pl.pallas_call(
        split_kernel,
        out_shape=jax.ShapeDtypeStruct((PAIR * rows, 2 * padded), BF16),
        in_specs=[SMEM, VMEM, VMEM],
        out_specs=VMEM,
        compiler_params=PARAMS,
        cost_estimate=cost(10**7, 4 * 10**6),
        name="split_queries",
    )(core, own, other)


def attend_kernel(
    places, block_ids, own, q, arrived, vp_own, fetched, passed, out, slots, keys_s, sems
):
    count = places.shape[0]
    part, padded = slots.shape[1:]
    heads, lat, vdim = vp_own.shape
    block = out.shape[0]
    keys = count * part
    tile = q.shape[0] // PAIR
    copies = []
    for i in range(count):
        copy = pltpu.make_async_copy(arrived.at[places[i]], slots.at[i], sems.at[i])
        copy.start()
        copies.append(copy)
    some = fetched.shape[0]
    step = 8
    rope = lane_ids((step * part, LANES)) < LANES // 2
    for c in range(count // step):
        for i in range(c * step, (c + 1) * step):
            copies[i].wait()
        wide = as_f32(slots[c * step : (c + 1) * step].reshape(step * part, padded))
        wide = wide * scale_of(wide[:, lat:])[:, LANES - 1 :]
        span = slice(c * step * part, (c + 1) * step * part)
        high, low = halves(wide[:, :lat])
        keys_s[span, :lat] = high
        keys_s[span, lat : 2 * lat] = low
        tail = jnp.where(rope, wide[:, lat:], 0.0)
        keys_s[span, 2 * lat : 2 * lat + LANES] = (tail + pltpu.roll(tail, LANES // 2, 1)).astype(BF16)
        keys_s[span, 2 * lat + LANES :] = halves(tail)[1]
    lane = lane_ids((1, keys))
    room = jnp.zeros((1, keys), jnp.int32)
    for i in range(count):
        room = jnp.where(lane // part == i, (own[0] - block_ids[i]) * block - own[1], room)
    room = room - lane % part
    spot = lax.broadcasted_iota(jnp.int32, (tile, 1), 0) % block
    results, stats = [], []
    for t in range(PAIR):
        span = slice(t * tile, (t + 1) * tile)
        s = (
            dot_nt(q[span, :lat], keys_s[:, :lat])
            + dot_nt(q[span, lat : 2 * lat], keys_s[:, :lat])
            + dot_nt(q[span, :lat], keys_s[:, lat : 2 * lat])
            + dot_nt(q[span, 2 * lat :], keys_s[:, 2 * lat :])
        )
        s = jnp.where(room + spot >= 0, s, NEG)
        peak = jnp.max(s, axis=-1, keepdims=True)
        p = jnp.exp2(s - peak)
        norm = jnp.sum(p, axis=-1, keepdims=True)
        high, low = halves(p)
        mixed = (
            dot_nn(high, keys_s[:, :lat]) + dot_nn(high, keys_s[:, lat : 2 * lat]) + dot_nn(low, keys_s[:, :lat])
        )
        high, low = halves(mixed / norm)
        stats.append(peak + jnp.log2(norm))
        for h in range(heads):
            rows = slice(h * block, (h + 1) * block)
            maps = vp_own[h] if t == 0 else (fetched[h] if h < some else passed[h - some])
            both = dot_nn(jnp.concatenate([high[rows], low[rows]], axis=0), maps)
            results.append(both[:block] + both[block:])
    head_out = jnp.concatenate(results, axis=-1)
    code = row_code(row_peak(head_out))
    inner = head_out.shape[-1]
    coded = as_s16(to_int(head_out, code))
    half = inner // PAIR
    width = some * vdim
    out[:, :half] = coded[:, :half]
    for n, turn in enumerate((own[2], 1 - own[2])):
        at = pl.multiple_of(half + turn * width, width)
        out[:, pl.ds(at, width)] = coded[:, half + n * width : half + (n + 1) * width]
    lane = lane_ids((block, LANES))
    tail = code
    for n in range(PAIR * heads):
        stat = stats[n // heads][(n % heads) * block : (n % heads + 1) * block] * 2.0
        coarse = jnp.floor(stat)
        at = n
        if n >= heads:
            turn = own[2] if n < heads + some else 1 - own[2]
            at = heads + turn * some + n % some
        tail = jnp.where(lane == at, coarse, tail)
        tail = jnp.where(lane == at + PAIR * heads, (stat - coarse) * 32767.0, tail)
    out[:, inner:] = as_s16(tail)


def attend(places, block_ids, own, q, arrived, vp_own, fetched, passed):
    count = places.shape[0]
    _, part, padded = arrived.shape
    heads, _, vdim = vp_own.shape
    block = q.shape[0] // (PAIR * heads)
    return pl.pallas_call(
        attend_kernel,
        out_shape=jax.ShapeDtypeStruct((block, PAIR * heads * vdim + LANES), S16),
        in_specs=[SMEM, SMEM, SMEM, VMEM, HBM, VMEM, VMEM, VMEM],
        out_specs=VMEM,
        scratch_shapes=[
            pltpu.VMEM((count, part, padded), S16),
            pltpu.VMEM((count * part, 2 * padded), BF16),
            pltpu.SemaphoreType.DMA((count,)),
        ],
        compiler_params=PARAMS,
        cost_estimate=cost(7 * 10**9, 8 * 10**6, 10**6),
        name="attend",
    )(places, block_ids, own, q, arrived, vp_own, fetched, passed)


def merge_kernel(parts, out, *, heads):
    sources, rows, padded = parts.shape
    inner = padded - LANES
    vdim = inner // (PAIR * heads)
    tails = [as_f32(parts[n, :, inner:]) for n in range(sources)]
    logs = [(x + pltpu.roll(x, LANES - PAIR * heads, 1) * (1.0 / 32767.0)) * 0.5 for x in tails]
    scales = [scale_of(x)[:, LANES - 1 :] for x in tails]
    merged = []
    for g in range(sources):
        near, far = g, g ^ 1
        a, b = logs[near], pltpu.roll(logs[far], LANES - heads, 1)
        top = jnp.maximum(a, b)
        a, b = jnp.exp2(a - top), jnp.exp2(b - top)
        total = a + b
        a, b = a / total * scales[near], b / total * scales[far]
        for h in range(heads):
            x = as_f32(parts[near, :, h * vdim : (h + 1) * vdim]) * a[:, h : h + 1]
            y = as_f32(parts[far, :, (heads + h) * vdim : (heads + h + 1) * vdim]) * b[:, h : h + 1]
            merged.append((x + y).astype(BF16).astype(F32))
    head_out = jnp.concatenate(merged, axis=-1)
    code = row_code(row_peak(head_out))
    width = head_out.shape[-1]
    out[:, :width] = as_s16(to_int(head_out, code))
    out[:, width:] = as_s16(jnp.broadcast_to(code, (rows, LANES)))


def merge(parts, heads):
    sources, rows, padded = parts.shape
    return pl.pallas_call(
        functools.partial(merge_kernel, heads=heads),
        out_shape=jax.ShapeDtypeStruct((rows, sources * (padded - LANES) // PAIR + LANES), S16),
        in_specs=[VMEM],
        out_specs=VMEM,
        compiler_params=PARAMS,
        cost_estimate=cost(10**6, 5 * 10**5),
        name="merge",
    )(parts)


def project_kernel(place, rows_in, near_own, near_other, far_own, far_other, out, wide):
    chips, rows, padded = rows_in.shape
    inner = padded - LANES
    columns, depth = near_own.shape
    core = place[0]
    factor = scale_of(as_f32(rows_in[:, :, inner:]).reshape(chips * rows, LANES))[:, :1]
    sums = [None, None]
    for n, member in enumerate((place[1], 1 - place[1])):
        at = pl.multiple_of(member * depth, depth)
        a = as_f32(rows_in[:, :, pl.ds(at, depth)]).reshape(chips * rows, depth)
        a = (a * factor).astype(BF16)
        for k, weights in enumerate(((near_own, far_own), (near_other, far_other))[n]):
            term = dot_nt(a, weights[...])
            sums[k] = term if n == 0 else sums[k] + term
    lanes = lane_ids(wide.shape)
    for k, at in enumerate((core, 1 - core)):
        code = row_code(row_peak(sums[k]))
        wide[:, :columns] = sums[k]
        full = jnp.where(lanes < columns, to_int(wide[...], code), code)
        out[at] = as_s16(full).reshape(out.shape[1:])


def project(place, rows_in, near_own, near_other, far_own, far_other):
    chips, rows, _ = rows_in.shape
    return pl.pallas_call(
        project_kernel,
        out_shape=jax.ShapeDtypeStruct((2, chips, rows, 2 * LANES), S16),
        in_specs=[SMEM] + [VMEM] * 5,
        out_specs=VMEM,
        scratch_shapes=[pltpu.VMEM((chips * rows, 2 * LANES), F32)],
        compiler_params=PARAMS,
        cost_estimate=cost(10**9, 7 * 10**6),
        name="project",
    )(place, rows_in, near_own, near_other, far_own, far_other)


def add_kernel(parts, out):
    cores, outer, groups, rows, _ = parts.shape
    pieces = []
    for k in range(cores):
        for g in range(groups):
            total = None
            for z in range(outer):
                x = as_f32(parts[k, z, g])
                x = x * scale_of(x[:, LANES:])[:, LANES - 1 :]
                total = x if z == 0 else total + x
            pieces.append(total)
    full = jnp.concatenate(pieces, axis=0)
    out[...] = full.T[: out.shape[0], :].astype(BF16)


def add_parts(parts, columns):
    cores, _, groups, rows, _ = parts.shape
    return pl.pallas_call(
        add_kernel,
        out_shape=jax.ShapeDtypeStruct((columns, cores * groups * rows), BF16),
        in_specs=[VMEM],
        out_specs=VMEM,
        name="add_parts",
    )(parts)


def on_device(queries, latent, selected, value_proj, out_proj):
    plane = ("x", "y", "core")
    ctx_count = lax.axis_size(plane)
    ctx_index = lax.axis_index(plane)
    core = lax.axis_index("core").astype(jnp.int32)
    member = lax.axis_index("zb").astype(jnp.int32)
    block, heads, width = queries.shape
    per_owner = latent.shape[0] // block
    key_blocks = per_owner * ctx_count
    padded = -(-width // LANES) * LANES
    columns = out_proj.shape[1]
    part = block // PAIR
    swap = [(0, 1), (1, 0)]
    start = member * part

    where = jnp.stack([(ctx_index * per_owner).astype(jnp.int32), start])
    parcels = make_parcels(where, selected, latent.T, per_owner, part, padded)
    parcels, queries, value_near = lax.optimization_barrier((parcels, queries, value_proj))
    arrived = lax.all_to_all(parcels, plane, split_axis=0, concat_axis=0, tiled=True)

    q = jnp.transpose(queries, (1, 0, 2)).reshape(heads * block, width)
    q_own = pack_queries(q, padded)
    q_other = lax.ppermute(q_own, "zb", swap)
    near_own = out_proj.T
    q_other, near_own = lax.optimization_barrier((q_other, near_own))
    near_other = lax.ppermute(near_own, "zb", swap)
    far_own = lax.ppermute(near_own, "core", swap)
    q_split = split_queries(core[None], q_own, q_other)
    q_own, listed = lax.optimization_barrier((q_own, selected))
    own_list = lax.dynamic_slice_in_dim(listed, ctx_index, 1, 0)[0]
    owner = own_list // per_owner
    second = jnp.any((owner[None, :] == owner[:, None]) & (own_list[None, :] < own_list[:, None]), axis=1)
    places = owner * 2 + second.astype(jnp.int32)
    places, value_near = lax.optimization_barrier((places, value_near))
    fetched = lax.ppermute(lax.dynamic_slice_in_dim(value_near, core * (heads // 2), heads // 2, 0), "zb", swap)
    passed = lax.ppermute(fetched, "core", swap)

    own = jnp.stack([(key_blocks - ctx_count + ctx_index).astype(jnp.int32), start, core])
    arrived = arrived.reshape(2 * ctx_count, part, padded)
    halves_out = attend(places, own_list, own, q_split, arrived, value_proj, fetched, passed)

    halves_out, near_other = lax.optimization_barrier((halves_out, near_other))
    far_other = lax.ppermute(near_other, "core", swap)
    traded = lax.all_to_all(
        halves_out.reshape(PAIR, part, halves_out.shape[1]), "zb", split_axis=0, concat_axis=0, tiled=True
    )
    gathered = lax.all_gather(merge(traded, heads), ("x", "y"), axis=0, tiled=False)
    partial = project(jnp.stack([core, member]), gathered, near_own, near_other, far_own, far_other)
    sent = lax.all_to_all(
        partial.reshape(-1, part, 2 * LANES), ("core", "zq", "zb"), split_axis=0, concat_axis=0, tiled=True
    )
    return add_parts(sent.reshape(2, -1, PAIR, part, 2 * LANES), columns).T


def solution(mesh):
    shape = (4, 4, 2, mesh.shape["head"] // PAIR, PAIR)
    fine = Mesh(mesh.devices.reshape(shape), ("x", "y", "core", "zq", "zb"))
    ctx, head = ("x", "y", "core"), ("zq", "zb")
    in_specs = (
        P(ctx, head, None),
        P(ctx, None),
        P(),
        P(head, None, None),
        P(head, ctx),
    )
    return jax.shard_map(on_device, mesh=fine, in_specs=in_specs, out_specs=P(head, ctx), check_vma=False)
```

time: 205 us -> 156 us (0.76)
  waiting for transfers between devices: 60.3 us -> 19.8 us
  starting transfers between devices: 11.5 us -> 31.5 us
  between operations: 13.5 us -> 0.22 us
  local copies, waits for them, and re-layouts: 12.3 us -> 3.49 us
  blocking collectives: 76.5 us -> 72.8 us
  Pallas kernels: 28.1 us -> 24.5 us
    all_to_all x1, waiting for transfers between devices: 59.6 us -> 0.01 us  [on_device(): lax.all_to_all(parcels, plane, split_axis=0, concat_axis=0, tiled=True)]
    ppermute x0 -> x6, waiting for transfers between devices: none -> 19.8 us  [the longest x1 9.95 us: on_device(): q_other = lax.ppermute(q_own, 'zb', swap)]
    ppermute x0 -> x6, starting transfers between devices: none -> 16.6 us  [the longest x1 4 us: on_device(): passed = lax.ppermute(fetched, 'core', swap)]
    all_gather x1 -> x0, local copies, waits for them, and re-layouts: 6.25 us -> none  [on_device(): weights = lax.all_gather(out_proj, ('core', 'zl'), axis=0, tiled=False)]
    pallas_call x3 -> x6, Pallas kernels: 24 us -> 19.4 us  [the longest x1 12.9 us: attend(): pl.pallas_call(attend_kernel, out_shape=jax.ShapeDtypeStruct((block, PAIR...]
    all_to_all x0 -> x1, starting transfers between devices: none -> 3.46 us  [on_device(): lax.all_to_all(halves_out.reshape(PAIR, part, halves_out.shape[1]), 'zb',...]
    all_to_all x2 -> x1, blocking collectives: 52.1 us -> 49.4 us  [on_device(): lax.all_to_all(partial.reshape(-1, part, 2 * LANES), ('core', 'zq', 'zb')...]
  transfers between devices with their start and end apart: 2 -> 8, of which waited for: 1 -> 2; matrix products, arithmetic and copies ran while one was open for 2% -> 1% of each run, Pallas kernels for 9% -> 9%
where the time goes in v2:
time: 156 us; the launch traced here: 155 us
  blocking collectives  72.8 us (47%)
  starting transfers between devices  31.5 us (20%)
  Pallas kernels  24.5 us (16%)
  waiting for transfers between devices  19.8 us (13%)
  local copies, waits for them, and re-layouts  3.49 us (2%)
  other arithmetic  2.31 us (1%)
    all_to_all x1, blocking collectives, on_device(): lax.all_to_all(partial.reshape(-1, part, 2 * LANES), ('core', 'zq', 'zb')...  49.4 us
    all_gather x1, blocking collectives, on_device(): lax.all_gather(merge(traded, heads), ('x', 'y'), axis=0, tiled=False)  23.3 us
    pallas_call x1, Pallas kernels, attend(): pl.pallas_call(attend_kernel, out_shape=jax.ShapeDtypeStruct((block, PAIR...  12.9 us
    all_to_all x1, starting transfers between devices, on_device(): lax.all_to_all(parcels, plane, split_axis=0, concat_axis=0, tiled=True)  11.4 us
    ppermute x1, waiting for transfers between devices, on_device(): q_other = lax.ppermute(q_own, 'zb', swap)  9.95 us
    ppermute x1, waiting for transfers between devices, on_device(): lax.ppermute(lax.dynamic_slice_in_dim(value_near, core * (heads // 2), he...  9.79 us
    pallas_call x1, Pallas kernels, make_parcels(): pl.pallas_call(parcel_kernel, out_shape=jax.ShapeDtypeStruct((receivers,...  5.18 us
    ppermute x1, starting transfers between devices, on_device(): passed = lax.ppermute(fetched, 'core', swap)  4 us
  transfers between devices with their start and end apart: 8, of which 2 were waited for; matrix products, arithmetic and copies ran while one was open for 1% of the time, Pallas kernels for 9%

profile of v2, /device:TPU:1, one launch (start us, length us, event | category | flops | bytes accessed | tf_op | source)
XLA Modules:
  0.0 154.6 jit_solution(14546724843546988265)
XLA Ops:
  0.0 0.6 pad_add_fusion.1.where
  0.6 5.2 %parcels.1 = s16[32,2,32,640]{3,2,1,0:T(8,128)(2,1)} custom-call(s32[2]{0:T(128)} %pad_add_fusion.1.where, s32[32,32]{1,0:T(8,128)} %selected.1, f32[576,512]{1,0:T(8,128)} %bitcast.25), custom_call_target="tpu_custom_call" | custom-call | flops 10000000 | bytes 4000000 | tf_op jit(solution)/shard_map/parcels/pallas_call | solution.py:118
  5.8 11.4 %all-to-all-start = ((s16[32,2,32,640]{3,2,1,0:T(8,128)(2,1)}), s16[32,2,32,640]{3,2,1,0:T(8,128)(2,1)}, u32[]{:S(2)}, u32[]{:S(2)}) async-start(s16[32,2,32,640]{3,2,1,0:T(8,128)(2,1)} %parcels.1), calls=%async_computation | async-start | bytes 5242880 | tf_op jit(solution)/shard_map/all_to_all | solution.py:419
  17.8 0.7 fusion
  18.6 0.7 and_select_fusion.1
  19.5 1.9 %collective-permute-start.1 = (bf16[4,512,128]{2,1,0:T(8,128)(2,1)S(1)}, bf16[4,512,128]{2,1,0:T(8,128)(2,1)}, u32[]{:S(2)}, u32[]{:S(2)}) collective-permute-start(bf16[4,512,128]{2,1,0:T(8,128)(2,1)S(1)} %constant_dynamic-slice_fusion), channel_id=1, source_target_pairs={{0,1},{1,0},{2,3},{3,2},{4,5},{5,4},{6,7},{7,6},{8,9},{9,8},{10,11... | collective-permute-start | bytes 1572872 | tf_op jit(solution)/shard_map/ppermute | solution.py:435
  21.4 3.4 %collective-permute-start = (s16[512,640]{1,0:T(8,128)(2,1)S(1)}, s16[512,640]{1,0:T(8,128)(2,1)S(1)}, u32[]{:S(2)}, u32[]{:S(2)}) collective-permute-start(s16[512,640]{1,0:T(8,128)(2,1)S(1)} %pack_queries.1.own), channel_id=1, source_target_pairs={{0,1},{1,0},{2,3},{3,2},{4,5},{5,4},{6,7},{7,6},{8,9},{9,8},{10,11... | collective-permute-start | bytes 1966088 | tf_op jit(solution)/shard_map/ppermute | solution.py:423
  24.8 9.8 %collective-permute-done.1.fetched = bf16[4,512,128]{2,1,0:T(8,128)(2,1)} collective-permute-done((bf16[4,512,128]{2,1,0:T(8,128)(2,1)S(1)}, bf16[4,512,128]{2,1,0:T(8,128)(2,1)}, u32[]{:S(2)}, u32[]{:S(2)}) %collective-permute-start.1) | collective-permute-done | bytes 524320 | tf_op jit(solution)/shard_map/ppermute | solution.py:435
  34.6 4.0 %collective-permute-start.2 = (bf16[4,512,128]{2,1,0:T(8,128)(2,1)}, bf16[4,512,128]{2,1,0:T(8,128)(2,1)}, u32[]{:S(2)}, u32[]{:S(2)}) collective-permute-start(bf16[4,512,128]{2,1,0:T(8,128)(2,1)} %collective-permute-done.1.fetched), channel_id=1, source_target_pairs={{0,16},{16,0},{1,17},{17,1},{2,18},{18,2},{3,19},{19,3},{4,20},{20... | collective-permute-start | bytes 1572872 | tf_op jit(solution)/shard_map/ppermute | solution.py:436
  38.7 10.0 %collective-permute-done.other = s16[512,640]{1,0:T(8,128)(2,1)S(1)} collective-permute-done((s16[512,640]{1,0:T(8,128)(2,1)S(1)}, s16[512,640]{1,0:T(8,128)(2,1)S(1)}, u32[]{:S(2)}, u32[]{:S(2)}) %collective-permute-start) | collective-permute-done | bytes 655392 | tf_op jit(solution)/shard_map/ppermute | solution.py:423
  48.6 0.9 copy-done
  49.5 2.2 %collective-permute-start.3 = (bf16[224,1024]{1,0:T(8,128)(2,1)}, bf16[224,1024]{1,0:T(8,128)(2,1)}, u32[]{:S(2)}, u32[]{:S(2)}) collective-permute-start(bf16[224,1024]{1,0:T(8,128)(2,1)} %bitcast.10.near_own), channel_id=1, source_target_pairs={{0,1},{1,0},{2,3},{3,2},{4,5},{5,4},{6,7},{7,6},{8,9},{9,8},{10,11... | collective-permute-start | bytes 1376264 | tf_op jit(solution)/shard_map/ppermute | solution.py:426
  51.8 1.1 copy-done.1
  52.8 0.8 split_queries.1.q
  53.7 1.2 copy-done.3
  54.9 12.9 %attend.1 = s16[64,2176]{1,0:T(8,128)(2,1)} custom-call(s32[32]{0:T(128)S(1)} %convert_add_fusion.places, s32[32]{0:T(128)S(1)} %get-tuple-element.26.block_ids, s32[3]{0:T(128)S(1)} %pad_add_fusion.2.own, bf16[1024,1280]{1,0:T(8,128)(2,1)S(1)} %split_queries.1.q, s16[64,32,640]{2,1,0:T(8,128)(2,1)} %bitcast.11.arrived, bf16[8,512,128]{2,1,0:T(8,128)(2,1)S(1)} %copy-done.3, ...), custom_call_target="tpu_custom_call" | custom-call | flops 7000000000 | bytes 8000000 | tf_op jit(solution)/shard_map/attend/pallas_call | solution.py:284
  67.8 3.5 %all-to-all-start.1 = ((s16[2,32,2176]{2,1,0:T(8,128)(2,1)}), s16[2,32,2176]{2,1,0:T(8,128)(2,1)S(1)}, u32[]{:S(2)}, u32[]{:S(2)}) async-start(s16[2,32,2176]{2,1,0:T(8,128)(2,1)} %bitcast.12), calls=%async_computation.1 | async-start | bytes 557056 | tf_op jit(solution)/shard_map/all_to_all | solution.py:444
  71.3 3.0 %collective-permute-start.4 = (bf16[224,1024]{1,0:T(8,128)(2,1)}, bf16[224,1024]{1,0:T(8,128)(2,1)S(1)}, u32[]{:S(2)}, u32[]{:S(2)}) collective-permute-start(bf16[224,1024]{1,0:T(8,128)(2,1)} %bitcast.10.near_own), channel_id=1, source_target_pairs={{0,16},{16,0},{1,17},{17,1},{2,18},{18,2},{3,19},{19,3},{4,20},{20... | collective-permute-start | bytes 1376264 | tf_op jit(solution)/shard_map/ppermute | solution.py:427
  74.4 2.1 %collective-permute-start.5 = (bf16[224,1024]{1,0:T(8,128)(2,1)}, bf16[224,1024]{1,0:T(8,128)(2,1)S(1)}, u32[]{:S(2)}, u32[]{:S(2)}) collective-permute-start(bf16[224,1024]{1,0:T(8,128)(2,1)} %collective-permute-done.3.near_other), channel_id=1, source_target_pairs={{0,16},{16,0},{1,17},{17,1},{2,18},{18,2},{3,19},{19,3},{4,20},{20... | collective-permute-start | bytes 1376264 | tf_op jit(solution)/shard_map/ppermute | solution.py:443
  76.5 0.5 merge.1
  77.0 23.3 %all-gather.2 = s16[512,2176]{1,0:T(8,128)(2,1)S(1)} all-gather(s16[32,2176]{1,0:T(8,128)(2,1)S(1)} %merge.1), channel_id=2, replica_groups=mesh['x'=4,'y'=4,'core'=2,'zq'=8,'zb'=2] {'x','y'}, dimensions={0}, use_global_device_ids=true | all-gather | bytes 2367488 | tf_op jit(solution)/shard_map/all_gather | solution.py:447
  100.4 2.8 %project.1 = s16[2,16,32,256]{3,2,1,0:T(8,128)(2,1)S(1)} custom-call(s32[2]{0:T(128)S(1)} %pad_add_fusion.place, s16[16,32,2176]{2,1,0:T(8,128)(2,1)S(1)} %bitcast.20, bf16[224,1024]{1,0:T(8,128)(2,1)} %bitcast.10.near_own, bf16[224,1024]{1,0:T(8,128)(2,1)} %collective-permute-done.3.near_other, bf16[224,1024]{1,0:T(8,128)(2,1)S(1)} %collective-permute-done.4.far_own, ...), custom_call_target="tpu_custom_call" | custom-call | flops 1000000000 | bytes 7000000 | tf_op jit(solution)/shard_map/project/pallas_call | solution.py:363
  103.2 49.4 %all_to_all.15 = s16[32,32,256]{2,1,0:T(8,128)(2,1)} all-to-all(s16[32,32,256]{2,1,0:T(8,128)(2,1)S(1)} %bitcast.22), channel_id=1, replica_groups=mesh['x'=4,'y'=4,'core'=2,'zq'=8,'zb'=2] {'core','zq','zb'}, dimensions={0} | all-to-all | bytes 1048576 | tf_op jit(solution)/shard_map/all_to_all | solution.py:449
  152.6 1.9 %add_parts.1 = bf16[224,128]{1,0:T(8,128)(2,1)} custom-call(s16[2,8,2,32,256]{4,3,2,1,0:T(8,128)(2,1)} %bitcast.23), custom_call_target="tpu_custom_call" | custom-call | tf_op jit(solution)/shard_map/add_parts/pallas_call | solution.py:392
  (20 shorter events, 1.1 us)
Async XLA Ops:
  5.7 11.4 %copy-start.4 = (f32[64,8,576]{2,1,0:T(8,128)S(1)}, f32[64,8,576]{2,1,0:T(8,128)}, u32[]{:S(2)}) copy-start(f32[64,8,576]{2,1,0:T(8,128)} %param.5) | copy-start | bytes 3538948
  5.8 47.9 %all-to-all-start = ((s16[32,2,32,640]{3,2,1,0:T(8,128)(2,1)}), s16[32,2,32,640]{3,2,1,0:T(8,128)(2,1)}, u32[]{:S(2)}, u32[]{:S(2)}) async-start(s16[32,2,32,640]{3,2,1,0:T(8,128)(2,1)} %parcels.1), calls=%async_computation | async-start | bytes 5242880 | tf_op jit(solution)/shard_map/all_to_all | solution.py:419
  17.2 2.3 %copy-start.2 = (bf16[8,512,128]{2,1,0:T(8,128)(2,1)S(1)}, bf16[8,512,128]{2,1,0:T(8,128)(2,1)}, u32[]{:S(2)}) copy-start(bf16[8,512,128]{2,1,0:T(8,128)(2,1)} %vp_own.1) | copy-start | bytes 3145732
  19.5 15.1 %collective-permute-start.1 = (bf16[4,512,128]{2,1,0:T(8,128)(2,1)S(1)}, bf16[4,512,128]{2,1,0:T(8,128)(2,1)}, u32[]{:S(2)}, u32[]{:S(2)}) collective-permute-start(bf16[4,512,128]{2,1,0:T(8,128)(2,1)S(1)} %constant_dynamic-slice_fusion), channel_id=1, source_target_pairs={{0,1},{1,0},{2,3},{3,2},{4,5},{5,4},{6,7},{7,6},{8,9},{9,8},{10,11... | collective-permute-start | bytes 1572872 | tf_op jit(solution)/shard_map/ppermute | solution.py:435
  21.4 27.2 %collective-permute-start = (s16[512,640]{1,0:T(8,128)(2,1)S(1)}, s16[512,640]{1,0:T(8,128)(2,1)S(1)}, u32[]{:S(2)}, u32[]{:S(2)}) collective-permute-start(s16[512,640]{1,0:T(8,128)(2,1)S(1)} %pack_queries.1.own), channel_id=1, source_target_pairs={{0,1},{1,0},{2,3},{3,2},{4,5},{5,4},{6,7},{7,6},{8,9},{9,8},{10,11... | collective-permute-start | bytes 1966088 | tf_op jit(solution)/shard_map/ppermute | solution.py:423
  34.6 19.0 %collective-permute-start.2 = (bf16[4,512,128]{2,1,0:T(8,128)(2,1)}, bf16[4,512,128]{2,1,0:T(8,128)(2,1)}, u32[]{:S(2)}, u32[]{:S(2)}) collective-permute-start(bf16[4,512,128]{2,1,0:T(8,128)(2,1)} %collective-permute-done.1.fetched), channel_id=1, source_target_pairs={{0,16},{16,0},{1,17},{17,1},{2,18},{18,2},{3,19},{19,3},{4,20},{20... | collective-permute-start | bytes 1572872 | tf_op jit(solution)/shard_map/ppermute | solution.py:436
  48.6 0.9 copy-start
  49.5 18.3 %collective-permute-start.3 = (bf16[224,1024]{1,0:T(8,128)(2,1)}, bf16[224,1024]{1,0:T(8,128)(2,1)}, u32[]{:S(2)}, u32[]{:S(2)}) collective-permute-start(bf16[224,1024]{1,0:T(8,128)(2,1)} %bitcast.10.near_own), channel_id=1, source_target_pairs={{0,1},{1,0},{2,3},{3,2},{4,5},{5,4},{6,7},{7,6},{8,9},{9,8},{10,11... | collective-permute-start | bytes 1376264 | tf_op jit(solution)/shard_map/ppermute | solution.py:426
  51.8 1.1 copy-start.1
  53.6 1.2 copy-start.3
  67.8 8.7 %all-to-all-start.1 = ((s16[2,32,2176]{2,1,0:T(8,128)(2,1)}), s16[2,32,2176]{2,1,0:T(8,128)(2,1)S(1)}, u32[]{:S(2)}, u32[]{:S(2)}) async-start(s16[2,32,2176]{2,1,0:T(8,128)(2,1)} %bitcast.12), calls=%async_computation.1 | async-start | bytes 557056 | tf_op jit(solution)/shard_map/all_to_all | solution.py:444
  71.3 29.0 %collective-permute-start.4 = (bf16[224,1024]{1,0:T(8,128)(2,1)}, bf16[224,1024]{1,0:T(8,128)(2,1)S(1)}, u32[]{:S(2)}, u32[]{:S(2)}) collective-permute-start(bf16[224,1024]{1,0:T(8,128)(2,1)} %bitcast.10.near_own), channel_id=1, source_target_pairs={{0,16},{16,0},{1,17},{17,1},{2,18},{18,2},{3,19},{19,3},{4,20},{20... | collective-permute-start | bytes 1376264 | tf_op jit(solution)/shard_map/ppermute | solution.py:427
  74.4 26.0 %collective-permute-start.5 = (bf16[224,1024]{1,0:T(8,128)(2,1)}, bf16[224,1024]{1,0:T(8,128)(2,1)S(1)}, u32[]{:S(2)}, u32[]{:S(2)}) collective-permute-start(bf16[224,1024]{1,0:T(8,128)(2,1)} %collective-permute-done.3.near_other), channel_id=1, source_target_pairs={{0,16},{16,0},{1,17},{17,1},{2,18},{18,2},{3,19},{19,3},{4,20},{20... | collective-permute-start | bytes 1376264 | tf_op jit(solution)/shard_map/ppermute | solution.py:443

commit v3 on v2

v3 whole, which is shorter than its diff:
```python
import functools
import math

import jax
import jax.numpy as jnp
from jax import lax
from jax.experimental import pallas as pl
from jax.experimental.pallas import tpu as pltpu
from jax.sharding import Mesh
from jax.sharding import PartitionSpec as P

NEG = -1e30
SCALE = 1.0 / 192.0**0.5
LOG2E = math.log2(math.e)
F32, BF16, S16 = jnp.float32, jnp.bfloat16, jnp.int16
LANES = 128
PAIR = 2
LIMIT = 24 * 1024 * 1024
WHOLE = 60 * 1024 * 1024
SMEM = pl.BlockSpec(memory_space=pltpu.SMEM)
VMEM = pl.BlockSpec(memory_space=pltpu.VMEM)
ANY = pl.BlockSpec(memory_space=pl.ANY)
HBM = pl.BlockSpec(memory_space=pltpu.HBM)
PARAMS = pltpu.CompilerParams(vmem_limit_bytes=LIMIT)


def row_code(peak):
    return jnp.ceil(jnp.log2(jnp.maximum(peak, 1e-30)) * 256.0)


def to_int(x, code):
    y = jnp.round(x * (jnp.exp2(code * (-1.0 / 256.0)) * 32767.0))
    return jnp.clip(y, -32767.0, 32767.0)


def scale_of(code):
    return jnp.exp2(code * (1.0 / 256.0)) * (1.0 / 32767.0)


def as_s16(x):
    return x.astype(jnp.int32).astype(S16)


def as_f32(x):
    return x.astype(jnp.int32).astype(F32)


def row_peak(x):
    return jnp.max(jnp.abs(x), axis=-1, keepdims=True)


def lane_ids(shape):
    return lax.broadcasted_iota(jnp.int32, shape, len(shape) - 1)


def dot_nt(a, b):
    return lax.dot_general(a, b, (((1,), (1,)), ((), ())), preferred_element_type=F32)


def dot_nn(a, b):
    return jnp.dot(a, b, preferred_element_type=F32)


def halves(x):
    high = x.astype(BF16)
    return high, (x - high.astype(F32)).astype(BF16)


def cost(flops, nbytes, exps=0):
    return pl.CostEstimate(flops=flops, bytes_accessed=nbytes, transcendentals=exps)


def parcel_kernel(where, selected, latent_t, out, lists, stage, wide, coded, ids_v, ids, in_sems, id_sems, sems):
    width, total = latent_t.shape
    blocks, part, padded = coded.shape
    block = total // blocks
    groups = total // LANES
    fetch = pltpu.make_async_copy(selected, lists, id_sems.at[0])
    fetch.start()
    loads = []
    for n in range(groups):
        columns = pl.ds(n * LANES, LANES)
        load = pltpu.make_async_copy(latent_t.at[:, columns], stage.at[:, columns], in_sems.at[n])
        load.start()
        loads.append(load)
    fetch.wait()
    offset = lists[...] - where[0]
    mine = (offset >= 0) & (offset < blocks)
    first = jnp.min(jnp.where(mine, offset, blocks), axis=1, keepdims=True)
    last = jnp.max(jnp.where(mine, offset, -1), axis=1, keepdims=True)
    ids_v[...] = jnp.where(lane_ids(ids_v.shape) == 0, first, last)
    move = pltpu.make_async_copy(ids_v, ids, id_sems.at[1])
    move.start()
    lanes = lane_ids((part, padded))
    for n in range(groups):
        loads[n].wait()
        wide[:, :width] = stage[:, n * LANES : (n + 1) * LANES].T
        for m in range(LANES // block):
            at = pl.multiple_of(m * block + where[1], part)
            x = jnp.where(lanes < width, wide[pl.ds(at, part), :], 0.0)
            code = row_code(row_peak(x))
            full = jnp.where(lanes < width, to_int(x, code), code)
            coded[n * (LANES // block) + m] = as_s16(full)
    move.wait()
    copies = []
    for d in range(out.shape[0]):
        low, high = ids[d, 0], ids[d, 1]
        for s, (block_id, filled) in enumerate(((low, low <= high), (high, low < high))):
            copy = pltpu.make_async_copy(coded.at[jnp.clip(block_id, 0, blocks - 1)], out.at[d, s], sems.at[2 * d + s])
            pl.when(filled)(copy.start)
            copies.append((filled, copy))
    for filled, copy in copies:
        pl.when(filled)(copy.wait)


def make_parcels(where, selected, latent_t, blocks, part, padded):
    receivers = selected.shape[0]
    width, total = latent_t.shape
    return pl.pallas_call(
        parcel_kernel,
        out_shape=jax.ShapeDtypeStruct((receivers, 2, part, padded), S16),
        in_specs=[SMEM, HBM, HBM],
        out_specs=HBM,
        scratch_shapes=[
            pltpu.VMEM(selected.shape, jnp.int32),
            pltpu.VMEM((width, total), F32),
            pltpu.VMEM((LANES, padded), F32),
            pltpu.VMEM((blocks, part, padded), S16),
            pltpu.VMEM((receivers, LANES), jnp.int32),
            pltpu.SMEM((receivers, LANES), jnp.int32),
            pltpu.SemaphoreType.DMA((total // LANES,)),
            pltpu.SemaphoreType.DMA((2,)),
            pltpu.SemaphoreType.DMA((2 * receivers,)),
        ],
        compiler_params=pltpu.CompilerParams(vmem_limit_bytes=WHOLE),
        cost_estimate=cost(10**7, 4 * 10**6),
        name="parcels",
    )(where, selected, latent_t)


def pack_kernel(q, out, wide):
    width = q.shape[-1]
    wide[:, :width] = q[...]
    lanes = lane_ids(wide.shape)
    x = jnp.where(lanes < width, wide[...], 0.0)
    code = row_code(row_peak(x))
    out[...] = as_s16(jnp.where(lanes < width, to_int(x, code), code))


def pack_queries(q, padded):
    rows = q.shape[0]
    return pl.pallas_call(
        pack_kernel,
        out_shape=jax.ShapeDtypeStruct((rows, padded), S16),
        in_specs=[VMEM],
        out_specs=VMEM,
        scratch_shapes=[pltpu.VMEM((rows, padded), F32)],
        compiler_params=PARAMS,
        cost_estimate=cost(10**7, 2 * 10**6),
        name="pack_queries",
    )(q)


def load_queries(place, half, own, other, q_s, heads):
    rows, padded = own.shape
    block = rows // heads
    part = block // PAIR
    some = heads // 2
    lat = padded - LANES
    core, member = place[0], place[1]
    begin = (member if half == 1 else 1 - member) * part
    rope = lane_ids((part, LANES)) < LANES // 2
    for n in range(PAIR * heads):
        head = n
        if n >= heads:
            head = ((n - heads) // some + core) % 2 * some + n % some
        at = pl.multiple_of(head * block + begin, part)
        wide = as_f32((own if n < heads else other)[pl.ds(at, part), :])
        wide = wide * (scale_of(wide[:, lat:])[:, LANES - 1 :] * (SCALE * LOG2E))
        span = slice(n * part, (n + 1) * part)
        high, low = halves(wide[:, :lat])
        q_s[span, :lat] = high
        q_s[span, lat : 2 * lat] = low
        high, low = halves(jnp.where(rope, wide[:, lat:], 0.0))
        both = high.astype(F32) + pltpu.roll(low.astype(F32), LANES // 2, 1)
        q_s[span, 2 * lat : 2 * lat + LANES] = both.astype(BF16)
        q_s[span, 2 * lat + LANES :] = high


def fetch_keys(places, arrived, slots, sems):
    copies = []
    for i in range(places.shape[0]):
        copy = pltpu.make_async_copy(arrived.at[places[i]], slots.at[i], sems.at[i])
        copy.start()
        copies.append(copy)
    return copies


def split_keys(copies, slots, keys_s):
    count, part, padded = slots.shape
    lat = padded - LANES
    step = 8
    rope = lane_ids((step * part, LANES)) < LANES // 2
    for c in range(count // step):
        for i in range(c * step, (c + 1) * step):
            copies[i].wait()
        wide = as_f32(slots[c * step : (c + 1) * step].reshape(step * part, padded))
        wide = wide * scale_of(wide[:, lat:])[:, LANES - 1 :]
        span = slice(c * step * part, (c + 1) * step * part)
        high, low = halves(wide[:, :lat])
        keys_s[span, :lat] = high
        keys_s[span, lat : 2 * lat] = low
        tail = jnp.where(rope, wide[:, lat:], 0.0)
        keys_s[span, 2 * lat : 2 * lat + LANES] = (tail + pltpu.roll(tail, LANES // 2, 1)).astype(BF16)
        keys_s[span, 2 * lat + LANES :] = halves(tail)[1]


def attend_rows(block_ids, place, half, q, keys_s, vp_own, fetched, passed, out):
    heads, lat, vdim = vp_own.shape
    count = block_ids.shape[0]
    part = out.shape[0]
    some = fetched.shape[0]
    keys = keys_s.shape[0]
    lane = lane_ids((1, keys))
    room = jnp.zeros((1, keys), jnp.int32)
    for i in range(count):
        room = jnp.where(lane // part == i, (place[2] - block_ids[i]) * (PAIR * part), room)
    if half == 0:
        room = room + (1 - 2 * place[1]) * part
    room = room - lane % part
    spot = lax.broadcasted_iota(jnp.int32, (q.shape[0], 1), 0) % part
    s = (
        dot_nt(q[:, :lat], keys_s[:, :lat])
        + dot_nt(q[:, lat : 2 * lat], keys_s[:, :lat])
        + dot_nt(q[:, :lat], keys_s[:, lat : 2 * lat])
        + dot_nt(q[:, 2 * lat :], keys_s[:, 2 * lat :])
    )
    s = jnp.where(room + spot >= 0, s, NEG)
    peak = jnp.max(s, axis=-1, keepdims=True)
    p = jnp.exp2(s - peak)
    norm = jnp.sum(p, axis=-1, keepdims=True)
    high, low = halves(p)
    mixed = dot_nn(high, keys_s[:, :lat]) + dot_nn(high, keys_s[:, lat : 2 * lat]) + dot_nn(low, keys_s[:, :lat])
    high, low = halves(mixed / norm)
    stat = (peak + jnp.log2(norm)) * 2.0
    coarse = jnp.floor(stat)
    fine = (stat - coarse) * 32767.0
    results = []
    for n in range(PAIR * heads):
        rows = slice(n * part, (n + 1) * part)
        maps = vp_own[n] if n < heads else (fetched[n - heads] if n < heads + some else passed[n - heads - some])
        both = dot_nn(jnp.concatenate([high[rows], low[rows]], axis=0), maps)
        results.append(both[:part] + both[part:])
    head_out = jnp.concatenate(results, axis=-1)
    code = row_code(row_peak(head_out))
    inner = head_out.shape[-1]
    coded = as_s16(to_int(head_out, code))
    half = inner // PAIR
    width = some * vdim
    out[:, :half] = coded[:, :half]
    for n, turn in enumerate((place[0], 1 - place[0])):
        at = pl.multiple_of(half + turn * width, width)
        out[:, pl.ds(at, width)] = coded[:, half + n * width : half + (n + 1) * width]
    lane = lane_ids((part, LANES))
    tail = code
    for n in range(PAIR * heads):
        rows = slice(n * part, (n + 1) * part)
        at = n
        if n >= heads:
            turn = place[0] if n < heads + some else 1 - place[0]
            at = heads + turn * some + n % some
        tail = jnp.where(lane == at, coarse[rows], tail)
        tail = jnp.where(lane == at + PAIR * heads, fine[rows], tail)
    out[:, inner:] = as_s16(tail)


def far_kernel(
    places, block_ids, place, own, other, arrived, vp_own, fetched, passed, out, keys_s, slots, q_s, sems
):
    copies = fetch_keys(places, arrived, slots, sems)
    load_queries(place, 0, own, other, q_s, vp_own.shape[0])
    split_keys(copies, slots, keys_s)
    attend_rows(block_ids, place, 0, q_s, keys_s, vp_own, fetched, passed, out)


def near_kernel(block_ids, place, own, other, keys_s, vp_own, fetched, passed, out, q_s):
    load_queries(place, 1, own, other, q_s, vp_own.shape[0])
    attend_rows(block_ids, place, 1, q_s, keys_s, vp_own, fetched, passed, out)


def attend_far(places, block_ids, place, own, other, arrived, vp_own, fetched, passed):
    count = places.shape[0]
    _, part, padded = arrived.shape
    heads, _, vdim = vp_own.shape
    return pl.pallas_call(
        far_kernel,
        out_shape=(
            jax.ShapeDtypeStruct((part, PAIR * heads * vdim + LANES), S16),
            jax.ShapeDtypeStruct((count * part, 2 * padded), BF16),
        ),
        in_specs=[SMEM, SMEM, SMEM, VMEM, VMEM, HBM, VMEM, VMEM, VMEM],
        out_specs=(VMEM, VMEM),
        scratch_shapes=[
            pltpu.VMEM((count, part, padded), S16),
            pltpu.VMEM((own.shape[0], 2 * padded), BF16),
            pltpu.SemaphoreType.DMA((count,)),
        ],
        compiler_params=PARAMS,
        cost_estimate=cost(4 * 10**9, 6 * 10**6, 10**6),
        name="attend_far",
    )(places, block_ids, place, own, other, arrived, vp_own, fetched, passed)


def attend_near(block_ids, place, own, other, keys, vp_own, fetched, passed, part):
    heads, _, vdim = vp_own.shape
    return pl.pallas_call(
        near_kernel,
        out_shape=jax.ShapeDtypeStruct((part, PAIR * heads * vdim + LANES), S16),
        in_specs=[SMEM, SMEM, VMEM, VMEM, VMEM, VMEM, VMEM, VMEM],
        out_specs=VMEM,
        scratch_shapes=[pltpu.VMEM((own.shape[0], 2 * own.shape[1]), BF16)],
        compiler_params=PARAMS,
        cost_estimate=cost(4 * 10**9, 6 * 10**6, 10**6),
        name="attend_near",
    )(block_ids, place, own, other, keys, vp_own, fetched, passed)


def merge_kernel(place, here, there, out, *, heads):
    rows, padded = here.shape
    inner = padded - LANES
    width = inner // PAIR
    vdim = width // heads
    tails = [as_f32(x[:, inner:]) for x in (here, there)]
    logs = [(x + pltpu.roll(x, LANES - PAIR * heads, 1) * (1.0 / 32767.0)) * 0.5 for x in tails]
    scales = [scale_of(x)[:, LANES - 1 :] for x in tails]
    merged = []
    for g in range(PAIR):
        a = logs[0] if g == 0 else pltpu.roll(logs[0], LANES - heads, 1)
        b = logs[1] if g == 1 else pltpu.roll(logs[1], LANES - heads, 1)
        top = jnp.maximum(a, b)
        a, b = jnp.exp2(a - top), jnp.exp2(b - top)
        total = a + b
        a, b = a / total * scales[0], b / total * scales[1]
        for h in range(heads):
            x = as_f32(here[:, g * width + h * vdim : g * width + (h + 1) * vdim]) * a[:, h : h + 1]
            y = as_f32(there[:, (1 - g) * width + h * vdim : (1 - g) * width + (h + 1) * vdim]) * b[:, h : h + 1]
            merged.append((x + y).astype(BF16).astype(F32))
    head_out = jnp.concatenate(merged, axis=-1)
    code = row_code(row_peak(head_out))
    coded = as_s16(to_int(head_out, code))
    for g, turn in enumerate((place[1], 1 - place[1])):
        out[:, pl.ds(pl.multiple_of(turn * width, width), width)] = coded[:, g * width : (g + 1) * width]
    out[:, inner:] = as_s16(jnp.broadcast_to(code, (rows, LANES)))


def merge(place, here, there, heads):
    return pl.pallas_call(
        functools.partial(merge_kernel, heads=heads),
        out_shape=jax.ShapeDtypeStruct(here.shape, S16),
        in_specs=[SMEM, VMEM, VMEM],
        out_specs=VMEM,
        compiler_params=PARAMS,
        cost_estimate=cost(10**6, 5 * 10**5),
        name="merge",
    )(place, here, there)


def project_kernel(place, rows_in, near_own, near_other, far_own, far_other, out, wide):
    chips, rows, padded = rows_in.shape
    inner = padded - LANES
    columns, depth = near_own.shape
    core = place[0]
    factor = scale_of(as_f32(rows_in[:, :, inner:]).reshape(chips * rows, LANES))[:, :1]
    sums = [None, None]
    for n, member in enumerate((place[1], 1 - place[1])):
        at = pl.multiple_of(member * depth, depth)
        a = as_f32(rows_in[:, :, pl.ds(at, depth)]).reshape(chips * rows, depth)
        a = (a * factor).astype(BF16)
        for k, weights in enumerate(((near_own, far_own), (near_other, far_other))[n]):
            term = dot_nt(a, weights[...])
            sums[k] = term if n == 0 else sums[k] + term
    spare = 2 * LANES - columns
    keep = LANES - spare
    groups = rows // 8
    for k, at in enumerate((core, 1 - core)):
        wide[:, :columns] = sums[k]
        out[at, :, :rows, :] = wide[:, :LANES].reshape(chips, rows, LANES).astype(BF16)
        rest = wide[:, LANES:].reshape(chips, groups, 8, LANES)
        last = rest[:, groups - 1].reshape(chips * 8, LANES)
        lanes = lane_ids(last.shape)
        packed = []
        for g in range(groups - 1):
            moved = pltpu.roll(last, (keep - spare * g) % LANES, 1)
            packed.append(jnp.where(lanes < keep, rest[:, g].reshape(chips * 8, LANES), moved))
        packed = jnp.concatenate([x.reshape(chips, 8, LANES) for x in packed], axis=1)
        out[at, :, rows:, :] = packed.astype(BF16)


def project(place, rows_in, near_own, near_other, far_own, far_other):
    chips, rows, _ = rows_in.shape
    return pl.pallas_call(
        project_kernel,
        out_shape=jax.ShapeDtypeStruct((2, chips, rows * near_own.shape[0] // LANES, LANES), BF16),
        in_specs=[SMEM] + [VMEM] * 5,
        out_specs=VMEM,
        scratch_shapes=[pltpu.VMEM((chips * rows, 2 * LANES), F32)],
        compiler_params=PARAMS,
        cost_estimate=cost(10**9, 7 * 10**6),
        name="project",
    )(place, rows_in, near_own, near_other, far_own, far_other)


def add_kernel(parts, out):
    cores, outer, groups, packed, _ = parts.shape
    columns, total = out.shape
    rows = total // (cores * groups)
    spare = 2 * LANES - columns
    keep = LANES - spare
    lanes = lane_ids((8, LANES))
    left, right = [], []
    for k in range(cores):
        for g in range(groups):
            full = parts[k, 0, g].astype(F32)
            for z in range(1, outer):
                full = full + parts[k, z, g].astype(F32)
            left.append(full[:rows])
            pieces = [full[rows + 8 * n : rows + 8 * (n + 1)] for n in range(rows // 8 - 1)]
            last = jnp.zeros((8, LANES), F32)
            for n, piece in enumerate(pieces):
                moved = pltpu.roll(piece, (spare * n - keep) % LANES, 1)
                last = jnp.where((lanes >= spare * n) & (lanes < spare * (n + 1)), moved, last)
            right.extend(pieces + [last])
    out[:LANES, :] = jnp.concatenate(left, axis=0).T.astype(BF16)
    out[LANES:, :] = jnp.concatenate(right, axis=0).T[: columns - LANES].astype(BF16)


def add_parts(parts, columns):
    cores, _, groups, packed, _ = parts.shape
    rows = packed * LANES // columns
    return pl.pallas_call(
        add_kernel,
        out_shape=jax.ShapeDtypeStruct((columns, cores * groups * rows), BF16),
        in_specs=[VMEM],
        out_specs=VMEM,
        name="add_parts",
    )(parts)


def on_device(queries, latent, selected, value_proj, out_proj):
    plane = ("x", "y", "core")
    ctx_count = lax.axis_size(plane)
    ctx_index = lax.axis_index(plane)
    core = lax.axis_index("core").astype(jnp.int32)
    member = lax.axis_index("zb").astype(jnp.int32)
    block, heads, width = queries.shape
    per_owner = latent.shape[0] // block
    key_blocks = per_owner * ctx_count
    padded = -(-width // LANES) * LANES
    columns = out_proj.shape[1]
    part = block // PAIR
    swap = [(0, 1), (1, 0)]
    start = member * part

    where = jnp.stack([(ctx_index * per_owner).astype(jnp.int32), start])
    parcels = make_parcels(where, selected, latent.T, per_owner, part, padded)
    parcels, queries, value_near = lax.optimization_barrier((parcels, queries, value_proj))
    arrived = lax.all_to_all(parcels, plane, split_axis=0, concat_axis=0, tiled=True)

    q = jnp.transpose(queries, (1, 0, 2)).reshape(heads * block, width)
    near_own = out_proj.T
    q_own = pack_queries(q, padded)
    q_other = lax.ppermute(q_own, "zb", swap)
    near_own = lax.optimization_barrier((q_own, near_own))[1]
    far_own = lax.ppermute(near_own, "core", swap)
    place = jnp.stack([core, member, key_blocks - ctx_count + ctx_index]).astype(jnp.int32)

    listed = lax.optimization_barrier((q_own, selected))[1]
    own_list = lax.dynamic_slice_in_dim(listed, ctx_index, 1, 0)[0]
    owner = own_list // per_owner
    second = jnp.any((owner[None, :] == owner[:, None]) & (own_list[None, :] < own_list[:, None]), axis=1)
    places = owner * 2 + second.astype(jnp.int32)
    places, value_near = lax.optimization_barrier((places, value_near))
    fetched = lax.ppermute(lax.dynamic_slice_in_dim(value_near, core * (heads // 2), heads // 2, 0), "zb", swap)
    passed = lax.ppermute(fetched, "core", swap)

    slab = lax.optimization_barrier((fetched, near_own))[1]
    near_other = lax.ppermute(slab, "zb", swap)
    arrived = arrived.reshape(2 * ctx_count, part, padded)
    arrived, q_own, q_other = lax.optimization_barrier((arrived, q_own, q_other))
    for_partner, keys = attend_far(places, own_list, place, q_own, q_other, arrived, value_proj, fetched, passed)
    there = lax.ppermute(for_partner, "zb", swap)
    here = attend_near(own_list, place, q_own, q_other, keys, value_proj, fetched, passed, part)
    here, near_other = lax.optimization_barrier((here, near_other))
    far_other = lax.ppermute(near_other, "core", swap)
    gathered = lax.all_gather(merge(place, here, there, heads), ("x", "y"), axis=0, tiled=False)
    partial = project(place, gathered, near_own, near_other, far_own, far_other)
    partial = partial.reshape(-1, *partial.shape[2:])
    sent = lax.all_to_all(partial, ("core", "zq", "zb"), split_axis=0, concat_axis=0, tiled=True)
    return add_parts(sent.reshape(2, -1, PAIR, *sent.shape[1:]), columns).T


def solution(mesh):
    shape = (4, 4, 2, mesh.shape["head"] // PAIR, PAIR)
    fine = Mesh(mesh.devices.reshape(shape), ("x", "y", "core", "zq", "zb"))
    ctx, head = ("x", "y", "core"), ("zq", "zb")
    in_specs = (
        P(ctx, head, None),
        P(ctx, None),
        P(),
        P(head, None, None),
        P(head, ctx),
    )
    return jax.shard_map(on_device, mesh=fine, in_specs=in_specs, out_specs=P(head, ctx), check_vma=False)
```

time: 156 us -> 150 us (0.962)
  waiting for transfers between devices: 19.8 us -> 16.2 us
  blocking collectives: 72.8 us -> 70.7 us
  starting transfers between devices: 31.5 us -> 29.9 us
    ppermute x1, waiting for transfers between devices: 9.95 us -> 6.25 us  [on_device(): q_other = lax.ppermute(q_own, 'zb', swap)]
    all_to_all x1 -> x0, starting transfers between devices: 3.46 us -> none  [on_device(): lax.all_to_all(halves_out.reshape(PAIR, part, halves_out.shape[1]), 'zb',...]
    all_to_all x1, blocking collectives: 49.4 us -> 47.3 us  [on_device(): lax.all_to_all(partial, ('core', 'zq', 'zb'), split_axis=0, concat_axis=0...]
    unnamed x10 -> x4, local copies, waits for them, and re-layouts: 3.19 us -> 1.23 us
    ppermute x1, starting transfers between devices: 2.1 us -> 3.95 us  [on_device(): far_other = lax.ppermute(near_other, 'core', swap)]
    pallas_call x2, Pallas kernels: 13.7 us -> 15.5 us  [the longest x1 9.39 us: attend_far(): pl.pallas_call(far_kernel, out_shape=(jax.ShapeDtypeStruct((part, PAIR *...]
    ppermute x1 -> x2, starting transfers between devices: 2.23 us -> 3.87 us  [the longest x1 1.96 us: on_device(): there = lax.ppermute(for_partner, 'zb', swap)]
  transfers between devices with their start and end apart: 8 -> 8, of which waited for: 2 -> 3; matrix products, arithmetic and copies ran while one was open for 1% -> 3% of each run, Pallas kernels for 9% -> 11%
where the time goes in v3:
time: 150 us; the launch traced here: 149 us
  blocking collectives  70.7 us (47%)
  starting transfers between devices  29.9 us (20%)
  Pallas kernels  25.8 us (17%)
  waiting for transfers between devices  16.2 us (11%)
  local copies, waits for them, and re-layouts  3.89 us (3%)
  other arithmetic  2.26 us (2%)
    all_to_all x1, blocking collectives, on_device(): lax.all_to_all(partial, ('core', 'zq', 'zb'), split_axis=0, concat_axis=0...  47.3 us
    all_gather x1, blocking collectives, on_device(): lax.all_gather(merge(place, here, there, heads), ('x', 'y'), axis=0, tile...  23.4 us
    all_to_all x1, starting transfers between devices, on_device(): lax.all_to_all(parcels, plane, split_axis=0, concat_axis=0, tiled=True)  11 us
    ppermute x1, waiting for transfers between devices, on_device(): lax.ppermute(lax.dynamic_slice_in_dim(value_near, core * (heads // 2), he...  9.86 us
    pallas_call x1, Pallas kernels, attend_far(): pl.pallas_call(far_kernel, out_shape=(jax.ShapeDtypeStruct((part, PAIR *...  9.39 us
    ppermute x1, waiting for transfers between devices, on_device(): q_other = lax.ppermute(q_own, 'zb', swap)  6.25 us
    pallas_call x1, Pallas kernels, attend_near(): pl.pallas_call(near_kernel, out_shape=jax.ShapeDtypeStruct((part, PAIR *...  6.09 us
    pallas_call x1, Pallas kernels, make_parcels(): pl.pallas_call(parcel_kernel, out_shape=jax.ShapeDtypeStruct((receivers,...  4.46 us
  transfers between devices with their start and end apart: 8, of which 3 were waited for; matrix products, arithmetic and copies ran while one was open for 3% of the time, Pallas kernels for 11%

profile of v3, /device:TPU:1, one launch (start us, length us, event | category | flops | bytes accessed | tf_op | source)
XLA Modules:
  0.0 149.0 jit_solution(6446964834544985558)
XLA Ops:
  0.0 0.6 pad_add_fusion.1.where
  0.6 4.5 %parcels.1 = s16[32,2,32,640]{3,2,1,0:T(8,128)(2,1)} custom-call(s32[2]{0:T(128)} %pad_add_fusion.1.where, s32[32,32]{1,0:T(8,128)} %selected.1, f32[576,512]{1,0:T(8,128)} %bitcast.28), custom_call_target="tpu_custom_call" | custom-call | flops 10000000 | bytes 4000000 | tf_op jit(solution)/shard_map/parcels/pallas_call | solution.py:119
  5.1 11.0 %all-to-all-start = ((s16[32,2,32,640]{3,2,1,0:T(8,128)(2,1)}), s16[32,2,32,640]{3,2,1,0:T(8,128)(2,1)S(1)}, u32[]{:S(2)}, u32[]{:S(2)}) async-start(s16[32,2,32,640]{3,2,1,0:T(8,128)(2,1)} %parcels.1), calls=%async_computation | async-start | bytes 5242880 | tf_op jit(solution)/shard_map/all_to_all | solution.py:467
  16.1 1.6 %copy.7 = f32[8,64,576]{2,1,0:T(8,128)S(1)} copy(f32[8,64,576]{2,0,1:T(8,128)} %bitcast.27) | data formatting | bytes 2359296 | tf_op jit(solution)/shard_map/transpose | solution.py:469
  18.0 0.7 fusion
  18.7 0.7 and_select_fusion.1
  19.6 1.1 constant_dynamic-slice_fusion
  20.7 1.9 %collective-permute-start.1 = (bf16[4,512,128]{2,1,0:T(8,128)(2,1)S(1)}, bf16[4,512,128]{2,1,0:T(8,128)(2,1)}, u32[]{:S(2)}, u32[]{:S(2)}) collective-permute-start(bf16[4,512,128]{2,1,0:T(8,128)(2,1)S(1)} %constant_dynamic-slice_fusion), channel_id=1, source_target_pairs={{0,1},{1,0},{2,3},{3,2},{4,5},{5,4},{6,7},{7,6},{8,9},{9,8},{10,11... | collective-permute-start | bytes 1572872 | tf_op jit(solution)/shard_map/ppermute | solution.py:483
  22.6 3.4 %collective-permute-start = (s16[512,640]{1,0:T(8,128)(2,1)S(1)}, s16[512,640]{1,0:T(8,128)(2,1)}, u32[]{:S(2)}, u32[]{:S(2)}) collective-permute-start(s16[512,640]{1,0:T(8,128)(2,1)S(1)} %pack_queries.1.own), channel_id=1, source_target_pairs={{0,1},{1,0},{2,3},{3,2},{4,5},{5,4},{6,7},{7,6},{8,9},{9,8},{10,11... | collective-permute-start | bytes 1966088 | tf_op jit(solution)/shard_map/ppermute | solution.py:472
  26.0 9.9 %collective-permute-done.1.fetched = bf16[4,512,128]{2,1,0:T(8,128)(2,1)} collective-permute-done((bf16[4,512,128]{2,1,0:T(8,128)(2,1)S(1)}, bf16[4,512,128]{2,1,0:T(8,128)(2,1)}, u32[]{:S(2)}, u32[]{:S(2)}) %collective-permute-start.1) | collective-permute-done | bytes 524320 | tf_op jit(solution)/shard_map/ppermute | solution.py:483
  35.9 3.9 %collective-permute-start.2 = (bf16[4,512,128]{2,1,0:T(8,128)(2,1)}, bf16[4,512,128]{2,1,0:T(8,128)(2,1)}, u32[]{:S(2)}, u32[]{:S(2)}) collective-permute-start(bf16[4,512,128]{2,1,0:T(8,128)(2,1)} %collective-permute-done.1.fetched), channel_id=1, source_target_pairs={{0,16},{16,0},{1,17},{17,1},{2,18},{18,2},{3,19},{19,3},{4,20},{20... | collective-permute-start | bytes 1572872 | tf_op jit(solution)/shard_map/ppermute | solution.py:484
  39.7 1.9 %collective-permute-start.5 = (bf16[224,1024]{1,0:T(8,128)(2,1)}, bf16[224,1024]{1,0:T(8,128)(2,1)}, u32[]{:S(2)}, u32[]{:S(2)}) collective-permute-start(bf16[224,1024]{1,0:T(8,128)(2,1)} %bitcast.23), channel_id=1, source_target_pairs={{0,16},{16,0},{1,17},{17,1},{2,18},{18,2},{3,19},{19,3},{4,20},{20... | collective-permute-start | bytes 1376264 | tf_op jit(solution)/shard_map/ppermute | solution.py:474
  41.8 1.9 %collective-permute-start.3 = (bf16[224,1024]{1,0:T(8,128)(2,1)}, bf16[224,1024]{1,0:T(8,128)(2,1)}, u32[]{:S(2)}, u32[]{:S(2)}) collective-permute-start(bf16[224,1024]{1,0:T(8,128)(2,1)} %bitcast.24), channel_id=1, source_target_pairs={{0,1},{1,0},{2,3},{3,2},{4,5},{5,4},{6,7},{7,6},{8,9},{9,8},{10,11... | collective-permute-start | bytes 1376264 | tf_op jit(solution)/shard_map/ppermute | solution.py:487
  43.7 6.2 %collective-permute-done.other = s16[512,640]{1,0:T(8,128)(2,1)} collective-permute-done((s16[512,640]{1,0:T(8,128)(2,1)S(1)}, s16[512,640]{1,0:T(8,128)(2,1)}, u32[]{:S(2)}, u32[]{:S(2)}) %collective-permute-start) | collective-permute-done | bytes 655392 | tf_op jit(solution)/shard_map/ppermute | solution.py:472
  50.0 1.2 copy-done.1
  51.3 9.4 %attend_far.1 = (s16[32,2176]{1,0:T(8,128)(2,1)S(1)}, bf16[1024,1280]{1,0:T(8,128)(2,1)S(1)}) custom-call(s32[32]{0:T(128)S(1)} %convert_add_fusion.places, s32[32]{0:T(128)S(1)} %get-tuple-element.36.block_ids, s32[3]{0:T(128)S(1)} %pad_add_fusion.place, s16[512,640]{1,0:T(8,128)(2,1)S(1)} %pack_queries.1.own, s16[512,640]{1,0:T(8,128)(2,1)} %collective-permute-done.other, ...), custom_call_target="tpu_custom_call" | custom-call | flops 4000000000 | bytes 6000000 | tf_op jit(solution)/shard_map/attend_far/pallas_call | solution.py:295
  60.7 2.0 %collective-permute-start.4 = (s16[32,2176]{1,0:T(8,128)(2,1)S(1)}, s16[32,2176]{1,0:T(8,128)(2,1)S(1)}, u32[]{:S(2)}, u32[]{:S(2)}) collective-permute-start(s16[32,2176]{1,0:T(8,128)(2,1)S(1)} %get-tuple-element.33), channel_id=1, source_target_pairs={{0,1},{1,0},{2,3},{3,2},{4,5},{5,4},{6,7},{7,6},{8,9},{9,8},{10,11... | collective-permute-start | bytes 417800 | tf_op jit(solution)/shard_map/ppermute | solution.py:491
  62.6 6.1 %attend_near.1.here = s16[32,2176]{1,0:T(8,128)(2,1)S(1)} custom-call(s32[32]{0:T(128)S(1)} %get-tuple-element.36.block_ids, s32[3]{0:T(128)S(1)} %pad_add_fusion.place, s16[512,640]{1,0:T(8,128)(2,1)S(1)} %pack_queries.1.own, s16[512,640]{1,0:T(8,128)(2,1)} %collective-permute-done.other, bf16[1024,1280]{1,0:T(8,128)(2,1)S(1)} %get-tuple-element.29.keys_s, ...), custom_call_target="tpu_custom_call" | custom-call | flops 4000000000 | bytes 6000000 | tf_op jit(solution)/shard_map/attend_near/pallas_call | solution.py:316
  68.7 4.0 %collective-permute-start.6 = (bf16[224,1024]{1,0:T(8,128)(2,1)}, bf16[224,1024]{1,0:T(8,128)(2,1)S(1)}, u32[]{:S(2)}, u32[]{:S(2)}) collective-permute-start(bf16[224,1024]{1,0:T(8,128)(2,1)} %collective-permute-done.3.near_other), channel_id=1, source_target_pairs={{0,16},{16,0},{1,17},{17,1},{2,18},{18,2},{3,19},{19,3},{4,20},{20... | collective-permute-start | bytes 1376264 | tf_op jit(solution)/shard_map/ppermute | solution.py:494
  72.7 1.1 merge.1
  73.8 23.4 %all-gather.2 = s16[512,2176]{1,0:T(8,128)(2,1)S(1)} all-gather(s16[32,2176]{1,0:T(8,128)(2,1)S(1)} %merge.1), channel_id=2, replica_groups=mesh['x'=4,'y'=4,'core'=2,'zq'=8,'zb'=2] {'x','y'}, dimensions={0}, use_global_device_ids=true | all-gather | bytes 2367488 | tf_op jit(solution)/shard_map/all_gather | solution.py:495
  97.2 2.6 %project.1 = bf16[2,16,56,128]{3,2,1,0:T(8,128)(2,1)S(1)} custom-call(s32[3]{0:T(128)S(1)} %pad_add_fusion.place, s16[16,32,2176]{2,1,0:T(8,128)(2,1)S(1)} %bitcast.19, bf16[224,1024]{1,0:T(8,128)(2,1)S(1)} %bitcast.25, bf16[224,1024]{1,0:T(8,128)(2,1)} %collective-permute-done.3.near_other, bf16[224,1024]{1,0:T(8,128)(2,1)} %collective-permute-done.5.far_own, ...), custom_call_target="tpu_custom_call" | custom-call | flops 1000000000 | bytes 7000000 | tf_op jit(solution)/shard_map/project/pallas_call | solution.py:401
  99.9 47.3 %all_to_all.10 = bf16[32,56,128]{2,1,0:T(8,128)(2,1)} all-to-all(bf16[32,56,128]{2,1,0:T(8,128)(2,1)S(1)} %bitcast.22), channel_id=1, replica_groups=mesh['x'=4,'y'=4,'core'=2,'zq'=8,'zb'=2] {'core','zq','zb'}, dimensions={0} | all-to-all | bytes 917504 | tf_op jit(solution)/shard_map/all_to_all | solution.py:498
  147.2 1.8 %add_parts.1 = bf16[224,128]{1,0:T(8,128)(2,1)} custom-call(bf16[2,8,2,56,128]{4,3,2,1,0:T(8,128)(2,1)} %bitcast.26), custom_call_target="tpu_custom_call" | custom-call | tf_op jit(solution)/shard_map/add_parts/pallas_call | solution.py:440
  (13 shorter events, 0.8 us)
Async XLA Ops:
  5.1 45.0 %all-to-all-start = ((s16[32,2,32,640]{3,2,1,0:T(8,128)(2,1)}), s16[32,2,32,640]{3,2,1,0:T(8,128)(2,1)S(1)}, u32[]{:S(2)}, u32[]{:S(2)}) async-start(s16[32,2,32,640]{3,2,1,0:T(8,128)(2,1)} %parcels.1), calls=%async_computation | async-start | bytes 5242880 | tf_op jit(solution)/shard_map/all_to_all | solution.py:467
  20.7 15.2 %collective-permute-start.1 = (bf16[4,512,128]{2,1,0:T(8,128)(2,1)S(1)}, bf16[4,512,128]{2,1,0:T(8,128)(2,1)}, u32[]{:S(2)}, u32[]{:S(2)}) collective-permute-start(bf16[4,512,128]{2,1,0:T(8,128)(2,1)S(1)} %constant_dynamic-slice_fusion), channel_id=1, source_target_pairs={{0,1},{1,0},{2,3},{3,2},{4,5},{5,4},{6,7},{7,6},{8,9},{9,8},{10,11... | collective-permute-start | bytes 1572872 | tf_op jit(solution)/shard_map/ppermute | solution.py:483
  22.6 27.3 %collective-permute-start = (s16[512,640]{1,0:T(8,128)(2,1)S(1)}, s16[512,640]{1,0:T(8,128)(2,1)}, u32[]{:S(2)}, u32[]{:S(2)}) collective-permute-start(s16[512,640]{1,0:T(8,128)(2,1)S(1)} %pack_queries.1.own), channel_id=1, source_target_pairs={{0,1},{1,0},{2,3},{3,2},{4,5},{5,4},{6,7},{7,6},{8,9},{9,8},{10,11... | collective-permute-start | bytes 1966088 | tf_op jit(solution)/shard_map/ppermute | solution.py:472
  35.9 14.2 %collective-permute-start.2 = (bf16[4,512,128]{2,1,0:T(8,128)(2,1)}, bf16[4,512,128]{2,1,0:T(8,128)(2,1)}, u32[]{:S(2)}, u32[]{:S(2)}) collective-permute-start(bf16[4,512,128]{2,1,0:T(8,128)(2,1)} %collective-permute-done.1.fetched), channel_id=1, source_target_pairs={{0,16},{16,0},{1,17},{17,1},{2,18},{18,2},{3,19},{19,3},{4,20},{20... | collective-permute-start | bytes 1572872 | tf_op jit(solution)/shard_map/ppermute | solution.py:484
  39.7 57.5 %collective-permute-start.5 = (bf16[224,1024]{1,0:T(8,128)(2,1)}, bf16[224,1024]{1,0:T(8,128)(2,1)}, u32[]{:S(2)}, u32[]{:S(2)}) collective-permute-start(bf16[224,1024]{1,0:T(8,128)(2,1)} %bitcast.23), channel_id=1, source_target_pairs={{0,16},{16,0},{1,17},{17,1},{2,18},{18,2},{3,19},{19,3},{4,20},{20... | collective-permute-start | bytes 1376264 | tf_op jit(solution)/shard_map/ppermute | solution.py:474
  41.8 27.0 %collective-permute-start.3 = (bf16[224,1024]{1,0:T(8,128)(2,1)}, bf16[224,1024]{1,0:T(8,128)(2,1)}, u32[]{:S(2)}, u32[]{:S(2)}) collective-permute-start(bf16[224,1024]{1,0:T(8,128)(2,1)} %bitcast.24), channel_id=1, source_target_pairs={{0,1},{1,0},{2,3},{3,2},{4,5},{5,4},{6,7},{7,6},{8,9},{9,8},{10,11... | collective-permute-start | bytes 1376264 | tf_op jit(solution)/shard_map/ppermute | solution.py:487
  50.0 1.2 copy-start.1
  60.7 12.0 %collective-permute-start.4 = (s16[32,2176]{1,0:T(8,128)(2,1)S(1)}, s16[32,2176]{1,0:T(8,128)(2,1)S(1)}, u32[]{:S(2)}, u32[]{:S(2)}) collective-permute-start(s16[32,2176]{1,0:T(8,128)(2,1)S(1)} %get-tuple-element.33), channel_id=1, source_target_pairs={{0,1},{1,0},{2,3},{3,2},{4,5},{5,4},{6,7},{7,6},{8,9},{9,8},{10,11... | collective-permute-start | bytes 417800 | tf_op jit(solution)/shard_map/ppermute | solution.py:491
  68.7 28.5 %copy-start = (bf16[1024,224]{0,1:T(8,128)(2,1)S(1)}, bf16[1024,224]{0,1:T(8,128)(2,1)}, u32[]{:S(2)}) copy-start(bf16[1024,224]{0,1:T(8,128)(2,1)} %param.9) | copy-start | bytes 1376260
  68.7 28.5 %collective-permute-start.6 = (bf16[224,1024]{1,0:T(8,128)(2,1)}, bf16[224,1024]{1,0:T(8,128)(2,1)S(1)}, u32[]{:S(2)}, u32[]{:S(2)}) collective-permute-start(bf16[224,1024]{1,0:T(8,128)(2,1)} %collective-permute-done.3.near_other), channel_id=1, source_target_pairs={{0,16},{16,0},{1,17},{17,1},{2,18},{18,2},{3,19},{19,3},{4,20},{20... | collective-permute-start | bytes 1376264 | tf_op jit(solution)/shard_map/ppermute | solution.py:494

commit v4 on v3

--- a/solution.py
+++ b/solution.py
@@ -70,7 +70,7 @@
     return pl.CostEstimate(flops=flops, bytes_accessed=nbytes, transcendentals=exps)
 
 
-def parcel_kernel(where, selected, latent_t, out, lists, stage, wide, coded, ids_v, ids, in_sems, id_sems, sems):
+def parcel_kernel(owner, member, selected, latent_t, out, lists, stage, wide, coded, ids_v, ids, in_sems, id_sems, sems):
     width, total = latent_t.shape
     blocks, part, padded = coded.shape
     block = total // blocks
@@ -84,7 +84,7 @@
         load.start()
         loads.append(load)
     fetch.wait()
-    offset = lists[...] - where[0]
+    offset = lists[...] - owner[0] * blocks
     mine = (offset >= 0) & (offset < blocks)
     first = jnp.min(jnp.where(mine, offset, blocks), axis=1, keepdims=True)
     last = jnp.max(jnp.where(mine, offset, -1), axis=1, keepdims=True)
@@ -96,7 +96,7 @@
         loads[n].wait()
         wide[:, :width] = stage[:, n * LANES : (n + 1) * LANES].T
         for m in range(LANES // block):
-            at = pl.multiple_of(m * block + where[1], part)
+            at = pl.multiple_of(m * block + member[0] * part, part)
             x = jnp.where(lanes < width, wide[pl.ds(at, part), :], 0.0)
             code = row_code(row_peak(x))
             full = jnp.where(lanes < width, to_int(x, code), code)
@@ -113,13 +113,13 @@
         pl.when(filled)(copy.wait)
 
 
-def make_parcels(where, selected, latent_t, blocks, part, padded):
+def make_parcels(owner, member, selected, latent_t, blocks, part, padded):
     receivers = selected.shape[0]
     width, total = latent_t.shape
     return pl.pallas_call(
         parcel_kernel,
         out_shape=jax.ShapeDtypeStruct((receivers, 2, part, padded), S16),
-        in_specs=[SMEM, HBM, HBM],
+        in_specs=[SMEM, SMEM, HBM, HBM],
         out_specs=HBM,
         scratch_shapes=[
             pltpu.VMEM(selected.shape, jnp.int32),
@@ -135,7 +135,7 @@
         compiler_params=pltpu.CompilerParams(vmem_limit_bytes=WHOLE),
         cost_estimate=cost(10**7, 4 * 10**6),
         name="parcels",
-    )(where, selected, latent_t)
+    )(owner, member, selected, latent_t)
 
 
 def pack_kernel(q, out, wide):
@@ -459,10 +459,8 @@
     columns = out_proj.shape[1]
     part = block // PAIR
     swap = [(0, 1), (1, 0)]
-    start = member * part
-
-    where = jnp.stack([(ctx_index * per_owner).astype(jnp.int32), start])
-    parcels = make_parcels(where, selected, latent.T, per_owner, part, padded)
+
+    parcels = make_parcels(ctx_index[None].astype(jnp.int32), member[None], selected, latent.T, per_owner, part, padded)
     parcels, queries, value_near = lax.optimization_barrier((parcels, queries, value_proj))
     arrived = lax.all_to_all(parcels, plane, split_axis=0, concat_axis=0, tiled=True)
 
@@ -474,14 +472,13 @@
     far_own = lax.ppermute(near_own, "core", swap)
     place = jnp.stack([core, member, key_blocks - ctx_count + ctx_index]).astype(jnp.int32)
 
-    listed = lax.optimization_barrier((q_own, selected))[1]
+    fetched = lax.ppermute(lax.dynamic_slice_in_dim(value_near, core * (heads // 2), heads // 2, 0), "zb", swap)
+    passed = lax.ppermute(fetched, "core", swap)
+    listed = lax.optimization_barrier((fetched, selected))[1]
     own_list = lax.dynamic_slice_in_dim(listed, ctx_index, 1, 0)[0]
     owner = own_list // per_owner
     second = jnp.any((owner[None, :] == owner[:, None]) & (own_list[None, :] < own_list[:, None]), axis=1)
     places = owner * 2 + second.astype(jnp.int32)
-    places, value_near = lax.optimization_barrier((places, value_near))
-    fetched = lax.ppermute(lax.dynamic_slice_in_dim(value_near, core * (heads // 2), heads // 2, 0), "zb", swap)
-    passed = lax.ppermute(fetched, "core", swap)
 
     slab = lax.optimization_barrier((fetched, near_own))[1]
     near_other = lax.ppermute(slab, "zb", swap)

time: 150 us -> 146 us (0.973)
  blocking collectives: 70.7 us -> 68.7 us
  waiting for transfers between devices: 16.2 us -> 14.5 us
    ppermute x1, waiting for transfers between devices: 9.86 us -> 5.2 us  [on_device(): lax.ppermute(lax.dynamic_slice_in_dim(value_near, core * (heads // 2), he...]
    all_to_all x1, waiting for transfers between devices: 0.12 us -> 2.68 us  [on_device(): lax.all_to_all(parcels, plane, split_axis=0, concat_axis=0, tiled=True)]
    all_gather x1, blocking collectives: 23.4 us -> 21.8 us  [on_device(): lax.all_gather(merge(place, here, there, heads), ('x', 'y'), axis=0, tile...]
  transfers between devices with their start and end apart: 8 -> 8, of which waited for: 3 -> 3; matrix products, arithmetic and copies ran while one was open for 3% -> 4% of each run, Pallas kernels for 11% -> 12%
where the time goes in v4:
time: 146 us; the launch traced here: 145 us
  blocking collectives  68.7 us (47%)
  starting transfers between devices  29 us (20%)
  Pallas kernels  26 us (18%)
  waiting for transfers between devices  14.5 us (10%)
  local copies, waits for them, and re-layouts  4.68 us (3%)
  other arithmetic  1.67 us (1%)
    all_to_all x1, blocking collectives, on_device(): lax.all_to_all(partial, ('core', 'zq', 'zb'), split_axis=0, concat_axis=0...  47 us
    all_gather x1, blocking collectives, on_device(): lax.all_gather(merge(place, here, there, heads), ('x', 'y'), axis=0, tile...  21.8 us
    all_to_all x1, starting transfers between devices, on_device(): lax.all_to_all(parcels, plane, split_axis=0, concat_axis=0, tiled=True)  10.3 us
    pallas_call x1, Pallas kernels, attend_far(): pl.pallas_call(far_kernel, out_shape=(jax.ShapeDtypeStruct((part, PAIR *...  9.38 us
    ppermute x1, waiting for transfers between devices, on_device(): q_other = lax.ppermute(q_own, 'zb', swap)  6.65 us
    pallas_call x1, Pallas kernels, attend_near(): pl.pallas_call(near_kernel, out_shape=jax.ShapeDtypeStruct((part, PAIR *...  6.09 us
    ppermute x1, waiting for transfers between devices, on_device(): lax.ppermute(lax.dynamic_slice_in_dim(value_near, core * (heads // 2), he...  5.2 us
    pallas_call x1, Pallas kernels, make_parcels(): pl.pallas_call(parcel_kernel, out_shape=jax.ShapeDtypeStruct((receivers,...  4.53 us
  transfers between devices with their start and end apart: 8, of which 3 were waited for; matrix products, arithmetic and copies ran while one was open for 4% of the time, Pallas kernels for 12%

profile of v4, /device:TPU:1, one launch (start us, length us, event | category | flops | bytes accessed | tf_op | source)
XLA Modules:
  0.0 144.9 jit_solution(14826474283264885927)
XLA Ops:
  0.0 4.5 %parcels.1 = s16[32,2,32,640]{3,2,1,0:T(8,128)(2,1)} custom-call(s32[1]{0:T(128)} %bitcast.3.owner, s32[1]{0:T(128)} %bitcast.1.member, s32[32,32]{1,0:T(8,128)} %selected.1, f32[576,512]{1,0:T(8,128)} %bitcast.24), custom_call_target="tpu_custom_call" | custom-call | flops 10000000 | bytes 4000000 | tf_op jit(solution)/shard_map/parcels/pallas_call | solution.py:119
  4.5 10.3 %all-to-all-start = ((s16[32,2,32,640]{3,2,1,0:T(8,128)(2,1)}), s16[32,2,32,640]{3,2,1,0:T(8,128)(2,1)S(1)}, u32[]{:S(2)}, u32[]{:S(2)}) async-start(s16[32,2,32,640]{3,2,1,0:T(8,128)(2,1)} %parcels.1), calls=%async_computation | async-start | bytes 5242880 | tf_op jit(solution)/shard_map/all_to_all | solution.py:465
  14.9 1.9 %constant_dynamic-slice_fusion.1 = bf16[4,512,128]{2,1,0:T(8,128)(2,1)} fusion(bf16[8,512,128]{2,1,0:T(8,128)(2,1)} %vp_own.3, s32[]{:T(128)S(6)} %select_n.18), kind=kLoop, calls=%fused_computation.13 | loop fusion | bytes 1048580 | tf_op jit(solution)/shard_map/dynamic_slice | solution.py:475
  16.8 1.9 %collective-permute-start = (bf16[4,512,128]{2,1,0:T(8,128)(2,1)}, bf16[4,512,128]{2,1,0:T(8,128)(2,1)}, u32[]{:S(2)}, u32[]{:S(2)}) collective-permute-start(bf16[4,512,128]{2,1,0:T(8,128)(2,1)} %constant_dynamic-slice_fusion.1), channel_id=1, source_target_pairs={{0,1},{1,0},{2,3},{3,2},{4,5},{5,4},{6,7},{7,6},{8,9},{9,8},{10,11... | collective-permute-start | bytes 1572872 | tf_op jit(solution)/shard_map/ppermute | solution.py:475
  18.7 1.6 %copy.7 = f32[8,64,576]{2,1,0:T(8,128)S(1)} copy(f32[8,64,576]{2,0,1:T(8,128)} %bitcast.23) | data formatting | bytes 2359296 | tf_op jit(solution)/shard_map/transpose | solution.py:467
  20.6 3.4 %collective-permute-start.1 = (s16[512,640]{1,0:T(8,128)(2,1)S(1)}, s16[512,640]{1,0:T(8,128)(2,1)}, u32[]{:S(2)}, u32[]{:S(2)}) collective-permute-start(s16[512,640]{1,0:T(8,128)(2,1)S(1)} %pack_queries.1.own), channel_id=1, source_target_pairs={{0,1},{1,0},{2,3},{3,2},{4,5},{5,4},{6,7},{7,6},{8,9},{9,8},{10,11... | collective-permute-start | bytes 1966088 | tf_op jit(solution)/shard_map/ppermute | solution.py:470
  24.0 2.8 %collective-permute-start.5 = (bf16[224,1024]{1,0:T(8,128)(2,1)}, bf16[224,1024]{1,0:T(8,128)(2,1)}, u32[]{:S(2)}, u32[]{:S(2)}) collective-permute-start(bf16[224,1024]{1,0:T(8,128)(2,1)} %bitcast.10.near_own), channel_id=1, source_target_pairs={{0,16},{16,0},{1,17},{17,1},{2,18},{18,2},{3,19},{19,3},{4,20},{20... | collective-permute-start | bytes 1376264 | tf_op jit(solution)/shard_map/ppermute | solution.py:472
  26.9 5.2 %collective-permute-done.fetched = bf16[4,512,128]{2,1,0:T(8,128)(2,1)} collective-permute-done((bf16[4,512,128]{2,1,0:T(8,128)(2,1)}, bf16[4,512,128]{2,1,0:T(8,128)(2,1)}, u32[]{:S(2)}, u32[]{:S(2)}) %collective-permute-start) | collective-permute-done | bytes 524320 | tf_op jit(solution)/shard_map/ppermute | solution.py:475
  32.1 2.2 %collective-permute-start.3 = (bf16[224,1024]{1,0:T(8,128)(2,1)}, bf16[224,1024]{1,0:T(8,128)(2,1)}, u32[]{:S(2)}, u32[]{:S(2)}) collective-permute-start(bf16[224,1024]{1,0:T(8,128)(2,1)} %bitcast.10.near_own), channel_id=1, source_target_pairs={{0,1},{1,0},{2,3},{3,2},{4,5},{5,4},{6,7},{7,6},{8,9},{9,8},{10,11... | collective-permute-start | bytes 1376264 | tf_op jit(solution)/shard_map/ppermute | solution.py:484
  34.4 3.5 %collective-permute-start.2 = (bf16[4,512,128]{2,1,0:T(8,128)(2,1)}, bf16[4,512,128]{2,1,0:T(8,128)(2,1)}, u32[]{:S(2)}, u32[]{:S(2)}) collective-permute-start(bf16[4,512,128]{2,1,0:T(8,128)(2,1)} %collective-permute-done.fetched), channel_id=1, source_target_pairs={{0,16},{16,0},{1,17},{17,1},{2,18},{18,2},{3,19},{19,3},{4,20},{20... | collective-permute-start | bytes 1572872 | tf_op jit(solution)/shard_map/ppermute | solution.py:476
  37.9 0.7 fusion
  38.6 0.7 and_select_fusion.1
  39.5 6.7 %collective-permute-done.1.other = s16[512,640]{1,0:T(8,128)(2,1)} collective-permute-done((s16[512,640]{1,0:T(8,128)(2,1)S(1)}, s16[512,640]{1,0:T(8,128)(2,1)}, u32[]{:S(2)}, u32[]{:S(2)}) %collective-permute-start.1) | collective-permute-done | bytes 655392 | tf_op jit(solution)/shard_map/ppermute | solution.py:470
  46.2 2.7 %all-to-all-done = s16[32,2,32,640]{3,2,1,0:T(8,128)(2,1)S(1)} async-done(((s16[32,2,32,640]{3,2,1,0:T(8,128)(2,1)}), s16[32,2,32,640]{3,2,1,0:T(8,128)(2,1)S(1)}, u32[]{:S(2)}, u32[]{:S(2)}) %all-to-all-start) | async-done | bytes 2621472 | tf_op jit(solution)/shard_map/all_to_all | solution.py:465
  48.9 1.2 copy-done
  50.1 9.4 %attend_far.1 = (s16[32,2176]{1,0:T(8,128)(2,1)S(1)}, bf16[1024,1280]{1,0:T(8,128)(2,1)S(1)}) custom-call(s32[32]{0:T(128)S(1)} %convert_add_fusion.places, s32[32]{0:T(128)S(1)} %get-tuple-element.32.block_ids, s32[3]{0:T(128)S(1)} %pad_add_fusion.place, s16[512,640]{1,0:T(8,128)(2,1)S(1)} %pack_queries.1.own, ...), custom_call_target="tpu_custom_call" | custom-call | flops 4000000000 | bytes 6000000 | tf_op jit(solution)/shard_map/attend_far/pallas_call | solution.py:295
  59.5 1.9 %collective-permute-start.4 = (s16[32,2176]{1,0:T(8,128)(2,1)S(1)}, s16[32,2176]{1,0:T(8,128)(2,1)S(1)}, u32[]{:S(2)}, u32[]{:S(2)}) collective-permute-start(s16[32,2176]{1,0:T(8,128)(2,1)S(1)} %get-tuple-element.29), channel_id=1, source_target_pairs={{0,1},{1,0},{2,3},{3,2},{4,5},{5,4},{6,7},{7,6},{8,9},{9,8},{10,11... | collective-permute-start | bytes 417800 | tf_op jit(solution)/shard_map/ppermute | solution.py:488
  61.4 6.1 %attend_near.1.here = s16[32,2176]{1,0:T(8,128)(2,1)S(1)} custom-call(s32[32]{0:T(128)S(1)} %get-tuple-element.32.block_ids, s32[3]{0:T(128)S(1)} %pad_add_fusion.place, s16[512,640]{1,0:T(8,128)(2,1)S(1)} %pack_queries.1.own, s16[512,640]{1,0:T(8,128)(2,1)} %collective-permute-done.1.other, bf16[1024,1280]{1,0:T(8,128)(2,1)S(1)} %get-tuple-element.25.keys_s, ...), custom_call_target="tpu_custom_call" | custom-call | flops 4000000000 | bytes 6000000 | tf_op jit(solution)/shard_map/attend_near/pallas_call | solution.py:316
  67.5 2.9 %collective-permute-start.6 = (bf16[224,1024]{1,0:T(8,128)(2,1)}, bf16[224,1024]{1,0:T(8,128)(2,1)S(1)}, u32[]{:S(2)}, u32[]{:S(2)}) collective-permute-start(bf16[224,1024]{1,0:T(8,128)(2,1)} %collective-permute-done.3.near_other), channel_id=1, source_target_pairs={{0,16},{16,0},{1,17},{17,1},{2,18},{18,2},{3,19},{19,3},{4,20},{20... | collective-permute-start | bytes 1376264 | tf_op jit(solution)/shard_map/ppermute | solution.py:491
  70.4 1.1 merge.1
  71.5 21.8 %all-gather.2 = s16[512,2176]{1,0:T(8,128)(2,1)S(1)} all-gather(s16[32,2176]{1,0:T(8,128)(2,1)S(1)} %merge.1), channel_id=2, replica_groups=mesh['x'=4,'y'=4,'core'=2,'zq'=8,'zb'=2] {'x','y'}, dimensions={0}, use_global_device_ids=true | all-gather | bytes 2367488 | tf_op jit(solution)/shard_map/all_gather | solution.py:492
  93.3 2.8 %project.1 = bf16[2,16,56,128]{3,2,1,0:T(8,128)(2,1)S(1)} custom-call(s32[3]{0:T(128)S(1)} %pad_add_fusion.place, s16[16,32,2176]{2,1,0:T(8,128)(2,1)S(1)} %bitcast.18, bf16[224,1024]{1,0:T(8,128)(2,1)} %bitcast.10.near_own, bf16[224,1024]{1,0:T(8,128)(2,1)} %collective-permute-done.3.near_other, bf16[224,1024]{1,0:T(8,128)(2,1)} %collective-permute-done.5.far_own, ...), custom_call_target="tpu_custom_call" | custom-call | flops 1000000000 | bytes 7000000 | tf_op jit(solution)/shard_map/project/pallas_call | solution.py:401
  96.1 47.0 %all_to_all.10 = bf16[32,56,128]{2,1,0:T(8,128)(2,1)} all-to-all(bf16[32,56,128]{2,1,0:T(8,128)(2,1)S(1)} %bitcast.21), channel_id=1, replica_groups=mesh['x'=4,'y'=4,'core'=2,'zq'=8,'zb'=2] {'core','zq','zb'}, dimensions={0} | all-to-all | bytes 917504 | tf_op jit(solution)/shard_map/all_to_all | solution.py:495
  143.0 1.8 %add_parts.1 = bf16[224,128]{1,0:T(8,128)(2,1)} custom-call(bf16[2,8,2,56,128]{4,3,2,1,0:T(8,128)(2,1)} %bitcast.22), custom_call_target="tpu_custom_call" | custom-call | tf_op jit(solution)/shard_map/add_parts/pallas_call | solution.py:440
  (10 shorter events, 0.7 us)
Async XLA Ops:
  4.5 44.3 %all-to-all-start = ((s16[32,2,32,640]{3,2,1,0:T(8,128)(2,1)}), s16[32,2,32,640]{3,2,1,0:T(8,128)(2,1)S(1)}, u32[]{:S(2)}, u32[]{:S(2)}) async-start(s16[32,2,32,640]{3,2,1,0:T(8,128)(2,1)} %parcels.1), calls=%async_computation | async-start | bytes 5242880 | tf_op jit(solution)/shard_map/all_to_all | solution.py:465
  16.8 15.4 %collective-permute-start = (bf16[4,512,128]{2,1,0:T(8,128)(2,1)}, bf16[4,512,128]{2,1,0:T(8,128)(2,1)}, u32[]{:S(2)}, u32[]{:S(2)}) collective-permute-start(bf16[4,512,128]{2,1,0:T(8,128)(2,1)} %constant_dynamic-slice_fusion.1), channel_id=1, source_target_pairs={{0,1},{1,0},{2,3},{3,2},{4,5},{5,4},{6,7},{7,6},{8,9},{9,8},{10,11... | collective-permute-start | bytes 1572872 | tf_op jit(solution)/shard_map/ppermute | solution.py:475
  20.6 25.5 %collective-permute-start.1 = (s16[512,640]{1,0:T(8,128)(2,1)S(1)}, s16[512,640]{1,0:T(8,128)(2,1)}, u32[]{:S(2)}, u32[]{:S(2)}) collective-permute-start(s16[512,640]{1,0:T(8,128)(2,1)S(1)} %pack_queries.1.own), channel_id=1, source_target_pairs={{0,1},{1,0},{2,3},{3,2},{4,5},{5,4},{6,7},{7,6},{8,9},{9,8},{10,11... | collective-permute-start | bytes 1966088 | tf_op jit(solution)/shard_map/ppermute | solution.py:470
  24.0 69.3 %collective-permute-start.5 = (bf16[224,1024]{1,0:T(8,128)(2,1)}, bf16[224,1024]{1,0:T(8,128)(2,1)}, u32[]{:S(2)}, u32[]{:S(2)}) collective-permute-start(bf16[224,1024]{1,0:T(8,128)(2,1)} %bitcast.10.near_own), channel_id=1, source_target_pairs={{0,16},{16,0},{1,17},{17,1},{2,18},{18,2},{3,19},{19,3},{4,20},{20... | collective-permute-start | bytes 1376264 | tf_op jit(solution)/shard_map/ppermute | solution.py:472
  32.1 35.4 %collective-permute-start.3 = (bf16[224,1024]{1,0:T(8,128)(2,1)}, bf16[224,1024]{1,0:T(8,128)(2,1)}, u32[]{:S(2)}, u32[]{:S(2)}) collective-permute-start(bf16[224,1024]{1,0:T(8,128)(2,1)} %bitcast.10.near_own), channel_id=1, source_target_pairs={{0,1},{1,0},{2,3},{3,2},{4,5},{5,4},{6,7},{7,6},{8,9},{9,8},{10,11... | collective-permute-start | bytes 1376264 | tf_op jit(solution)/shard_map/ppermute | solution.py:484
  34.4 14.5 %collective-permute-start.2 = (bf16[4,512,128]{2,1,0:T(8,128)(2,1)}, bf16[4,512,128]{2,1,0:T(8,128)(2,1)}, u32[]{:S(2)}, u32[]{:S(2)}) collective-permute-start(bf16[4,512,128]{2,1,0:T(8,128)(2,1)} %collective-permute-done.fetched), channel_id=1, source_target_pairs={{0,16},{16,0},{1,17},{17,1},{2,18},{18,2},{3,19},{19,3},{4,20},{20... | collective-permute-start | bytes 1572872 | tf_op jit(solution)/shard_map/ppermute | solution.py:476
  48.8 1.2 copy-start
  59.5 11.0 %collective-permute-start.4 = (s16[32,2176]{1,0:T(8,128)(2,1)S(1)}, s16[32,2176]{1,0:T(8,128)(2,1)S(1)}, u32[]{:S(2)}, u32[]{:S(2)}) collective-permute-start(s16[32,2176]{1,0:T(8,128)(2,1)S(1)} %get-tuple-element.29), channel_id=1, source_target_pairs={{0,1},{1,0},{2,3},{3,2},{4,5},{5,4},{6,7},{7,6},{8,9},{9,8},{10,11... | collective-permute-start | bytes 417800 | tf_op jit(solution)/shard_map/ppermute | solution.py:488
  67.5 25.8 %collective-permute-start.6 = (bf16[224,1024]{1,0:T(8,128)(2,1)}, bf16[224,1024]{1,0:T(8,128)(2,1)S(1)}, u32[]{:S(2)}, u32[]{:S(2)}) collective-permute-start(bf16[224,1024]{1,0:T(8,128)(2,1)} %collective-permute-done.3.near_other), channel_id=1, source_target_pairs={{0,16},{16,0},{1,17},{17,1},{2,18},{18,2},{3,19},{19,3},{4,20},{20... | collective-permute-start | bytes 1376264 | tf_op jit(solution)/shard_map/ppermute | solution.py:491

commit v5 on v4

--- a/solution.py
+++ b/solution.py
@@ -15,7 +15,7 @@
 F32, BF16, S16 = jnp.float32, jnp.bfloat16, jnp.int16
 LANES = 128
 PAIR = 2
-LIMIT = 24 * 1024 * 1024
+LIMIT = 32 * 1024 * 1024
 WHOLE = 60 * 1024 * 1024
 SMEM = pl.BlockSpec(memory_space=pltpu.SMEM)
 VMEM = pl.BlockSpec(memory_space=pltpu.VMEM)
@@ -70,7 +70,14 @@
     return pl.CostEstimate(flops=flops, bytes_accessed=nbytes, transcendentals=exps)
 
 
-def parcel_kernel(owner, member, selected, latent_t, out, lists, stage, wide, coded, ids_v, ids, in_sems, id_sems, sems):
+def place_of(ctx, count, columns):
+    rest = count // columns
+    return ctx % rest * columns + ctx // rest
+
+
+def parcel_kernel(
+    owner, member, selected, latent_t, out, lists, stage, wide, coded, ids_v, ids, in_sems, id_sems, sems, *, columns
+):
     width, total = latent_t.shape
     blocks, part, padded = coded.shape
     block = total // blocks
@@ -79,8 +86,8 @@
     fetch.start()
     loads = []
     for n in range(groups):
-        columns = pl.ds(n * LANES, LANES)
-        load = pltpu.make_async_copy(latent_t.at[:, columns], stage.at[:, columns], in_sems.at[n])
+        span = pl.ds(n * LANES, LANES)
+        load = pltpu.make_async_copy(latent_t.at[:, span], stage.at[:, span], in_sems.at[n])
         load.start()
         loads.append(load)
     fetch.wait()
@@ -106,18 +113,19 @@
     for d in range(out.shape[0]):
         low, high = ids[d, 0], ids[d, 1]
         for s, (block_id, filled) in enumerate(((low, low <= high), (high, low < high))):
-            copy = pltpu.make_async_copy(coded.at[jnp.clip(block_id, 0, blocks - 1)], out.at[d, s], sems.at[2 * d + s])
+            source = coded.at[jnp.clip(block_id, 0, blocks - 1)]
+            copy = pltpu.make_async_copy(source, out.at[place_of(d, out.shape[0], columns), s], sems.at[2 * d + s])
             pl.when(filled)(copy.start)
             copies.append((filled, copy))
     for filled, copy in copies:
         pl.when(filled)(copy.wait)
 
 
-def make_parcels(owner, member, selected, latent_t, blocks, part, padded):
+def make_parcels(owner, member, selected, latent_t, blocks, part, padded, columns):
     receivers = selected.shape[0]
     width, total = latent_t.shape
     return pl.pallas_call(
-        parcel_kernel,
+        functools.partial(parcel_kernel, columns=columns),
         out_shape=jax.ShapeDtypeStruct((receivers, 2, part, padded), S16),
         in_specs=[SMEM, SMEM, HBM, HBM],
         out_specs=HBM,
@@ -138,75 +146,84 @@
     )(owner, member, selected, latent_t)
 
 
-def pack_kernel(q, out, wide):
-    width = q.shape[-1]
-    wide[:, :width] = q[...]
-    lanes = lane_ids(wide.shape)
-    x = jnp.where(lanes < width, wide[...], 0.0)
-    code = row_code(row_peak(x))
-    out[...] = as_s16(jnp.where(lanes < width, to_int(x, code), code))
-
-
-def pack_queries(q, padded):
-    rows = q.shape[0]
+def pack_kernel(q, out):
+    rows, width = q.shape
+    main = width // LANES
+    code = row_code(row_peak(jnp.max(jnp.abs(q[...]), axis=0, keepdims=True)))
+    for t in range(main):
+        out[t * rows : (t + 1) * rows, :] = as_s16(to_int(q[:, t * LANES : (t + 1) * LANES], code))
+    rest = to_int(q[:, main * LANES :], code)
+    both = jnp.concatenate([rest[: rows // 2], rest[rows // 2 :]], axis=-1)
+    out[main * rows : main * rows + rows // 2, :] = as_s16(both)
+    out[main * rows + rows // 2 :, :] = as_s16(jnp.broadcast_to(code, (16, LANES)))
+
+
+def pack_queries(q):
+    rows, width = q.shape
     return pl.pallas_call(
         pack_kernel,
-        out_shape=jax.ShapeDtypeStruct((rows, padded), S16),
+        out_shape=jax.ShapeDtypeStruct((rows * width // LANES + 16, LANES), S16),
         in_specs=[VMEM],
         out_specs=VMEM,
-        scratch_shapes=[pltpu.VMEM((rows, padded), F32)],
         compiler_params=PARAMS,
         cost_estimate=cost(10**7, 2 * 10**6),
         name="pack_queries",
     )(q)
 
 
-def load_queries(place, half, own, other, q_s, heads):
-    rows, padded = own.shape
-    block = rows // heads
-    part = block // PAIR
-    some = heads // 2
-    lat = padded - LANES
-    core, member = place[0], place[1]
-    begin = (member if half == 1 else 1 - member) * part
-    rope = lane_ids((part, LANES)) < LANES // 2
-    for n in range(PAIR * heads):
-        head = n
-        if n >= heads:
-            head = ((n - heads) // some + core) % 2 * some + n % some
-        at = pl.multiple_of(head * block + begin, part)
-        wide = as_f32((own if n < heads else other)[pl.ds(at, part), :])
-        wide = wide * (scale_of(wide[:, lat:])[:, LANES - 1 :] * (SCALE * LOG2E))
-        span = slice(n * part, (n + 1) * part)
-        high, low = halves(wide[:, :lat])
-        q_s[span, :lat] = high
-        q_s[span, lat : 2 * lat] = low
-        high, low = halves(jnp.where(rope, wide[:, lat:], 0.0))
+def load_queries(place, half, own, other, q_s):
+    some = q_s.shape[0] // PAIR
+    lat = (q_s.shape[1] - 2 * LANES) // 2
+    rows = PAIR * some
+    turn = place[1] if half == 1 else 1 - place[1]
+    lanes = lane_ids((some, LANES))
+    for n, q in enumerate((own, other)):
+        end = q.shape[0] - 16
+        factor = scale_of(as_f32(q[end:, :]))[:1, :1] * (SCALE * LOG2E)
+        span = slice(n * some, (n + 1) * some)
+        for t in range(lat // LANES):
+            at = pl.multiple_of(t * rows + turn * some, some)
+            high, low = halves(as_f32(q[pl.ds(at, some), :]) * factor)
+            q_s[span, t * LANES : (t + 1) * LANES] = high
+            q_s[span, lat + t * LANES : lat + (t + 1) * LANES] = low
+        rest = as_f32(q[end - some : end, :]) * factor
+        rest = jnp.where(turn == 0, rest, pltpu.roll(rest, LANES // 2, 1))
+        high, low = halves(jnp.where(lanes < LANES // 2, rest, 0.0))
         both = high.astype(F32) + pltpu.roll(low.astype(F32), LANES // 2, 1)
         q_s[span, 2 * lat : 2 * lat + LANES] = both.astype(BF16)
         q_s[span, 2 * lat + LANES :] = high
 
 
-def fetch_keys(places, arrived, slots, sems):
-    copies = []
-    for i in range(places.shape[0]):
-        copy = pltpu.make_async_copy(arrived.at[places[i]], slots.at[i], sems.at[i])
-        copy.start()
-        copies.append(copy)
-    return copies
-
-
-def split_keys(copies, slots, keys_s):
-    count, part, padded = slots.shape
+def half_kernel(core, values, half, sem):
+    some = half.shape[0]
+    copy = pltpu.make_async_copy(values.at[pl.ds(core[0] * some, some)], half, sem)
+    copy.start()
+    copy.wait()
+
+
+def half_values(core, values):
+    heads, lat, vdim = values.shape
+    return pl.pallas_call(
+        half_kernel,
+        out_shape=jax.ShapeDtypeStruct((heads // 2, lat, vdim), BF16),
+        in_specs=[SMEM, HBM],
+        out_specs=VMEM,
+        scratch_shapes=[pltpu.SemaphoreType.DMA],
+        compiler_params=pltpu.CompilerParams(vmem_limit_bytes=WHOLE),
+        cost_estimate=cost(10**4, 10**6),
+        name="half_values",
+    )(core, values)
+
+
+def split_keys(places, arrived, keys_s):
+    count = places.shape[0]
+    _, part, padded = arrived.shape
     lat = padded - LANES
-    step = 8
-    rope = lane_ids((step * part, LANES)) < LANES // 2
-    for c in range(count // step):
-        for i in range(c * step, (c + 1) * step):
-            copies[i].wait()
-        wide = as_f32(slots[c * step : (c + 1) * step].reshape(step * part, padded))
+    rope = lane_ids((part, LANES)) < LANES // 2
+    for i in range(count):
+        wide = as_f32(arrived[places[i]])
         wide = wide * scale_of(wide[:, lat:])[:, LANES - 1 :]
-        span = slice(c * step * part, (c + 1) * step * part)
+        span = slice(i * part, (i + 1) * part)
         high, low = halves(wide[:, :lat])
         keys_s[span, :lat] = high
         keys_s[span, lat : 2 * lat] = low
@@ -215,7 +232,7 @@
         keys_s[span, 2 * lat + LANES :] = halves(tail)[1]
 
 
-def attend_rows(block_ids, place, half, q, keys_s, vp_own, fetched, passed, out):
+def attend_rows(block_ids, place, half, q, keys_s, vp_own, fetched, passed, out, mixed_s, stat_s):
     heads, lat, vdim = vp_own.shape
     count = block_ids.shape[0]
     part = out.shape[0]
@@ -228,7 +245,7 @@
     if half == 0:
         room = room + (1 - 2 * place[1]) * part
     room = room - lane % part
-    spot = lax.broadcasted_iota(jnp.int32, (q.shape[0], 1), 0) % part
+    spot = lax.broadcasted_iota(jnp.int32, (q.shape[0], 1), 0) // heads % part
     s = (
         dot_nt(q[:, :lat], keys_s[:, :lat])
         + dot_nt(q[:, lat : 2 * lat], keys_s[:, :lat])
@@ -241,16 +258,19 @@
     norm = jnp.sum(p, axis=-1, keepdims=True)
     high, low = halves(p)
     mixed = dot_nn(high, keys_s[:, :lat]) + dot_nn(high, keys_s[:, lat : 2 * lat]) + dot_nn(low, keys_s[:, :lat])
-    high, low = halves(mixed / norm)
-    stat = (peak + jnp.log2(norm)) * 2.0
-    coarse = jnp.floor(stat)
-    fine = (stat - coarse) * 32767.0
-    results = []
+    mixed = mixed / norm
+    for t in range(lat // LANES):
+        mixed_s[t] = mixed[:, t * LANES : (t + 1) * LANES]
+    stat_s[...] = jnp.broadcast_to((peak + jnp.log2(norm)) * 2.0, stat_s.shape)
+    results, stats = [], []
     for n in range(PAIR * heads):
-        rows = slice(n * part, (n + 1) * part)
+        head = n if n < heads else heads * part + ((n - heads) // some + place[0]) % 2 * some + n % some
+        rows = pl.ds(head, part, stride=heads)
+        high, low = halves(jnp.concatenate([mixed_s[t, rows, :] for t in range(lat // LANES)], axis=-1))
         maps = vp_own[n] if n < heads else (fetched[n - heads] if n < heads + some else passed[n - heads - some])
-        both = dot_nn(jnp.concatenate([high[rows], low[rows]], axis=0), maps)
+        both = dot_nn(jnp.concatenate([high, low], axis=0), maps)
         results.append(both[:part] + both[part:])
+        stats.append(stat_s[rows, :])
     head_out = jnp.concatenate(results, axis=-1)
     code = row_code(row_peak(head_out))
     inner = head_out.shape[-1]
@@ -264,46 +284,46 @@
     lane = lane_ids((part, LANES))
     tail = code
     for n in range(PAIR * heads):
-        rows = slice(n * part, (n + 1) * part)
         at = n
         if n >= heads:
             turn = place[0] if n < heads + some else 1 - place[0]
             at = heads + turn * some + n % some
-        tail = jnp.where(lane == at, coarse[rows], tail)
-        tail = jnp.where(lane == at + PAIR * heads, fine[rows], tail)
+        coarse = jnp.floor(stats[n])
+        tail = jnp.where(lane == at, coarse, tail)
+        tail = jnp.where(lane == at + PAIR * heads, (stats[n] - coarse) * 32767.0, tail)
     out[:, inner:] = as_s16(tail)
 
 
 def far_kernel(
-    places, block_ids, place, own, other, arrived, vp_own, fetched, passed, out, keys_s, slots, q_s, sems
+    places, block_ids, place, own, other, arrived, vp_own, fetched, passed, out, keys_s, q_s, mixed_s, stat_s
 ):
-    copies = fetch_keys(places, arrived, slots, sems)
-    load_queries(place, 0, own, other, q_s, vp_own.shape[0])
-    split_keys(copies, slots, keys_s)
-    attend_rows(block_ids, place, 0, q_s, keys_s, vp_own, fetched, passed, out)
-
-
-def near_kernel(block_ids, place, own, other, keys_s, vp_own, fetched, passed, out, q_s):
-    load_queries(place, 1, own, other, q_s, vp_own.shape[0])
-    attend_rows(block_ids, place, 1, q_s, keys_s, vp_own, fetched, passed, out)
+    load_queries(place, 0, own, other, q_s)
+    split_keys(places, arrived, keys_s)
+    attend_rows(block_ids, place, 0, q_s, keys_s, vp_own, fetched, passed, out, mixed_s, stat_s)
+
+
+def near_kernel(block_ids, place, own, other, keys_s, vp_own, fetched, passed, out, q_s, mixed_s, stat_s):
+    load_queries(place, 1, own, other, q_s)
+    attend_rows(block_ids, place, 1, q_s, keys_s, vp_own, fetched, passed, out, mixed_s, stat_s)
 
 
 def attend_far(places, block_ids, place, own, other, arrived, vp_own, fetched, passed):
     count = places.shape[0]
     _, part, padded = arrived.shape
-    heads, _, vdim = vp_own.shape
+    heads, lat, vdim = vp_own.shape
+    rows = PAIR * heads * part
     return pl.pallas_call(
         far_kernel,
         out_shape=(
             jax.ShapeDtypeStruct((part, PAIR * heads * vdim + LANES), S16),
             jax.ShapeDtypeStruct((count * part, 2 * padded), BF16),
         ),
-        in_specs=[SMEM, SMEM, SMEM, VMEM, VMEM, HBM, VMEM, VMEM, VMEM],
+        in_specs=[SMEM, SMEM, SMEM] + [VMEM] * 6,
         out_specs=(VMEM, VMEM),
         scratch_shapes=[
-            pltpu.VMEM((count, part, padded), S16),
-            pltpu.VMEM((own.shape[0], 2 * padded), BF16),
-            pltpu.SemaphoreType.DMA((count,)),
+            pltpu.VMEM((rows, 2 * padded), BF16),
+            pltpu.VMEM((lat // LANES, rows, LANES), F32),
+            pltpu.VMEM((rows, LANES), F32),
         ],
         compiler_params=PARAMS,
         cost_estimate=cost(4 * 10**9, 6 * 10**6, 10**6),
@@ -312,13 +332,18 @@
 
 
 def attend_near(block_ids, place, own, other, keys, vp_own, fetched, passed, part):
-    heads, _, vdim = vp_own.shape
+    heads, lat, vdim = vp_own.shape
+    rows = PAIR * heads * part
     return pl.pallas_call(
         near_kernel,
         out_shape=jax.ShapeDtypeStruct((part, PAIR * heads * vdim + LANES), S16),
         in_specs=[SMEM, SMEM, VMEM, VMEM, VMEM, VMEM, VMEM, VMEM],
         out_specs=VMEM,
-        scratch_shapes=[pltpu.VMEM((own.shape[0], 2 * own.shape[1]), BF16)],
+        scratch_shapes=[
+            pltpu.VMEM((rows, keys.shape[1]), BF16),
+            pltpu.VMEM((lat // LANES, rows, LANES), F32),
+            pltpu.VMEM((rows, LANES), F32),
+        ],
         compiler_params=PARAMS,
         cost_estimate=cost(4 * 10**9, 6 * 10**6, 10**6),
         name="attend_near",
@@ -460,25 +485,25 @@
     part = block // PAIR
     swap = [(0, 1), (1, 0)]
 
-    parcels = make_parcels(ctx_index[None].astype(jnp.int32), member[None], selected, latent.T, per_owner, part, padded)
+    parcels = make_parcels(ctx_index[None].astype(jnp.int32), member[None], selected, latent.T, per_owner, part, padded, lax.axis_size("x"))
     parcels, queries, value_near = lax.optimization_barrier((parcels, queries, value_proj))
-    arrived = lax.all_to_all(parcels, plane, split_axis=0, concat_axis=0, tiled=True)
-
-    q = jnp.transpose(queries, (1, 0, 2)).reshape(heads * block, width)
+    arrived = lax.all_to_all(parcels, ("y", "core", "x"), split_axis=0, concat_axis=0, tiled=True)
+
+    q = queries.reshape(block * heads, width)
     near_own = out_proj.T
-    q_own = pack_queries(q, padded)
+    q_own = pack_queries(q)
     q_other = lax.ppermute(q_own, "zb", swap)
     near_own = lax.optimization_barrier((q_own, near_own))[1]
     far_own = lax.ppermute(near_own, "core", swap)
     place = jnp.stack([core, member, key_blocks - ctx_count + ctx_index]).astype(jnp.int32)
 
-    fetched = lax.ppermute(lax.dynamic_slice_in_dim(value_near, core * (heads // 2), heads // 2, 0), "zb", swap)
+    fetched = lax.ppermute(half_values(core[None], value_near), "zb", swap)
     passed = lax.ppermute(fetched, "core", swap)
     listed = lax.optimization_barrier((fetched, selected))[1]
     own_list = lax.dynamic_slice_in_dim(listed, ctx_index, 1, 0)[0]
     owner = own_list // per_owner
     second = jnp.any((owner[None, :] == owner[:, None]) & (own_list[None, :] < own_list[:, None]), axis=1)
-    places = owner * 2 + second.astype(jnp.int32)
+    places = place_of(owner, ctx_count, lax.axis_size("x")) * 2 + second.astype(jnp.int32)
 
     slab = lax.optimization_barrier((fetched, near_own))[1]
     near_other = lax.ppermute(slab, "zb", swap)

time: 146 us -> 142 us (0.973)
  local copies, waits for them, and re-layouts: 4.68 us -> 2.54 us
    pallas_call x1, Pallas kernels: 9.38 us -> 6.92 us  [attend_far(): pl.pallas_call(far_kernel, out_shape=(jax.ShapeDtypeStruct((part, PAIR *...]
    dynamic_slice x1 -> x0, local copies, waits for them, and re-layouts: 1.88 us -> none  [on_device(): lax.dynamic_slice_in_dim(value_near, core * (heads // 2), heads // 2, 0)]
    pallas_call x2 -> x3, Pallas kernels: 4.91 us -> 6.7 us  [the longest x1 4.44 us: make_parcels(): pl.pallas_call(functools.partial(parcel_kernel, columns=columns), out_sha...]
    transpose x1 -> x0, local copies, waits for them, and re-layouts: 1.57 us -> none  [on_device(): q = jnp.transpose(queries, (1, 0, 2)).reshape(heads * block, width)]
  transfers between devices with their start and end apart: 8 -> 8, of which waited for: 3 -> 3; matrix products, arithmetic and copies ran while one was open for 4% -> 1% of each run, Pallas kernels for 12% -> 12%
where the time goes in v5:
time: 142 us; the launch traced here: 141 us
  blocking collectives  69.4 us (49%)
  starting transfers between devices  28.8 us (20%)
  Pallas kernels  25.6 us (18%)
  waiting for transfers between devices  13.4 us (9%)
  local copies, waits for them, and re-layouts  2.54 us (2%)
  other arithmetic  1.68 us (1%)
    all_to_all x1, blocking collectives, on_device(): lax.all_to_all(partial, ('core', 'zq', 'zb'), split_axis=0, concat_axis=0...  47.3 us
    all_gather x1, blocking collectives, on_device(): lax.all_gather(merge(place, here, there, heads), ('x', 'y'), axis=0, tile...  22.1 us
    all_to_all x1, starting transfers between devices, on_device(): lax.all_to_all(parcels, ('y', 'core', 'x'), split_axis=0, concat_axis=0,...  10.3 us
    pallas_call x1, Pallas kernels, attend_far(): pl.pallas_call(far_kernel, out_shape=(jax.ShapeDtypeStruct((part, PAIR *...  6.92 us
    pallas_call x1, Pallas kernels, attend_near(): pl.pallas_call(near_kernel, out_shape=jax.ShapeDtypeStruct((part, PAIR *...  6.29 us
    ppermute x1, waiting for transfers between devices, on_device(): fetched = lax.ppermute(half_values(core[None], value_near), 'zb', swap)  5.46 us
    ppermute x1, waiting for transfers between devices, on_device(): q_other = lax.ppermute(q_own, 'zb', swap)  5.38 us
    pallas_call x1, Pallas kernels, make_parcels(): pl.pallas_call(functools.partial(parcel_kernel, columns=columns), out_sha...  4.44 us
  transfers between devices with their start and end apart: 8, of which 3 were waited for; matrix products, arithmetic and copies ran while one was open for 1% of the time, Pallas kernels for 12%

profile of v5, /device:TPU:1, one launch (start us, length us, event | category | flops | bytes accessed | tf_op | source)
XLA Modules:
  0.0 141.5 jit_solution(5913265866495780739)
XLA Ops:
  0.0 4.4 %parcels.1 = s16[32,2,32,640]{3,2,1,0:T(8,128)(2,1)} custom-call(s32[1]{0:T(128)} %bitcast.3.owner, s32[1]{0:T(128)} %bitcast.1.member, s32[32,32]{1,0:T(8,128)} %selected.1, f32[576,512]{1,0:T(8,128)} %bitcast.22), custom_call_target="tpu_custom_call" | custom-call | flops 10000000 | bytes 4000000 | tf_op jit(solution)/shard_map/parcels/pallas_call | solution.py:127
  4.4 10.3 %all-to-all-start = ((s16[32,2,32,640]{3,2,1,0:T(8,128)(2,1)}), s16[32,2,32,640]{3,2,1,0:T(8,128)(2,1)S(1)}, u32[]{:S(2)}, u32[]{:S(2)}) async-start(s16[32,2,32,640]{3,2,1,0:T(8,128)(2,1)} %parcels.1), calls=%async_computation | async-start | bytes 5242880 | tf_op jit(solution)/shard_map/all_to_all | solution.py:490
  14.7 1.8 %half_values.1 = bf16[4,512,128]{2,1,0:T(8,128)(2,1)} custom-call(s32[1]{0:T(128)} %bitcast.core, bf16[8,512,128]{2,1,0:T(8,128)(2,1)} %vp_own.3), custom_call_target="tpu_custom_call" | custom-call | flops 10000 | bytes 1000000 | tf_op jit(solution)/shard_map/half_values/pallas_call | solution.py:206
  16.6 1.9 %collective-permute-start = (bf16[4,512,128]{2,1,0:T(8,128)(2,1)}, bf16[4,512,128]{2,1,0:T(8,128)(2,1)}, u32[]{:S(2)}, u32[]{:S(2)}) collective-permute-start(bf16[4,512,128]{2,1,0:T(8,128)(2,1)} %half_values.1), channel_id=1, source_target_pairs={{0,1},{1,0},{2,3},{3,2},{4,5},{5,4},{6,7},{7,6},{8,9},{9,8},{10,11... | collective-permute-start | bytes 1572872 | tf_op jit(solution)/shard_map/ppermute | solution.py:500
  18.5 1.3 copy-done
  20.3 3.4 %collective-permute-start.1 = (s16[2320,128]{1,0:T(8,128)(2,1)S(1)}, s16[2320,128]{1,0:T(8,128)(2,1)}, u32[]{:S(2)}, u32[]{:S(2)}) collective-permute-start(s16[2320,128]{1,0:T(8,128)(2,1)S(1)} %pack_queries.1.own), channel_id=1, source_target_pairs={{0,1},{1,0},{2,3},{3,2},{4,5},{5,4},{6,7},{7,6},{8,9},{9,8},{10,11... | collective-permute-start | bytes 1781768 | tf_op jit(solution)/shard_map/ppermute | solution.py:495
  23.6 2.8 %collective-permute-start.5 = (bf16[224,1024]{1,0:T(8,128)(2,1)}, bf16[224,1024]{1,0:T(8,128)(2,1)}, u32[]{:S(2)}, u32[]{:S(2)}) collective-permute-start(bf16[224,1024]{1,0:T(8,128)(2,1)} %bitcast.9.near_own), channel_id=1, source_target_pairs={{0,16},{16,0},{1,17},{17,1},{2,18},{18,2},{3,19},{19,3},{4,20},{20... | collective-permute-start | bytes 1376264 | tf_op jit(solution)/shard_map/ppermute | solution.py:497
  26.5 5.5 %collective-permute-done.fetched = bf16[4,512,128]{2,1,0:T(8,128)(2,1)} collective-permute-done((bf16[4,512,128]{2,1,0:T(8,128)(2,1)}, bf16[4,512,128]{2,1,0:T(8,128)(2,1)}, u32[]{:S(2)}, u32[]{:S(2)}) %collective-permute-start) | collective-permute-done | bytes 524320 | tf_op jit(solution)/shard_map/ppermute | solution.py:500
  32.0 2.2 %collective-permute-start.3 = (bf16[224,1024]{1,0:T(8,128)(2,1)}, bf16[224,1024]{1,0:T(8,128)(2,1)}, u32[]{:S(2)}, u32[]{:S(2)}) collective-permute-start(bf16[224,1024]{1,0:T(8,128)(2,1)} %bitcast.9.near_own), channel_id=1, source_target_pairs={{0,1},{1,0},{2,3},{3,2},{4,5},{5,4},{6,7},{7,6},{8,9},{9,8},{10,11... | collective-permute-start | bytes 1376264 | tf_op jit(solution)/shard_map/ppermute | solution.py:509
  34.2 3.5 %collective-permute-start.2 = (bf16[4,512,128]{2,1,0:T(8,128)(2,1)}, bf16[4,512,128]{2,1,0:T(8,128)(2,1)}, u32[]{:S(2)}, u32[]{:S(2)}) collective-permute-start(bf16[4,512,128]{2,1,0:T(8,128)(2,1)} %collective-permute-done.fetched), channel_id=1, source_target_pairs={{0,16},{16,0},{1,17},{17,1},{2,18},{18,2},{3,19},{19,3},{4,20},{20... | collective-permute-start | bytes 1572872 | tf_op jit(solution)/shard_map/ppermute | solution.py:501
  37.7 0.7 fusion.2
  38.4 0.7 and_select_fusion.3
  39.3 5.4 %collective-permute-done.1.other = s16[2320,128]{1,0:T(8,128)(2,1)} collective-permute-done((s16[2320,128]{1,0:T(8,128)(2,1)S(1)}, s16[2320,128]{1,0:T(8,128)(2,1)}, u32[]{:S(2)}, u32[]{:S(2)}) %collective-permute-start.1) | collective-permute-done | bytes 593952 | tf_op jit(solution)/shard_map/ppermute | solution.py:495
  44.7 2.5 %all-to-all-done = s16[32,2,32,640]{3,2,1,0:T(8,128)(2,1)S(1)} async-done(((s16[32,2,32,640]{3,2,1,0:T(8,128)(2,1)}), s16[32,2,32,640]{3,2,1,0:T(8,128)(2,1)S(1)}, u32[]{:S(2)}, u32[]{:S(2)}) %all-to-all-start) | async-done | bytes 2621472 | tf_op jit(solution)/shard_map/all_to_all | solution.py:490
  47.3 1.2 copy-done.1
  48.5 6.9 %attend_far.1 = (s16[32,2176]{1,0:T(8,128)(2,1)S(1)}, bf16[1024,1280]{1,0:T(8,128)(2,1)S(1)}) custom-call(s32[32]{0:T(128)S(1)} %convert_add_fusion.places, s32[32]{0:T(128)S(1)} %get-tuple-element.32.block_ids, s32[3]{0:T(128)S(1)} %pad_add_fusion.place, s16[2320,128]{1,0:T(8,128)(2,1)S(1)} %pack_queries.1.own, ...), custom_call_target="tpu_custom_call" | custom-call | flops 4000000000 | bytes 6000000 | tf_op jit(solution)/shard_map/attend_far/pallas_call | solution.py:315
  55.4 1.9 %collective-permute-start.4 = (s16[32,2176]{1,0:T(8,128)(2,1)S(1)}, s16[32,2176]{1,0:T(8,128)(2,1)S(1)}, u32[]{:S(2)}, u32[]{:S(2)}) collective-permute-start(s16[32,2176]{1,0:T(8,128)(2,1)S(1)} %get-tuple-element.29), channel_id=1, source_target_pairs={{0,1},{1,0},{2,3},{3,2},{4,5},{5,4},{6,7},{7,6},{8,9},{9,8},{10,11... | collective-permute-start | bytes 417800 | tf_op jit(solution)/shard_map/ppermute | solution.py:513
  57.3 6.3 %attend_near.1.here = s16[32,2176]{1,0:T(8,128)(2,1)S(1)} custom-call(s32[32]{0:T(128)S(1)} %get-tuple-element.32.block_ids, s32[3]{0:T(128)S(1)} %pad_add_fusion.place, s16[2320,128]{1,0:T(8,128)(2,1)S(1)} %pack_queries.1.own, s16[2320,128]{1,0:T(8,128)(2,1)} %collective-permute-done.1.other, bf16[1024,1280]{1,0:T(8,128)(2,1)S(1)} %get-tuple-element.25.keys_s, ...), custom_call_target="tpu_custom_call" | custom-call | flops 4000000000 | bytes 6000000 | tf_op jit(solution)/shard_map/attend_near/pallas_call | solution.py:337
  63.6 2.8 %collective-permute-start.6 = (bf16[224,1024]{1,0:T(8,128)(2,1)}, bf16[224,1024]{1,0:T(8,128)(2,1)S(1)}, u32[]{:S(2)}, u32[]{:S(2)}) collective-permute-start(bf16[224,1024]{1,0:T(8,128)(2,1)} %collective-permute-done.3.near_other), channel_id=1, source_target_pairs={{0,16},{16,0},{1,17},{17,1},{2,18},{18,2},{3,19},{19,3},{4,20},{20... | collective-permute-start | bytes 1376264 | tf_op jit(solution)/shard_map/ppermute | solution.py:516
  66.4 1.1 merge.1
  67.5 22.1 %all-gather.2 = s16[512,2176]{1,0:T(8,128)(2,1)S(1)} all-gather(s16[32,2176]{1,0:T(8,128)(2,1)S(1)} %merge.1), channel_id=2, replica_groups=mesh['x'=4,'y'=4,'core'=2,'zq'=8,'zb'=2] {'x','y'}, dimensions={0}, use_global_device_ids=true | all-gather | bytes 2367488 | tf_op jit(solution)/shard_map/all_gather | solution.py:517
  89.6 2.8 %project.1 = bf16[2,16,56,128]{3,2,1,0:T(8,128)(2,1)S(1)} custom-call(s32[3]{0:T(128)S(1)} %pad_add_fusion.place, s16[16,32,2176]{2,1,0:T(8,128)(2,1)S(1)} %bitcast.17, bf16[224,1024]{1,0:T(8,128)(2,1)} %bitcast.9.near_own, bf16[224,1024]{1,0:T(8,128)(2,1)} %collective-permute-done.3.near_other, bf16[224,1024]{1,0:T(8,128)(2,1)} %collective-permute-done.5.far_own, ...), custom_call_target="tpu_custom_call" | custom-call | flops 1000000000 | bytes 7000000 | tf_op jit(solution)/shard_map/project/pallas_call | solution.py:426
  92.4 47.3 %all_to_all.10 = bf16[32,56,128]{2,1,0:T(8,128)(2,1)} all-to-all(bf16[32,56,128]{2,1,0:T(8,128)(2,1)S(1)} %bitcast.19), channel_id=1, replica_groups=mesh['x'=4,'y'=4,'core'=2,'zq'=8,'zb'=2] {'core','zq','zb'}, dimensions={0} | all-to-all | bytes 917504 | tf_op jit(solution)/shard_map/all_to_all | solution.py:520
  139.7 1.8 %add_parts.1 = bf16[224,128]{1,0:T(8,128)(2,1)} custom-call(bf16[2,8,2,56,128]{4,3,2,1,0:T(8,128)(2,1)} %bitcast.21), custom_call_target="tpu_custom_call" | custom-call | tf_op jit(solution)/shard_map/add_parts/pallas_call | solution.py:465
  (11 shorter events, 0.7 us)
Async XLA Ops:
  4.4 42.8 %all-to-all-start = ((s16[32,2,32,640]{3,2,1,0:T(8,128)(2,1)}), s16[32,2,32,640]{3,2,1,0:T(8,128)(2,1)S(1)}, u32[]{:S(2)}, u32[]{:S(2)}) async-start(s16[32,2,32,640]{3,2,1,0:T(8,128)(2,1)} %parcels.1), calls=%async_computation | async-start | bytes 5242880 | tf_op jit(solution)/shard_map/all_to_all | solution.py:490
  16.6 15.4 %collective-permute-start = (bf16[4,512,128]{2,1,0:T(8,128)(2,1)}, bf16[4,512,128]{2,1,0:T(8,128)(2,1)}, u32[]{:S(2)}, u32[]{:S(2)}) collective-permute-start(bf16[4,512,128]{2,1,0:T(8,128)(2,1)} %half_values.1), channel_id=1, source_target_pairs={{0,1},{1,0},{2,3},{3,2},{4,5},{5,4},{6,7},{7,6},{8,9},{9,8},{10,11... | collective-permute-start | bytes 1572872 | tf_op jit(solution)/shard_map/ppermute | solution.py:500
  18.5 1.3 copy-start
  20.3 24.5 %collective-permute-start.1 = (s16[2320,128]{1,0:T(8,128)(2,1)S(1)}, s16[2320,128]{1,0:T(8,128)(2,1)}, u32[]{:S(2)}, u32[]{:S(2)}) collective-permute-start(s16[2320,128]{1,0:T(8,128)(2,1)S(1)} %pack_queries.1.own), channel_id=1, source_target_pairs={{0,1},{1,0},{2,3},{3,2},{4,5},{5,4},{6,7},{7,6},{8,9},{9,8},{10,11... | collective-permute-start | bytes 1781768 | tf_op jit(solution)/shard_map/ppermute | solution.py:495
  23.6 66.0 %collective-permute-start.5 = (bf16[224,1024]{1,0:T(8,128)(2,1)}, bf16[224,1024]{1,0:T(8,128)(2,1)}, u32[]{:S(2)}, u32[]{:S(2)}) collective-permute-start(bf16[224,1024]{1,0:T(8,128)(2,1)} %bitcast.9.near_own), channel_id=1, source_target_pairs={{0,16},{16,0},{1,17},{17,1},{2,18},{18,2},{3,19},{19,3},{4,20},{20... | collective-permute-start | bytes 1376264 | tf_op jit(solution)/shard_map/ppermute | solution.py:497
  32.0 31.6 %collective-permute-start.3 = (bf16[224,1024]{1,0:T(8,128)(2,1)}, bf16[224,1024]{1,0:T(8,128)(2,1)}, u32[]{:S(2)}, u32[]{:S(2)}) collective-permute-start(bf16[224,1024]{1,0:T(8,128)(2,1)} %bitcast.9.near_own), channel_id=1, source_target_pairs={{0,1},{1,0},{2,3},{3,2},{4,5},{5,4},{6,7},{7,6},{8,9},{9,8},{10,11... | collective-permute-start | bytes 1376264 | tf_op jit(solution)/shard_map/ppermute | solution.py:509
  34.2 13.0 %collective-permute-start.2 = (bf16[4,512,128]{2,1,0:T(8,128)(2,1)}, bf16[4,512,128]{2,1,0:T(8,128)(2,1)}, u32[]{:S(2)}, u32[]{:S(2)}) collective-permute-start(bf16[4,512,128]{2,1,0:T(8,128)(2,1)} %collective-permute-done.fetched), channel_id=1, source_target_pairs={{0,16},{16,0},{1,17},{17,1},{2,18},{18,2},{3,19},{19,3},{4,20},{20... | collective-permute-start | bytes 1572872 | tf_op jit(solution)/shard_map/ppermute | solution.py:501
  47.3 1.2 copy-start.1
  55.4 11.0 %collective-permute-start.4 = (s16[32,2176]{1,0:T(8,128)(2,1)S(1)}, s16[32,2176]{1,0:T(8,128)(2,1)S(1)}, u32[]{:S(2)}, u32[]{:S(2)}) collective-permute-start(s16[32,2176]{1,0:T(8,128)(2,1)S(1)} %get-tuple-element.29), channel_id=1, source_target_pairs={{0,1},{1,0},{2,3},{3,2},{4,5},{5,4},{6,7},{7,6},{8,9},{9,8},{10,11... | collective-permute-start | bytes 417800 | tf_op jit(solution)/shard_map/ppermute | solution.py:513
  63.6 26.0 %collective-permute-start.6 = (bf16[224,1024]{1,0:T(8,128)(2,1)}, bf16[224,1024]{1,0:T(8,128)(2,1)S(1)}, u32[]{:S(2)}, u32[]{:S(2)}) collective-permute-start(bf16[224,1024]{1,0:T(8,128)(2,1)} %collective-permute-done.3.near_other), channel_id=1, source_target_pairs={{0,16},{16,0},{1,17},{17,1},{2,18},{18,2},{3,19},{19,3},{4,20},{20... | collective-permute-start | bytes 1376264 | tf_op jit(solution)/shard_map/ppermute | solution.py:516

commit v6 on v5

--- a/solution.py
+++ b/solution.py
@@ -192,6 +192,22 @@
         both = high.astype(F32) + pltpu.roll(low.astype(F32), LANES // 2, 1)
         q_s[span, 2 * lat : 2 * lat + LANES] = both.astype(BF16)
         q_s[span, 2 * lat + LANES :] = high
+
+
+def split_kernel(place, own, other, out):
+    load_queries(place, 0, own, other, out)
+
+
+def split_far(place, own, other, rows, width):
+    return pl.pallas_call(
+        split_kernel,
+        out_shape=jax.ShapeDtypeStruct((rows, width), BF16),
+        in_specs=[SMEM, VMEM, VMEM],
+        out_specs=VMEM,
+        compiler_params=PARAMS,
+        cost_estimate=cost(10**7, 4 * 10**6),
+        name="split_far",
+    )(place, own, other)
 
 
 def half_kernel(core, values, half, sem):
@@ -295,11 +311,10 @@
 
 
 def far_kernel(
-    places, block_ids, place, own, other, arrived, vp_own, fetched, passed, out, keys_s, q_s, mixed_s, stat_s
+    places, block_ids, place, q, arrived, vp_own, fetched, passed, out, keys_s, mixed_s, stat_s
 ):
-    load_queries(place, 0, own, other, q_s)
     split_keys(places, arrived, keys_s)
-    attend_rows(block_ids, place, 0, q_s, keys_s, vp_own, fetched, passed, out, mixed_s, stat_s)
+    attend_rows(block_ids, place, 0, q, keys_s, vp_own, fetched, passed, out, mixed_s, stat_s)
 
 
 def near_kernel(block_ids, place, own, other, keys_s, vp_own, fetched, passed, out, q_s, mixed_s, stat_s):
@@ -307,7 +322,7 @@
     attend_rows(block_ids, place, 1, q_s, keys_s, vp_own, fetched, passed, out, mixed_s, stat_s)
 
 
-def attend_far(places, block_ids, place, own, other, arrived, vp_own, fetched, passed):
+def attend_far(places, block_ids, place, q, arrived, vp_own, fetched, passed):
     count = places.shape[0]
     _, part, padded = arrived.shape
     heads, lat, vdim = vp_own.shape
@@ -318,17 +333,16 @@
             jax.ShapeDtypeStruct((part, PAIR * heads * vdim + LANES), S16),
             jax.ShapeDtypeStruct((count * part, 2 * padded), BF16),
         ),
-        in_specs=[SMEM, SMEM, SMEM] + [VMEM] * 6,
+        in_specs=[SMEM, SMEM, SMEM] + [VMEM] * 5,
         out_specs=(VMEM, VMEM),
         scratch_shapes=[
-            pltpu.VMEM((rows, 2 * padded), BF16),
             pltpu.VMEM((lat // LANES, rows, LANES), F32),
             pltpu.VMEM((rows, LANES), F32),
         ],
         compiler_params=PARAMS,
         cost_estimate=cost(4 * 10**9, 6 * 10**6, 10**6),
         name="attend_far",
-    )(places, block_ids, place, own, other, arrived, vp_own, fetched, passed)
+    )(places, block_ids, place, q, arrived, vp_own, fetched, passed)
 
 
 def attend_near(block_ids, place, own, other, keys, vp_own, fetched, passed, part):
@@ -467,6 +481,8 @@
         out_shape=jax.ShapeDtypeStruct((columns, cores * groups * rows), BF16),
         in_specs=[VMEM],
         out_specs=VMEM,
+        compiler_params=PARAMS,
+        cost_estimate=cost(10**6, 10**6),
         name="add_parts",
     )(parts)
 
@@ -509,7 +525,8 @@
     near_other = lax.ppermute(slab, "zb", swap)
     arrived = arrived.reshape(2 * ctx_count, part, padded)
     arrived, q_own, q_other = lax.optimization_barrier((arrived, q_own, q_other))
-    for_partner, keys = attend_far(places, own_list, place, q_own, q_other, arrived, value_proj, fetched, passed)
+    q_far = split_far(place, q_own, q_other, heads * block, 2 * padded)
+    for_partner, keys = attend_far(places, own_list, place, q_far, arrived, value_proj, fetched, passed)
     there = lax.ppermute(for_partner, "zb", swap)
     here = attend_near(own_list, place, q_own, q_other, keys, value_proj, fetched, passed, part)
     here, near_other = lax.optimization_barrier((here, near_other))

time: 142 us -> 141 us (level)
    pallas_call x0 -> x1, Pallas kernels: none -> 1.63 us  [split_far(): pl.pallas_call(split_kernel, out_shape=jax.ShapeDtypeStruct((rows, width)...]
  transfers between devices with their start and end apart: 8 -> 8, of which waited for: 3 -> 3; matrix products, arithmetic and copies ran while one was open for 1% -> 1% of each run, Pallas kernels for 12% -> 13%
where the time goes in v6:
time: 141 us
  blocking collectives  69.3 us (49%)
  starting transfers between devices  29.6 us (21%)
  Pallas kernels  25.1 us (18%)
  waiting for transfers between devices  13.3 us (9%)
  other arithmetic  1.68 us (1%)
    all_to_all x1, blocking collectives, on_device(): lax.all_to_all(partial, ('core', 'zq', 'zb'), split_axis=0, concat_axis=0...  47.3 us
    all_gather x1, blocking collectives, on_device(): lax.all_gather(merge(place, here, there, heads), ('x', 'y'), axis=0, tile...  22.1 us
    all_to_all x1, starting transfers between devices, on_device(): lax.all_to_all(parcels, ('y', 'core', 'x'), split_axis=0, concat_axis=0,...  11 us
    pallas_call x1, Pallas kernels, attend_far(): pl.pallas_call(far_kernel, out_shape=(jax.ShapeDtypeStruct((part, PAIR *...  6.42 us
    pallas_call x1, Pallas kernels, attend_near(): pl.pallas_call(near_kernel, out_shape=jax.ShapeDtypeStruct((part, PAIR *...  6.28 us
    ppermute x1, waiting for transfers between devices, on_device(): fetched = lax.ppermute(half_values(core[None], value_near), 'zb', swap)  5.46 us
    ppermute x1, waiting for transfers between devices, on_device(): q_other = lax.ppermute(q_own, 'zb', swap)  5.34 us
    pallas_call x1, Pallas kernels, make_parcels(): pl.pallas_call(functools.partial(parcel_kernel, columns=columns), out_sha...  3.86 us
  transfers between devices with their start and end apart: 8, of which 3 were waited for; matrix products, arithmetic and copies ran while one was open for 1% of the time, Pallas kernels for 13%

profile of v6, /device:TPU:1, one launch (start us, length us, event | category | flops | bytes accessed | tf_op | source)
XLA Modules:
  0.0 140.6 jit_solution(7234456726817594257)
XLA Ops:
  0.0 3.9 %parcels.1 = s16[32,2,32,640]{3,2,1,0:T(8,128)(2,1)} custom-call(s32[1]{0:T(128)} %bitcast.3.owner, s32[1]{0:T(128)} %bitcast.1.member, s32[32,32]{1,0:T(8,128)} %selected.1, f32[576,512]{1,0:T(8,128)} %bitcast.22), custom_call_target="tpu_custom_call" | custom-call | flops 10000000 | bytes 4000000 | tf_op jit(solution)/shard_map/parcels/pallas_call | solution.py:127
  3.9 11.0 %all-to-all-start = ((s16[32,2,32,640]{3,2,1,0:T(8,128)(2,1)}), s16[32,2,32,640]{3,2,1,0:T(8,128)(2,1)S(1)}, u32[]{:S(2)}, u32[]{:S(2)}) async-start(s16[32,2,32,640]{3,2,1,0:T(8,128)(2,1)} %parcels.1), calls=%async_computation | async-start | bytes 5242880 | tf_op jit(solution)/shard_map/all_to_all | solution.py:506
  14.9 1.8 %half_values.1 = bf16[4,512,128]{2,1,0:T(8,128)(2,1)} custom-call(s32[1]{0:T(128)} %bitcast.core, bf16[8,512,128]{2,1,0:T(8,128)(2,1)} %vp_own.3), custom_call_target="tpu_custom_call" | custom-call | flops 10000 | bytes 1000000 | tf_op jit(solution)/shard_map/half_values/pallas_call | solution.py:222
  16.7 1.9 %collective-permute-start = (bf16[4,512,128]{2,1,0:T(8,128)(2,1)}, bf16[4,512,128]{2,1,0:T(8,128)(2,1)}, u32[]{:S(2)}, u32[]{:S(2)}) collective-permute-start(bf16[4,512,128]{2,1,0:T(8,128)(2,1)} %half_values.1), channel_id=1, source_target_pairs={{0,1},{1,0},{2,3},{3,2},{4,5},{5,4},{6,7},{7,6},{8,9},{9,8},{10,11... | collective-permute-start | bytes 1572872 | tf_op jit(solution)/shard_map/ppermute | solution.py:516
  18.7 1.3 copy-done
  20.4 3.4 %collective-permute-start.1 = (s16[2320,128]{1,0:T(8,128)(2,1)S(1)}, s16[2320,128]{1,0:T(8,128)(2,1)}, u32[]{:S(2)}, u32[]{:S(2)}) collective-permute-start(s16[2320,128]{1,0:T(8,128)(2,1)S(1)} %pack_queries.1.own), channel_id=1, source_target_pairs={{0,1},{1,0},{2,3},{3,2},{4,5},{5,4},{6,7},{7,6},{8,9},{9,8},{10,11... | collective-permute-start | bytes 1781768 | tf_op jit(solution)/shard_map/ppermute | solution.py:511
  23.8 2.8 %collective-permute-start.5 = (bf16[224,1024]{1,0:T(8,128)(2,1)}, bf16[224,1024]{1,0:T(8,128)(2,1)}, u32[]{:S(2)}, u32[]{:S(2)}) collective-permute-start(bf16[224,1024]{1,0:T(8,128)(2,1)} %bitcast.9.near_own), channel_id=1, source_target_pairs={{0,16},{16,0},{1,17},{17,1},{2,18},{18,2},{3,19},{19,3},{4,20},{20... | collective-permute-start | bytes 1376264 | tf_op jit(solution)/shard_map/ppermute | solution.py:513
  26.7 5.5 %collective-permute-done.fetched = bf16[4,512,128]{2,1,0:T(8,128)(2,1)} collective-permute-done((bf16[4,512,128]{2,1,0:T(8,128)(2,1)}, bf16[4,512,128]{2,1,0:T(8,128)(2,1)}, u32[]{:S(2)}, u32[]{:S(2)}) %collective-permute-start) | collective-permute-done | bytes 524320 | tf_op jit(solution)/shard_map/ppermute | solution.py:516
  32.1 2.2 %collective-permute-start.3 = (bf16[224,1024]{1,0:T(8,128)(2,1)}, bf16[224,1024]{1,0:T(8,128)(2,1)}, u32[]{:S(2)}, u32[]{:S(2)}) collective-permute-start(bf16[224,1024]{1,0:T(8,128)(2,1)} %bitcast.9.near_own), channel_id=1, source_target_pairs={{0,1},{1,0},{2,3},{3,2},{4,5},{5,4},{6,7},{7,6},{8,9},{9,8},{10,11... | collective-permute-start | bytes 1376264 | tf_op jit(solution)/shard_map/ppermute | solution.py:525
  34.3 3.6 %collective-permute-start.2 = (bf16[4,512,128]{2,1,0:T(8,128)(2,1)}, bf16[4,512,128]{2,1,0:T(8,128)(2,1)}, u32[]{:S(2)}, u32[]{:S(2)}) collective-permute-start(bf16[4,512,128]{2,1,0:T(8,128)(2,1)} %collective-permute-done.fetched), channel_id=1, source_target_pairs={{0,16},{16,0},{1,17},{17,1},{2,18},{18,2},{3,19},{19,3},{4,20},{20... | collective-permute-start | bytes 1572872 | tf_op jit(solution)/shard_map/ppermute | solution.py:517
  37.9 0.7 fusion.2
  38.6 0.7 and_select_fusion.3
  39.5 5.3 %collective-permute-done.1.other = s16[2320,128]{1,0:T(8,128)(2,1)} collective-permute-done((s16[2320,128]{1,0:T(8,128)(2,1)S(1)}, s16[2320,128]{1,0:T(8,128)(2,1)}, u32[]{:S(2)}, u32[]{:S(2)}) %collective-permute-start.1) | collective-permute-done | bytes 593952 | tf_op jit(solution)/shard_map/ppermute | solution.py:511
  44.9 2.5 %all-to-all-done = s16[32,2,32,640]{3,2,1,0:T(8,128)(2,1)S(1)} async-done(((s16[32,2,32,640]{3,2,1,0:T(8,128)(2,1)}), s16[32,2,32,640]{3,2,1,0:T(8,128)(2,1)S(1)}, u32[]{:S(2)}, u32[]{:S(2)}) %all-to-all-start) | async-done | bytes 2621472 | tf_op jit(solution)/shard_map/all_to_all | solution.py:506
  47.4 1.6 %split_far.1.q = bf16[512,1280]{1,0:T(8,128)(2,1)S(1)} custom-call(s32[3]{0:T(128)S(1)} %pad_add_fusion.place, s16[2320,128]{1,0:T(8,128)(2,1)S(1)} %pack_queries.1.own, s16[2320,128]{1,0:T(8,128)(2,1)} %collective-permute-done.1.other), custom_call_target="tpu_custom_call" | custom-call | flops 10000000 | bytes 4000000 | tf_op jit(solution)/shard_map/split_far/pallas_call | solution.py:202
  49.0 6.4 %attend_far.1 = (s16[32,2176]{1,0:T(8,128)(2,1)S(1)}, bf16[1024,1280]{1,0:T(8,128)(2,1)S(1)}) custom-call(s32[32]{0:T(128)S(1)} %convert_add_fusion.places, s32[32]{0:T(128)S(1)} %get-tuple-element.32.block_ids, s32[3]{0:T(128)S(1)} %pad_add_fusion.place, bf16[512,1280]{1,0:T(8,128)(2,1)S(1)} %split_far.1.q, s16[64,32,640]{2,1,0:T(8,128)(2,1)S(1)} %bitcast.18, ...), custom_call_target="tpu_custom_call" | custom-call | flops 4000000000 | bytes 6000000 | tf_op jit(solution)/shard_map/attend_far/pallas_call | solution.py:330
  55.5 1.9 %collective-permute-start.4 = (s16[32,2176]{1,0:T(8,128)(2,1)S(1)}, s16[32,2176]{1,0:T(8,128)(2,1)S(1)}, u32[]{:S(2)}, u32[]{:S(2)}) collective-permute-start(s16[32,2176]{1,0:T(8,128)(2,1)S(1)} %get-tuple-element.29), channel_id=1, source_target_pairs={{0,1},{1,0},{2,3},{3,2},{4,5},{5,4},{6,7},{7,6},{8,9},{9,8},{10,11... | collective-permute-start | bytes 417800 | tf_op jit(solution)/shard_map/ppermute | solution.py:530
  57.4 6.3 %attend_near.1.here = s16[32,2176]{1,0:T(8,128)(2,1)S(1)} custom-call(s32[32]{0:T(128)S(1)} %get-tuple-element.32.block_ids, s32[3]{0:T(128)S(1)} %pad_add_fusion.place, s16[2320,128]{1,0:T(8,128)(2,1)S(1)} %pack_queries.1.own, s16[2320,128]{1,0:T(8,128)(2,1)} %collective-permute-done.1.other, bf16[1024,1280]{1,0:T(8,128)(2,1)S(1)} %get-tuple-element.25.keys_s, ...), custom_call_target="tpu_custom_call" | custom-call | flops 4000000000 | bytes 6000000 | tf_op jit(solution)/shard_map/attend_near/pallas_call | solution.py:351
  63.7 2.9 %collective-permute-start.6 = (bf16[224,1024]{1,0:T(8,128)(2,1)}, bf16[224,1024]{1,0:T(8,128)(2,1)S(1)}, u32[]{:S(2)}, u32[]{:S(2)}) collective-permute-start(bf16[224,1024]{1,0:T(8,128)(2,1)} %collective-permute-done.3.near_other), channel_id=1, source_target_pairs={{0,16},{16,0},{1,17},{17,1},{2,18},{18,2},{3,19},{19,3},{4,20},{20... | collective-permute-start | bytes 1376264 | tf_op jit(solution)/shard_map/ppermute | solution.py:533
  66.6 1.1 merge.1
  67.7 22.1 %all-gather.2 = s16[512,2176]{1,0:T(8,128)(2,1)S(1)} all-gather(s16[32,2176]{1,0:T(8,128)(2,1)S(1)} %merge.1), channel_id=2, replica_groups=mesh['x'=4,'y'=4,'core'=2,'zq'=8,'zb'=2] {'x','y'}, dimensions={0}, use_global_device_ids=true | all-gather | bytes 2367488 | tf_op jit(solution)/shard_map/all_gather | solution.py:534
  89.7 2.8 %project.1 = bf16[2,16,56,128]{3,2,1,0:T(8,128)(2,1)S(1)} custom-call(s32[3]{0:T(128)S(1)} %pad_add_fusion.place, s16[16,32,2176]{2,1,0:T(8,128)(2,1)S(1)} %bitcast.17, bf16[224,1024]{1,0:T(8,128)(2,1)} %bitcast.9.near_own, bf16[224,1024]{1,0:T(8,128)(2,1)} %collective-permute-done.3.near_other, bf16[224,1024]{1,0:T(8,128)(2,1)} %collective-permute-done.5.far_own, ...), custom_call_target="tpu_custom_call" | custom-call | flops 1000000000 | bytes 7000000 | tf_op jit(solution)/shard_map/project/pallas_call | solution.py:440
  92.5 47.3 %all_to_all.10 = bf16[32,56,128]{2,1,0:T(8,128)(2,1)S(1)} all-to-all(bf16[32,56,128]{2,1,0:T(8,128)(2,1)S(1)} %bitcast.19), channel_id=1, replica_groups=mesh['x'=4,'y'=4,'core'=2,'zq'=8,'zb'=2] {'core','zq','zb'}, dimensions={0} | all-to-all | bytes 917504 | tf_op jit(solution)/shard_map/all_to_all | solution.py:537
  139.8 0.8 add_parts.1
  (12 shorter events, 0.7 us)
Async XLA Ops:
  3.9 43.5 %all-to-all-start = ((s16[32,2,32,640]{3,2,1,0:T(8,128)(2,1)}), s16[32,2,32,640]{3,2,1,0:T(8,128)(2,1)S(1)}, u32[]{:S(2)}, u32[]{:S(2)}) async-start(s16[32,2,32,640]{3,2,1,0:T(8,128)(2,1)} %parcels.1), calls=%async_computation | async-start | bytes 5242880 | tf_op jit(solution)/shard_map/all_to_all | solution.py:506
  16.7 15.4 %collective-permute-start = (bf16[4,512,128]{2,1,0:T(8,128)(2,1)}, bf16[4,512,128]{2,1,0:T(8,128)(2,1)}, u32[]{:S(2)}, u32[]{:S(2)}) collective-permute-start(bf16[4,512,128]{2,1,0:T(8,128)(2,1)} %half_values.1), channel_id=1, source_target_pairs={{0,1},{1,0},{2,3},{3,2},{4,5},{5,4},{6,7},{7,6},{8,9},{9,8},{10,11... | collective-permute-start | bytes 1572872 | tf_op jit(solution)/shard_map/ppermute | solution.py:516
  18.7 1.3 copy-start
  20.4 24.5 %collective-permute-start.1 = (s16[2320,128]{1,0:T(8,128)(2,1)S(1)}, s16[2320,128]{1,0:T(8,128)(2,1)}, u32[]{:S(2)}, u32[]{:S(2)}) collective-permute-start(s16[2320,128]{1,0:T(8,128)(2,1)S(1)} %pack_queries.1.own), channel_id=1, source_target_pairs={{0,1},{1,0},{2,3},{3,2},{4,5},{5,4},{6,7},{7,6},{8,9},{9,8},{10,11... | collective-permute-start | bytes 1781768 | tf_op jit(solution)/shard_map/ppermute | solution.py:511
  23.8 65.9 %collective-permute-start.5 = (bf16[224,1024]{1,0:T(8,128)(2,1)}, bf16[224,1024]{1,0:T(8,128)(2,1)}, u32[]{:S(2)}, u32[]{:S(2)}) collective-permute-start(bf16[224,1024]{1,0:T(8,128)(2,1)} %bitcast.9.near_own), channel_id=1, source_target_pairs={{0,16},{16,0},{1,17},{17,1},{2,18},{18,2},{3,19},{19,3},{4,20},{20... | collective-permute-start | bytes 1376264 | tf_op jit(solution)/shard_map/ppermute | solution.py:513
  32.1 31.5 %collective-permute-start.3 = (bf16[224,1024]{1,0:T(8,128)(2,1)}, bf16[224,1024]{1,0:T(8,128)(2,1)}, u32[]{:S(2)}, u32[]{:S(2)}) collective-permute-start(bf16[224,1024]{1,0:T(8,128)(2,1)} %bitcast.9.near_own), channel_id=1, source_target_pairs={{0,1},{1,0},{2,3},{3,2},{4,5},{5,4},{6,7},{7,6},{8,9},{9,8},{10,11... | collective-permute-start | bytes 1376264 | tf_op jit(solution)/shard_map/ppermute | solution.py:525
  34.3 14.7 %collective-permute-start.2 = (bf16[4,512,128]{2,1,0:T(8,128)(2,1)}, bf16[4,512,128]{2,1,0:T(8,128)(2,1)}, u32[]{:S(2)}, u32[]{:S(2)}) collective-permute-start(bf16[4,512,128]{2,1,0:T(8,128)(2,1)} %collective-permute-done.fetched), channel_id=1, source_target_pairs={{0,16},{16,0},{1,17},{17,1},{2,18},{18,2},{3,19},{19,3},{4,20},{20... | collective-permute-start | bytes 1572872 | tf_op jit(solution)/shard_map/ppermute | solution.py:517
  47.4 1.6 %copy-start.1 = (bf16[8,512,128]{2,1,0:T(8,128)(2,1)S(1)}, bf16[8,512,128]{2,1,0:T(8,128)(2,1)}, u32[]{:S(2)}) copy-start(bf16[8,512,128]{2,1,0:T(8,128)(2,1)} %vp_own.3) | copy-start | bytes 3145732
  55.5 11.1 %collective-permute-start.4 = (s16[32,2176]{1,0:T(8,128)(2,1)S(1)}, s16[32,2176]{1,0:T(8,128)(2,1)S(1)}, u32[]{:S(2)}, u32[]{:S(2)}) collective-permute-start(s16[32,2176]{1,0:T(8,128)(2,1)S(1)} %get-tuple-element.29), channel_id=1, source_target_pairs={{0,1},{1,0},{2,3},{3,2},{4,5},{5,4},{6,7},{7,6},{8,9},{9,8},{10,11... | collective-permute-start | bytes 417800 | tf_op jit(solution)/shard_map/ppermute | solution.py:530
  63.7 26.0 %collective-permute-start.6 = (bf16[224,1024]{1,0:T(8,128)(2,1)}, bf16[224,1024]{1,0:T(8,128)(2,1)S(1)}, u32[]{:S(2)}, u32[]{:S(2)}) collective-permute-start(bf16[224,1024]{1,0:T(8,128)(2,1)} %collective-permute-done.3.near_other), channel_id=1, source_target_pairs={{0,16},{16,0},{1,17},{17,1},{2,18},{18,2},{3,19},{19,3},{4,20},{20... | collective-permute-start | bytes 1376264 | tf_op jit(solution)/shard_map/ppermute | solution.py:533

commit v7 on v6

--- a/solution.py
+++ b/solution.py
@@ -271,9 +271,9 @@
     s = jnp.where(room + spot >= 0, s, NEG)
     peak = jnp.max(s, axis=-1, keepdims=True)
     p = jnp.exp2(s - peak)
-    norm = jnp.sum(p, axis=-1, keepdims=True)
-    high, low = halves(p)
-    mixed = dot_nn(high, keys_s[:, :lat]) + dot_nn(high, keys_s[:, lat : 2 * lat]) + dot_nn(low, keys_s[:, :lat])
+    high = p.astype(BF16)
+    norm = jnp.sum(high.astype(F32), axis=-1, keepdims=True)
+    mixed = dot_nn(high, keys_s[:, :lat]) + dot_nn(high, keys_s[:, lat : 2 * lat])
     mixed = mixed / norm
     for t in range(lat // LANES):
         mixed_s[t] = mixed[:, t * LANES : (t + 1) * LANES]

time: 141 us -> 140 us (level)
  transfers between devices with their start and end apart: 8 -> 8, of which waited for: 3 -> 3; matrix products, arithmetic and copies ran while one was open for 1% -> 1% of each run, Pallas kernels for 13% -> 12%
where the time goes in v7:
time: 140 us; the launch traced here: 139 us
  blocking collectives  69.1 us (49%)
  starting transfers between devices  29.6 us (21%)
  Pallas kernels  24.1 us (17%)
  waiting for transfers between devices  13.4 us (10%)
  other arithmetic  1.68 us (1%)
    all_to_all x1, blocking collectives, on_device(): lax.all_to_all(partial, ('core', 'zq', 'zb'), split_axis=0, concat_axis=0...  47 us
    all_gather x1, blocking collectives, on_device(): lax.all_gather(merge(place, here, there, heads), ('x', 'y'), axis=0, tile...  22.1 us
    all_to_all x1, starting transfers between devices, on_device(): lax.all_to_all(parcels, ('y', 'core', 'x'), split_axis=0, concat_axis=0,...  11.1 us
    pallas_call x1, Pallas kernels, attend_far(): pl.pallas_call(far_kernel, out_shape=(jax.ShapeDtypeStruct((part, PAIR *...  5.93 us
    pallas_call x1, Pallas kernels, attend_near(): pl.pallas_call(near_kernel, out_shape=jax.ShapeDtypeStruct((part, PAIR *...  5.76 us
    ppermute x1, waiting for transfers between devices, on_device(): fetched = lax.ppermute(half_values(core[None], value_near), 'zb', swap)  5.46 us
    ppermute x1, waiting for transfers between devices, on_device(): q_other = lax.ppermute(q_own, 'zb', swap)  5.38 us
    pallas_call x1, Pallas kernels, make_parcels(): pl.pallas_call(functools.partial(parcel_kernel, columns=columns), out_sha...  3.84 us
  transfers between devices with their start and end apart: 8, of which 3 were waited for; matrix products, arithmetic and copies ran while one was open for 1% of the time, Pallas kernels for 12%

profile of v7, /device:TPU:1, one launch (start us, length us, event | category | flops | bytes accessed | tf_op | source)
XLA Modules:
  0.0 139.3 jit_solution(6881834926498246787)
XLA Ops:
  0.0 3.8 %parcels.1 = s16[32,2,32,640]{3,2,1,0:T(8,128)(2,1)} custom-call(s32[1]{0:T(128)} %bitcast.3.owner, s32[1]{0:T(128)} %bitcast.1.member, s32[32,32]{1,0:T(8,128)} %selected.1, f32[576,512]{1,0:T(8,128)} %bitcast.22), custom_call_target="tpu_custom_call" | custom-call | flops 10000000 | bytes 4000000 | tf_op jit(solution)/shard_map/parcels/pallas_call | solution.py:127
  3.8 11.1 %all-to-all-start = ((s16[32,2,32,640]{3,2,1,0:T(8,128)(2,1)}), s16[32,2,32,640]{3,2,1,0:T(8,128)(2,1)S(1)}, u32[]{:S(2)}, u32[]{:S(2)}) async-start(s16[32,2,32,640]{3,2,1,0:T(8,128)(2,1)} %parcels.1), calls=%async_computation | async-start | bytes 5242880 | tf_op jit(solution)/shard_map/all_to_all | solution.py:506
  14.9 1.8 %half_values.1 = bf16[4,512,128]{2,1,0:T(8,128)(2,1)} custom-call(s32[1]{0:T(128)} %bitcast.core, bf16[8,512,128]{2,1,0:T(8,128)(2,1)} %vp_own.3), custom_call_target="tpu_custom_call" | custom-call | flops 10000 | bytes 1000000 | tf_op jit(solution)/shard_map/half_values/pallas_call | solution.py:222
  16.8 1.9 %collective-permute-start = (bf16[4,512,128]{2,1,0:T(8,128)(2,1)}, bf16[4,512,128]{2,1,0:T(8,128)(2,1)}, u32[]{:S(2)}, u32[]{:S(2)}) collective-permute-start(bf16[4,512,128]{2,1,0:T(8,128)(2,1)} %half_values.1), channel_id=1, source_target_pairs={{0,1},{1,0},{2,3},{3,2},{4,5},{5,4},{6,7},{7,6},{8,9},{9,8},{10,11... | collective-permute-start | bytes 1572872 | tf_op jit(solution)/shard_map/ppermute | solution.py:516
  18.7 1.3 copy-done
  20.4 3.4 %collective-permute-start.1 = (s16[2320,128]{1,0:T(8,128)(2,1)S(1)}, s16[2320,128]{1,0:T(8,128)(2,1)}, u32[]{:S(2)}, u32[]{:S(2)}) collective-permute-start(s16[2320,128]{1,0:T(8,128)(2,1)S(1)} %pack_queries.1.own), channel_id=1, source_target_pairs={{0,1},{1,0},{2,3},{3,2},{4,5},{5,4},{6,7},{7,6},{8,9},{9,8},{10,11... | collective-permute-start | bytes 1781768 | tf_op jit(solution)/shard_map/ppermute | solution.py:511
  23.8 2.8 %collective-permute-start.5 = (bf16[224,1024]{1,0:T(8,128)(2,1)}, bf16[224,1024]{1,0:T(8,128)(2,1)}, u32[]{:S(2)}, u32[]{:S(2)}) collective-permute-start(bf16[224,1024]{1,0:T(8,128)(2,1)} %bitcast.9.near_own), channel_id=1, source_target_pairs={{0,16},{16,0},{1,17},{17,1},{2,18},{18,2},{3,19},{19,3},{4,20},{20... | collective-permute-start | bytes 1376264 | tf_op jit(solution)/shard_map/ppermute | solution.py:513
  26.7 5.5 %collective-permute-done.fetched = bf16[4,512,128]{2,1,0:T(8,128)(2,1)} collective-permute-done((bf16[4,512,128]{2,1,0:T(8,128)(2,1)}, bf16[4,512,128]{2,1,0:T(8,128)(2,1)}, u32[]{:S(2)}, u32[]{:S(2)}) %collective-permute-start) | collective-permute-done | bytes 524320 | tf_op jit(solution)/shard_map/ppermute | solution.py:516
  32.2 2.2 %collective-permute-start.3 = (bf16[224,1024]{1,0:T(8,128)(2,1)}, bf16[224,1024]{1,0:T(8,128)(2,1)}, u32[]{:S(2)}, u32[]{:S(2)}) collective-permute-start(bf16[224,1024]{1,0:T(8,128)(2,1)} %bitcast.9.near_own), channel_id=1, source_target_pairs={{0,1},{1,0},{2,3},{3,2},{4,5},{5,4},{6,7},{7,6},{8,9},{9,8},{10,11... | collective-permute-start | bytes 1376264 | tf_op jit(solution)/shard_map/ppermute | solution.py:525
  34.4 3.5 %collective-permute-start.2 = (bf16[4,512,128]{2,1,0:T(8,128)(2,1)}, bf16[4,512,128]{2,1,0:T(8,128)(2,1)}, u32[]{:S(2)}, u32[]{:S(2)}) collective-permute-start(bf16[4,512,128]{2,1,0:T(8,128)(2,1)} %collective-permute-done.fetched), channel_id=1, source_target_pairs={{0,16},{16,0},{1,17},{17,1},{2,18},{18,2},{3,19},{19,3},{4,20},{20... | collective-permute-start | bytes 1572872 | tf_op jit(solution)/shard_map/ppermute | solution.py:517
  37.9 0.7 fusion.2
  38.6 0.7 and_select_fusion.3
  39.5 5.4 %collective-permute-done.1.other = s16[2320,128]{1,0:T(8,128)(2,1)} collective-permute-done((s16[2320,128]{1,0:T(8,128)(2,1)S(1)}, s16[2320,128]{1,0:T(8,128)(2,1)}, u32[]{:S(2)}, u32[]{:S(2)}) %collective-permute-start.1) | collective-permute-done | bytes 593952 | tf_op jit(solution)/shard_map/ppermute | solution.py:511
  44.9 2.5 %all-to-all-done = s16[32,2,32,640]{3,2,1,0:T(8,128)(2,1)S(1)} async-done(((s16[32,2,32,640]{3,2,1,0:T(8,128)(2,1)}), s16[32,2,32,640]{3,2,1,0:T(8,128)(2,1)S(1)}, u32[]{:S(2)}, u32[]{:S(2)}) %all-to-all-start) | async-done | bytes 2621472 | tf_op jit(solution)/shard_map/all_to_all | solution.py:506
  47.4 1.6 %split_far.1.q = bf16[512,1280]{1,0:T(8,128)(2,1)S(1)} custom-call(s32[3]{0:T(128)S(1)} %pad_add_fusion.place, s16[2320,128]{1,0:T(8,128)(2,1)S(1)} %pack_queries.1.own, s16[2320,128]{1,0:T(8,128)(2,1)} %collective-permute-done.1.other), custom_call_target="tpu_custom_call" | custom-call | flops 10000000 | bytes 4000000 | tf_op jit(solution)/shard_map/split_far/pallas_call | solution.py:202
  49.1 5.9 %attend_far.1 = (s16[32,2176]{1,0:T(8,128)(2,1)S(1)}, bf16[1024,1280]{1,0:T(8,128)(2,1)S(1)}) custom-call(s32[32]{0:T(128)S(1)} %convert_add_fusion.places, s32[32]{0:T(128)S(1)} %get-tuple-element.32.block_ids, s32[3]{0:T(128)S(1)} %pad_add_fusion.place, bf16[512,1280]{1,0:T(8,128)(2,1)S(1)} %split_far.1.q, s16[64,32,640]{2,1,0:T(8,128)(2,1)S(1)} %bitcast.18, ...), custom_call_target="tpu_custom_call" | custom-call | flops 4000000000 | bytes 6000000 | tf_op jit(solution)/shard_map/attend_far/pallas_call | solution.py:330
  55.0 1.9 %collective-permute-start.4 = (s16[32,2176]{1,0:T(8,128)(2,1)S(1)}, s16[32,2176]{1,0:T(8,128)(2,1)S(1)}, u32[]{:S(2)}, u32[]{:S(2)}) collective-permute-start(s16[32,2176]{1,0:T(8,128)(2,1)S(1)} %get-tuple-element.29), channel_id=1, source_target_pairs={{0,1},{1,0},{2,3},{3,2},{4,5},{5,4},{6,7},{7,6},{8,9},{9,8},{10,11... | collective-permute-start | bytes 417800 | tf_op jit(solution)/shard_map/ppermute | solution.py:530
  56.9 5.8 %attend_near.1.here = s16[32,2176]{1,0:T(8,128)(2,1)S(1)} custom-call(s32[32]{0:T(128)S(1)} %get-tuple-element.32.block_ids, s32[3]{0:T(128)S(1)} %pad_add_fusion.place, s16[2320,128]{1,0:T(8,128)(2,1)S(1)} %pack_queries.1.own, s16[2320,128]{1,0:T(8,128)(2,1)} %collective-permute-done.1.other, bf16[1024,1280]{1,0:T(8,128)(2,1)S(1)} %get-tuple-element.25.keys_s, ...), custom_call_target="tpu_custom_call" | custom-call | flops 4000000000 | bytes 6000000 | tf_op jit(solution)/shard_map/attend_near/pallas_call | solution.py:351
  62.7 2.8 %collective-permute-start.6 = (bf16[224,1024]{1,0:T(8,128)(2,1)}, bf16[224,1024]{1,0:T(8,128)(2,1)S(1)}, u32[]{:S(2)}, u32[]{:S(2)}) collective-permute-start(bf16[224,1024]{1,0:T(8,128)(2,1)} %collective-permute-done.3.near_other), channel_id=1, source_target_pairs={{0,16},{16,0},{1,17},{17,1},{2,18},{18,2},{3,19},{19,3},{4,20},{20... | collective-permute-start | bytes 1376264 | tf_op jit(solution)/shard_map/ppermute | solution.py:533
  65.5 1.1 merge.1
  66.6 22.1 %all-gather.2 = s16[512,2176]{1,0:T(8,128)(2,1)S(1)} all-gather(s16[32,2176]{1,0:T(8,128)(2,1)S(1)} %merge.1), channel_id=2, replica_groups=mesh['x'=4,'y'=4,'core'=2,'zq'=8,'zb'=2] {'x','y'}, dimensions={0}, use_global_device_ids=true | all-gather | bytes 2367488 | tf_op jit(solution)/shard_map/all_gather | solution.py:534
  88.7 2.8 %project.1 = bf16[2,16,56,128]{3,2,1,0:T(8,128)(2,1)S(1)} custom-call(s32[3]{0:T(128)S(1)} %pad_add_fusion.place, s16[16,32,2176]{2,1,0:T(8,128)(2,1)S(1)} %bitcast.17, bf16[224,1024]{1,0:T(8,128)(2,1)} %bitcast.9.near_own, bf16[224,1024]{1,0:T(8,128)(2,1)} %collective-permute-done.3.near_other, bf16[224,1024]{1,0:T(8,128)(2,1)} %collective-permute-done.5.far_own, ...), custom_call_target="tpu_custom_call" | custom-call | flops 1000000000 | bytes 7000000 | tf_op jit(solution)/shard_map/project/pallas_call | solution.py:440
  91.5 47.0 %all_to_all.10 = bf16[32,56,128]{2,1,0:T(8,128)(2,1)S(1)} all-to-all(bf16[32,56,128]{2,1,0:T(8,128)(2,1)S(1)} %bitcast.19), channel_id=1, replica_groups=mesh['x'=4,'y'=4,'core'=2,'zq'=8,'zb'=2] {'core','zq','zb'}, dimensions={0} | all-to-all | bytes 917504 | tf_op jit(solution)/shard_map/all_to_all | solution.py:537
  138.5 0.8 add_parts.1
  (12 shorter events, 0.7 us)
Async XLA Ops:
  3.8 43.6 %all-to-all-start = ((s16[32,2,32,640]{3,2,1,0:T(8,128)(2,1)}), s16[32,2,32,640]{3,2,1,0:T(8,128)(2,1)S(1)}, u32[]{:S(2)}, u32[]{:S(2)}) async-start(s16[32,2,32,640]{3,2,1,0:T(8,128)(2,1)} %parcels.1), calls=%async_computation | async-start | bytes 5242880 | tf_op jit(solution)/shard_map/all_to_all | solution.py:506
  16.8 15.4 %collective-permute-start = (bf16[4,512,128]{2,1,0:T(8,128)(2,1)}, bf16[4,512,128]{2,1,0:T(8,128)(2,1)}, u32[]{:S(2)}, u32[]{:S(2)}) collective-permute-start(bf16[4,512,128]{2,1,0:T(8,128)(2,1)} %half_values.1), channel_id=1, source_target_pairs={{0,1},{1,0},{2,3},{3,2},{4,5},{5,4},{6,7},{7,6},{8,9},{9,8},{10,11... | collective-permute-start | bytes 1572872 | tf_op jit(solution)/shard_map/ppermute | solution.py:516
  18.7 1.3 copy-start
  20.4 24.5 %collective-permute-start.1 = (s16[2320,128]{1,0:T(8,128)(2,1)S(1)}, s16[2320,128]{1,0:T(8,128)(2,1)}, u32[]{:S(2)}, u32[]{:S(2)}) collective-permute-start(s16[2320,128]{1,0:T(8,128)(2,1)S(1)} %pack_queries.1.own), channel_id=1, source_target_pairs={{0,1},{1,0},{2,3},{3,2},{4,5},{5,4},{6,7},{7,6},{8,9},{9,8},{10,11... | collective-permute-start | bytes 1781768 | tf_op jit(solution)/shard_map/ppermute | solution.py:511
  23.8 64.9 %collective-permute-start.5 = (bf16[224,1024]{1,0:T(8,128)(2,1)}, bf16[224,1024]{1,0:T(8,128)(2,1)}, u32[]{:S(2)}, u32[]{:S(2)}) collective-permute-start(bf16[224,1024]{1,0:T(8,128)(2,1)} %bitcast.9.near_own), channel_id=1, source_target_pairs={{0,16},{16,0},{1,17},{17,1},{2,18},{18,2},{3,19},{19,3},{4,20},{20... | collective-permute-start | bytes 1376264 | tf_op jit(solution)/shard_map/ppermute | solution.py:513
  32.2 30.5 %collective-permute-start.3 = (bf16[224,1024]{1,0:T(8,128)(2,1)}, bf16[224,1024]{1,0:T(8,128)(2,1)}, u32[]{:S(2)}, u32[]{:S(2)}) collective-permute-start(bf16[224,1024]{1,0:T(8,128)(2,1)} %bitcast.9.near_own), channel_id=1, source_target_pairs={{0,1},{1,0},{2,3},{3,2},{4,5},{5,4},{6,7},{7,6},{8,9},{9,8},{10,11... | collective-permute-start | bytes 1376264 | tf_op jit(solution)/shard_map/ppermute | solution.py:525
  34.4 14.7 %collective-permute-start.2 = (bf16[4,512,128]{2,1,0:T(8,128)(2,1)}, bf16[4,512,128]{2,1,0:T(8,128)(2,1)}, u32[]{:S(2)}, u32[]{:S(2)}) collective-permute-start(bf16[4,512,128]{2,1,0:T(8,128)(2,1)} %collective-permute-done.fetched), channel_id=1, source_target_pairs={{0,16},{16,0},{1,17},{17,1},{2,18},{18,2},{3,19},{19,3},{4,20},{20... | collective-permute-start | bytes 1572872 | tf_op jit(solution)/shard_map/ppermute | solution.py:517
  47.4 1.6 %copy-start.1 = (bf16[8,512,128]{2,1,0:T(8,128)(2,1)S(1)}, bf16[8,512,128]{2,1,0:T(8,128)(2,1)}, u32[]{:S(2)}) copy-start(bf16[8,512,128]{2,1,0:T(8,128)(2,1)} %vp_own.3) | copy-start | bytes 3145732
  55.0 10.5 %collective-permute-start.4 = (s16[32,2176]{1,0:T(8,128)(2,1)S(1)}, s16[32,2176]{1,0:T(8,128)(2,1)S(1)}, u32[]{:S(2)}, u32[]{:S(2)}) collective-permute-start(s16[32,2176]{1,0:T(8,128)(2,1)S(1)} %get-tuple-element.29), channel_id=1, source_target_pairs={{0,1},{1,0},{2,3},{3,2},{4,5},{5,4},{6,7},{7,6},{8,9},{9,8},{10,11... | collective-permute-start | bytes 417800 | tf_op jit(solution)/shard_map/ppermute | solution.py:530
  62.7 26.0 %collective-permute-start.6 = (bf16[224,1024]{1,0:T(8,128)(2,1)}, bf16[224,1024]{1,0:T(8,128)(2,1)S(1)}, u32[]{:S(2)}, u32[]{:S(2)}) collective-permute-start(bf16[224,1024]{1,0:T(8,128)(2,1)} %collective-permute-done.3.near_other), channel_id=1, source_target_pairs={{0,16},{16,0},{1,17},{17,1},{2,18},{18,2},{3,19},{19,3},{4,20},{20... | collective-permute-start | bytes 1376264 | tf_op jit(solution)/shard_map/ppermute | solution.py:533

commit v8 on v6

--- a/solution.py
+++ b/solution.py
@@ -527,10 +527,10 @@
     arrived, q_own, q_other = lax.optimization_barrier((arrived, q_own, q_other))
     q_far = split_far(place, q_own, q_other, heads * block, 2 * padded)
     for_partner, keys = attend_far(places, own_list, place, q_far, arrived, value_proj, fetched, passed)
+    for_partner, near_other = lax.optimization_barrier((for_partner, near_other))
     there = lax.ppermute(for_partner, "zb", swap)
+    far_other = lax.ppermute(near_other, "core", swap)
     here = attend_near(own_list, place, q_own, q_other, keys, value_proj, fetched, passed, part)
-    here, near_other = lax.optimization_barrier((here, near_other))
-    far_other = lax.ppermute(near_other, "core", swap)
     gathered = lax.all_gather(merge(place, here, there, heads), ("x", "y"), axis=0, tiled=False)
     partial = project(place, gathered, near_own, near_other, far_own, far_other)
     partial = partial.reshape(-1, *partial.shape[2:])

time: 141 us -> 142 us (level)
  no operation moved by 1% of the time
where the time goes in v8:
time: 142 us; the launch traced here: 141 us
  blocking collectives  69.9 us (49%)
  starting transfers between devices  29.4 us (21%)
  Pallas kernels  25.1 us (18%)
  waiting for transfers between devices  13.4 us (9%)
  other arithmetic  1.68 us (1%)
    all_to_all x1, blocking collectives, on_device(): lax.all_to_all(partial, ('core', 'zq', 'zb'), split_axis=0, concat_axis=0...  46.7 us
    all_gather x1, blocking collectives, on_device(): lax.all_gather(merge(place, here, there, heads), ('x', 'y'), axis=0, tile...  23.2 us
    all_to_all x1, starting transfers between devices, on_device(): lax.all_to_all(parcels, ('y', 'core', 'x'), split_axis=0, concat_axis=0,...  10.9 us
    pallas_call x1, Pallas kernels, attend_far(): pl.pallas_call(far_kernel, out_shape=(jax.ShapeDtypeStruct((part, PAIR *...  6.41 us
    pallas_call x1, Pallas kernels, attend_near(): pl.pallas_call(near_kernel, out_shape=jax.ShapeDtypeStruct((part, PAIR *...  6.28 us
    ppermute x1, waiting for transfers between devices, on_device(): fetched = lax.ppermute(half_values(core[None], value_near), 'zb', swap)  5.46 us
    ppermute x1, waiting for transfers between devices, on_device(): q_other = lax.ppermute(q_own, 'zb', swap)  5.38 us
    pallas_call x1, Pallas kernels, make_parcels(): pl.pallas_call(functools.partial(parcel_kernel, columns=columns), out_sha...  3.86 us
  transfers between devices with their start and end apart: 8, of which 3 were waited for; matrix products, arithmetic and copies ran while one was open for 1% of the time, Pallas kernels for 13%

profile of v8, /device:TPU:1, one launch (start us, length us, event | category | flops | bytes accessed | tf_op | source)
XLA Modules:
  0.0 141.0 jit_solution(7668783384637266530)
XLA Ops:
  0.0 3.9 %parcels.1 = s16[32,2,32,640]{3,2,1,0:T(8,128)(2,1)} custom-call(s32[1]{0:T(128)} %bitcast.3.owner, s32[1]{0:T(128)} %bitcast.1.member, s32[32,32]{1,0:T(8,128)} %selected.1, f32[576,512]{1,0:T(8,128)} %bitcast.22), custom_call_target="tpu_custom_call" | custom-call | flops 10000000 | bytes 4000000 | tf_op jit(solution)/shard_map/parcels/pallas_call | solution.py:127
  3.9 10.9 %all-to-all-start = ((s16[32,2,32,640]{3,2,1,0:T(8,128)(2,1)}), s16[32,2,32,640]{3,2,1,0:T(8,128)(2,1)S(1)}, u32[]{:S(2)}, u32[]{:S(2)}) async-start(s16[32,2,32,640]{3,2,1,0:T(8,128)(2,1)} %parcels.1), calls=%async_computation | async-start | bytes 5242880 | tf_op jit(solution)/shard_map/all_to_all | solution.py:506
  14.8 1.8 %half_values.1 = bf16[4,512,128]{2,1,0:T(8,128)(2,1)} custom-call(s32[1]{0:T(128)} %bitcast.core, bf16[8,512,128]{2,1,0:T(8,128)(2,1)} %vp_own.3), custom_call_target="tpu_custom_call" | custom-call | flops 10000 | bytes 1000000 | tf_op jit(solution)/shard_map/half_values/pallas_call | solution.py:222
  16.7 1.9 %collective-permute-start = (bf16[4,512,128]{2,1,0:T(8,128)(2,1)}, bf16[4,512,128]{2,1,0:T(8,128)(2,1)}, u32[]{:S(2)}, u32[]{:S(2)}) collective-permute-start(bf16[4,512,128]{2,1,0:T(8,128)(2,1)} %half_values.1), channel_id=1, source_target_pairs={{0,1},{1,0},{2,3},{3,2},{4,5},{5,4},{6,7},{7,6},{8,9},{9,8},{10,11... | collective-permute-start | bytes 1572872 | tf_op jit(solution)/shard_map/ppermute | solution.py:516
  18.6 1.3 copy-done
  20.3 3.4 %collective-permute-start.1 = (s16[2320,128]{1,0:T(8,128)(2,1)S(1)}, s16[2320,128]{1,0:T(8,128)(2,1)}, u32[]{:S(2)}, u32[]{:S(2)}) collective-permute-start(s16[2320,128]{1,0:T(8,128)(2,1)S(1)} %pack_queries.1.own), channel_id=1, source_target_pairs={{0,1},{1,0},{2,3},{3,2},{4,5},{5,4},{6,7},{7,6},{8,9},{9,8},{10,11... | collective-permute-start | bytes 1781768 | tf_op jit(solution)/shard_map/ppermute | solution.py:511
  23.7 2.8 %collective-permute-start.5 = (bf16[224,1024]{1,0:T(8,128)(2,1)}, bf16[224,1024]{1,0:T(8,128)(2,1)}, u32[]{:S(2)}, u32[]{:S(2)}) collective-permute-start(bf16[224,1024]{1,0:T(8,128)(2,1)} %bitcast.9.near_own), channel_id=1, source_target_pairs={{0,16},{16,0},{1,17},{17,1},{2,18},{18,2},{3,19},{19,3},{4,20},{20... | collective-permute-start | bytes 1376264 | tf_op jit(solution)/shard_map/ppermute | solution.py:513
  26.6 5.5 %collective-permute-done.fetched = bf16[4,512,128]{2,1,0:T(8,128)(2,1)} collective-permute-done((bf16[4,512,128]{2,1,0:T(8,128)(2,1)}, bf16[4,512,128]{2,1,0:T(8,128)(2,1)}, u32[]{:S(2)}, u32[]{:S(2)}) %collective-permute-start) | collective-permute-done | bytes 524320 | tf_op jit(solution)/shard_map/ppermute | solution.py:516
  32.1 2.2 %collective-permute-start.3 = (bf16[224,1024]{1,0:T(8,128)(2,1)}, bf16[224,1024]{1,0:T(8,128)(2,1)}, u32[]{:S(2)}, u32[]{:S(2)}) collective-permute-start(bf16[224,1024]{1,0:T(8,128)(2,1)} %bitcast.9.near_own), channel_id=1, source_target_pairs={{0,1},{1,0},{2,3},{3,2},{4,5},{5,4},{6,7},{7,6},{8,9},{9,8},{10,11... | collective-permute-start | bytes 1376264 | tf_op jit(solution)/shard_map/ppermute | solution.py:525
  34.3 3.5 %collective-permute-start.2 = (bf16[4,512,128]{2,1,0:T(8,128)(2,1)}, bf16[4,512,128]{2,1,0:T(8,128)(2,1)}, u32[]{:S(2)}, u32[]{:S(2)}) collective-permute-start(bf16[4,512,128]{2,1,0:T(8,128)(2,1)} %collective-permute-done.fetched), channel_id=1, source_target_pairs={{0,16},{16,0},{1,17},{17,1},{2,18},{18,2},{3,19},{19,3},{4,20},{20... | collective-permute-start | bytes 1572872 | tf_op jit(solution)/shard_map/ppermute | solution.py:517
  37.8 0.7 fusion.2
  38.5 0.7 and_select_fusion.3
  39.4 5.4 %collective-permute-done.1.other = s16[2320,128]{1,0:T(8,128)(2,1)} collective-permute-done((s16[2320,128]{1,0:T(8,128)(2,1)S(1)}, s16[2320,128]{1,0:T(8,128)(2,1)}, u32[]{:S(2)}, u32[]{:S(2)}) %collective-permute-start.1) | collective-permute-done | bytes 593952 | tf_op jit(solution)/shard_map/ppermute | solution.py:511
  44.8 2.5 %all-to-all-done = s16[32,2,32,640]{3,2,1,0:T(8,128)(2,1)S(1)} async-done(((s16[32,2,32,640]{3,2,1,0:T(8,128)(2,1)}), s16[32,2,32,640]{3,2,1,0:T(8,128)(2,1)S(1)}, u32[]{:S(2)}, u32[]{:S(2)}) %all-to-all-start) | async-done | bytes 2621472 | tf_op jit(solution)/shard_map/all_to_all | solution.py:506
  47.3 1.6 %split_far.1.q = bf16[512,1280]{1,0:T(8,128)(2,1)S(1)} custom-call(s32[3]{0:T(128)S(1)} %pad_add_fusion.place, s16[2320,128]{1,0:T(8,128)(2,1)S(1)} %pack_queries.1.own, s16[2320,128]{1,0:T(8,128)(2,1)} %collective-permute-done.1.other), custom_call_target="tpu_custom_call" | custom-call | flops 10000000 | bytes 4000000 | tf_op jit(solution)/shard_map/split_far/pallas_call | solution.py:202
  49.0 6.4 %attend_far.1 = (s16[32,2176]{1,0:T(8,128)(2,1)S(1)}, bf16[1024,1280]{1,0:T(8,128)(2,1)S(1)}) custom-call(s32[32]{0:T(128)S(1)} %convert_add_fusion.places, s32[32]{0:T(128)S(1)} %get-tuple-element.32.block_ids, s32[3]{0:T(128)S(1)} %pad_add_fusion.place, bf16[512,1280]{1,0:T(8,128)(2,1)S(1)} %split_far.1.q, s16[64,32,640]{2,1,0:T(8,128)(2,1)S(1)} %bitcast.18, ...), custom_call_target="tpu_custom_call" | custom-call | flops 4000000000 | bytes 6000000 | tf_op jit(solution)/shard_map/attend_far/pallas_call | solution.py:330
  55.4 1.9 %collective-permute-start.4 = (s16[32,2176]{1,0:T(8,128)(2,1)S(1)}, s16[32,2176]{1,0:T(8,128)(2,1)S(1)}, u32[]{:S(2)}, u32[]{:S(2)}) collective-permute-start(s16[32,2176]{1,0:T(8,128)(2,1)S(1)} %get-tuple-element.29), channel_id=1, source_target_pairs={{0,1},{1,0},{2,3},{3,2},{4,5},{5,4},{6,7},{7,6},{8,9},{9,8},{10,11... | collective-permute-start | bytes 417800 | tf_op jit(solution)/shard_map/ppermute | solution.py:531
  57.3 2.8 %collective-permute-start.6 = (bf16[224,1024]{1,0:T(8,128)(2,1)}, bf16[224,1024]{1,0:T(8,128)(2,1)S(1)}, u32[]{:S(2)}, u32[]{:S(2)}) collective-permute-start(bf16[224,1024]{1,0:T(8,128)(2,1)} %collective-permute-done.3.near_other), channel_id=1, source_target_pairs={{0,16},{16,0},{1,17},{17,1},{2,18},{18,2},{3,19},{19,3},{4,20},{20... | collective-permute-start | bytes 1376264 | tf_op jit(solution)/shard_map/ppermute | solution.py:532
  60.1 6.3 %attend_near.1.here = s16[32,2176]{1,0:T(8,128)(2,1)S(1)} custom-call(s32[32]{0:T(128)S(1)} %get-tuple-element.32.block_ids, s32[3]{0:T(128)S(1)} %pad_add_fusion.place, s16[2320,128]{1,0:T(8,128)(2,1)S(1)} %pack_queries.1.own, s16[2320,128]{1,0:T(8,128)(2,1)} %collective-permute-done.1.other, bf16[1024,1280]{1,0:T(8,128)(2,1)S(1)} %get-tuple-element.25.keys_s, ...), custom_call_target="tpu_custom_call" | custom-call | flops 4000000000 | bytes 6000000 | tf_op jit(solution)/shard_map/attend_near/pallas_call | solution.py:351
  66.4 1.1 merge.1
  67.5 23.2 %all-gather.2 = s16[512,2176]{1,0:T(8,128)(2,1)S(1)} all-gather(s16[32,2176]{1,0:T(8,128)(2,1)S(1)} %merge.1), channel_id=2, replica_groups=mesh['x'=4,'y'=4,'core'=2,'zq'=8,'zb'=2] {'x','y'}, dimensions={0}, use_global_device_ids=true | all-gather | bytes 2367488 | tf_op jit(solution)/shard_map/all_gather | solution.py:534
  90.7 2.8 %project.1 = bf16[2,16,56,128]{3,2,1,0:T(8,128)(2,1)S(1)} custom-call(s32[3]{0:T(128)S(1)} %pad_add_fusion.place, s16[16,32,2176]{2,1,0:T(8,128)(2,1)S(1)} %bitcast.17, bf16[224,1024]{1,0:T(8,128)(2,1)} %bitcast.9.near_own, bf16[224,1024]{1,0:T(8,128)(2,1)} %collective-permute-done.3.near_other, bf16[224,1024]{1,0:T(8,128)(2,1)} %collective-permute-done.5.far_own, ...), custom_call_target="tpu_custom_call" | custom-call | flops 1000000000 | bytes 7000000 | tf_op jit(solution)/shard_map/project/pallas_call | solution.py:440
  93.5 46.7 %all_to_all.10 = bf16[32,56,128]{2,1,0:T(8,128)(2,1)S(1)} all-to-all(bf16[32,56,128]{2,1,0:T(8,128)(2,1)S(1)} %bitcast.19), channel_id=1, replica_groups=mesh['x'=4,'y'=4,'core'=2,'zq'=8,'zb'=2] {'core','zq','zb'}, dimensions={0} | all-to-all | bytes 917504 | tf_op jit(solution)/shard_map/all_to_all | solution.py:537
  140.2 0.8 add_parts.1
  (12 shorter events, 0.7 us)
Async XLA Ops:
  3.9 43.4 %all-to-all-start = ((s16[32,2,32,640]{3,2,1,0:T(8,128)(2,1)}), s16[32,2,32,640]{3,2,1,0:T(8,128)(2,1)S(1)}, u32[]{:S(2)}, u32[]{:S(2)}) async-start(s16[32,2,32,640]{3,2,1,0:T(8,128)(2,1)} %parcels.1), calls=%async_computation | async-start | bytes 5242880 | tf_op jit(solution)/shard_map/all_to_all | solution.py:506
  16.7 15.4 %collective-permute-start = (bf16[4,512,128]{2,1,0:T(8,128)(2,1)}, bf16[4,512,128]{2,1,0:T(8,128)(2,1)}, u32[]{:S(2)}, u32[]{:S(2)}) collective-permute-start(bf16[4,512,128]{2,1,0:T(8,128)(2,1)} %half_values.1), channel_id=1, source_target_pairs={{0,1},{1,0},{2,3},{3,2},{4,5},{5,4},{6,7},{7,6},{8,9},{9,8},{10,11... | collective-permute-start | bytes 1572872 | tf_op jit(solution)/shard_map/ppermute | solution.py:516
  18.6 1.3 copy-start
  20.3 24.5 %collective-permute-start.1 = (s16[2320,128]{1,0:T(8,128)(2,1)S(1)}, s16[2320,128]{1,0:T(8,128)(2,1)}, u32[]{:S(2)}, u32[]{:S(2)}) collective-permute-start(s16[2320,128]{1,0:T(8,128)(2,1)S(1)} %pack_queries.1.own), channel_id=1, source_target_pairs={{0,1},{1,0},{2,3},{3,2},{4,5},{5,4},{6,7},{7,6},{8,9},{9,8},{10,11... | collective-permute-start | bytes 1781768 | tf_op jit(solution)/shard_map/ppermute | solution.py:511
  23.7 67.0 %collective-permute-start.5 = (bf16[224,1024]{1,0:T(8,128)(2,1)}, bf16[224,1024]{1,0:T(8,128)(2,1)}, u32[]{:S(2)}, u32[]{:S(2)}) collective-permute-start(bf16[224,1024]{1,0:T(8,128)(2,1)} %bitcast.9.near_own), channel_id=1, source_target_pairs={{0,16},{16,0},{1,17},{17,1},{2,18},{18,2},{3,19},{19,3},{4,20},{20... | collective-permute-start | bytes 1376264 | tf_op jit(solution)/shard_map/ppermute | solution.py:513
  32.1 23.3 %collective-permute-start.3 = (bf16[224,1024]{1,0:T(8,128)(2,1)}, bf16[224,1024]{1,0:T(8,128)(2,1)}, u32[]{:S(2)}, u32[]{:S(2)}) collective-permute-start(bf16[224,1024]{1,0:T(8,128)(2,1)} %bitcast.9.near_own), channel_id=1, source_target_pairs={{0,1},{1,0},{2,3},{3,2},{4,5},{5,4},{6,7},{7,6},{8,9},{9,8},{10,11... | collective-permute-start | bytes 1376264 | tf_op jit(solution)/shard_map/ppermute | solution.py:525
  34.3 14.7 %collective-permute-start.2 = (bf16[4,512,128]{2,1,0:T(8,128)(2,1)}, bf16[4,512,128]{2,1,0:T(8,128)(2,1)}, u32[]{:S(2)}, u32[]{:S(2)}) collective-permute-start(bf16[4,512,128]{2,1,0:T(8,128)(2,1)} %collective-permute-done.fetched), channel_id=1, source_target_pairs={{0,16},{16,0},{1,17},{17,1},{2,18},{18,2},{3,19},{19,3},{4,20},{20... | collective-permute-start | bytes 1572872 | tf_op jit(solution)/shard_map/ppermute | solution.py:517
  47.3 1.6 %copy-start.1 = (bf16[8,512,128]{2,1,0:T(8,128)(2,1)S(1)}, bf16[8,512,128]{2,1,0:T(8,128)(2,1)}, u32[]{:S(2)}) copy-start(bf16[8,512,128]{2,1,0:T(8,128)(2,1)} %vp_own.3) | copy-start | bytes 3145732
  55.4 11.0 %collective-permute-start.4 = (s16[32,2176]{1,0:T(8,128)(2,1)S(1)}, s16[32,2176]{1,0:T(8,128)(2,1)S(1)}, u32[]{:S(2)}, u32[]{:S(2)}) collective-permute-start(s16[32,2176]{1,0:T(8,128)(2,1)S(1)} %get-tuple-element.29), channel_id=1, source_target_pairs={{0,1},{1,0},{2,3},{3,2},{4,5},{5,4},{6,7},{7,6},{8,9},{9,8},{10,11... | collective-permute-start | bytes 417800 | tf_op jit(solution)/shard_map/ppermute | solution.py:531
  57.3 33.4 %collective-permute-start.6 = (bf16[224,1024]{1,0:T(8,128)(2,1)}, bf16[224,1024]{1,0:T(8,128)(2,1)S(1)}, u32[]{:S(2)}, u32[]{:S(2)}) collective-permute-start(bf16[224,1024]{1,0:T(8,128)(2,1)} %collective-permute-done.3.near_other), channel_id=1, source_target_pairs={{0,16},{16,0},{1,17},{17,1},{2,18},{18,2},{3,19},{19,3},{4,20},{20... | collective-permute-start | bytes 1376264 | tf_op jit(solution)/shard_map/ppermute | solution.py:532
